TPU v7x, 256 devices: a whole 4x4x8 slice. The times are simulated.
256 devices in a mesh: seq: 16 (over z, y_hi), head: 8 (over x, core), dp: 2 (over y_lo).
Axes of the slice: x: 4, y: 4 (y_hi: 2, y_lo: 2; y = y_hi * 2 + y_lo), z: 8, core: 2. Of those that a mesh axis runs over, the one named last changes fastest.
Arguments:
- query_proj: bfloat16 [8192, 3072], P(('dp', 'seq'), 'head'), parts along dimension 0, may hold values from -12.5 to 12.5
- query_tangent: bfloat16 [8192, 3072], P(('dp', 'seq'), 'head'), parts along dimension 0, may hold values from -6 to 6
- key_proj: bfloat16 [8192, 3072], P(('dp', 'seq'), 'head'), parts along dimension 0, may hold values from -5 to 5
- key_tangent: bfloat16 [8192, 3072], P(('dp', 'seq'), 'head'), parts along dimension 0, may hold values from -5 to 5
- value_proj: bfloat16 [8192, 3072], P(('dp', 'seq'), 'head'), parts along dimension 0, may hold values from -6 to 6
- value_tangent: bfloat16 [8192, 3072], P(('dp', 'seq'), 'head'), parts along dimension 0, may hold values from -6 to 6
- residual: bfloat16 [8192, 6144], P(('dp', 'seq'), 'head'), parts along dimension 0, may hold values from -6 to 6
- residual_tangent: bfloat16 [8192, 6144], P(('dp', 'seq'), 'head'), parts along dimension 0, may hold values from -6 to 6
- out_weight: bfloat16 [3072, 6144], P('head'), may hold values from -0.15625 to 0.15625
- out_gate: float32 [12288], P(('dp', 'head')), parts along dimension 0, may hold values from 0.5 to 1.5
- out_gate_tangent: float32 [12288], P(('dp', 'head')), parts along dimension 0, may hold values from -3 to 3
Outputs:
- block_out: bfloat16 [8192, 6144], P(('dp', 'seq'), 'head'), parts along dimension 0
- block_tangent: bfloat16 [8192, 6144], P(('dp', 'seq'), 'head'), parts along dimension 0
There are 2 independent parts, one for each index of `dp`. A program takes and returns all parts, laid end to end along the dimension named above; an argument that names none is the same for every part. Nothing has to cross between parts.
All inputs are finite; a program needn't handle non-finite values.
Results may differ from a plain program's by a relative error of at most 0.015.
Values may be sent and summed in bfloat16 or wider, within the bound.
No kernel may reach another device: no remote copies, remote signals or barrier semaphores. Data moves between devices by JAX's collectives and lax.ppermute only.
A program may use at most 64 MiB of HBM per device.

v0:
```python
import functools

import jax
import jax.numpy as jnp
from jax import lax
from jax.experimental import pallas as pl
from jax.experimental.pallas import tpu as pltpu
from jax.sharding import Mesh
from jax.sharding import PartitionSpec as P

HD = 128
SCALE = HD ** (-0.5)
SCALE2 = SCALE * 1.4426950408889634
NT = (((1,), (1,)), ((), ()))
BF16 = jnp.bfloat16
F32 = jnp.float32
VMEM_LIMIT = 48 * 1024 * 1024
STATS = 8


def spec_whole():
    return pl.BlockSpec(memory_space=pltpu.VMEM)


def params():
    return pltpu.CompilerParams(vmem_limit_bytes=VMEM_LIMIT)


def query_kernel(q, qt, out):
    out[:, 0:HD] = qt[...]
    out[:, HD:] = q[...]


def pack_queries(q, qt):
    rows, width = q.shape
    spec = pl.BlockSpec((rows, HD), lambda h: (0, h))
    return pl.pallas_call(
        query_kernel,
        grid=(width // HD,),
        out_shape=jax.ShapeDtypeStruct((rows, 2 * width), BF16),
        in_specs=[spec] * 2,
        out_specs=pl.BlockSpec((rows, 2 * HD), lambda h: (0, h)),
        compiler_params=params(),
        cost_estimate=pl.CostEstimate(flops=0, bytes_accessed=8 * rows * width, transcendentals=0),
        name="pack_queries",
    )(q, qt)


def pack_kernel(k, kt, v, vt, out):
    out[0, :, 0:HD] = k[...]
    out[0, :, HD:] = kt[...]
    out[1, 0:HD, :] = v[...].T
    out[1, HD:, :] = vt[...].T


def pack(k, kt, v, vt, first, heads):
    rows = k.shape[0]
    spec = pl.BlockSpec((rows, HD), lambda h: (0, first + h))
    out = pl.pallas_call(
        pack_kernel,
        grid=(heads,),
        out_shape=jax.ShapeDtypeStruct((2, heads * 2 * HD, rows), BF16),
        in_specs=[spec] * 4,
        out_specs=pl.BlockSpec((2, 2 * HD, rows), lambda h: (0, h, 0)),
        compiler_params=params(),
        cost_estimate=pl.CostEstimate(
            flops=0, bytes_accessed=16 * rows * heads * HD, transcendentals=0
        ),
        name="pack",
    )(k, kt, v, vt)
    return out


def three_parts(value):
    high = value.astype(BF16)
    rest = value - high.astype(F32)
    middle = rest.astype(BF16)
    low = (rest - middle.astype(F32)).astype(BF16)
    return [high, middle, low]


def attend_kernel(blocks, with_state, final, *refs):
    refs = list(refs)
    q_refs = [refs.pop(0), refs.pop(0)]
    k_refs = [refs.pop(0) for _ in range(blocks)]
    v_refs = [refs.pop(0) for _ in range(blocks)]
    state = refs.pop(0) if with_state else None
    scores_ref = refs.pop()
    rows = q_refs[0].shape[0]
    keys = rows
    for group in range(2):
        q2 = q_refs[group][...]
        q = q2[:, HD:]
        base = group * (2 * HD + STATS)
        top = state[base + 2 * HD : base + 2 * HD + 1, :] if with_state else None
        old_top = top
        for i, k_ref in enumerate(k_refs):
            part = k_ref[:, 0:HD]
            scores = lax.dot_general(part, q, NT, preferred_element_type=F32)
            scores_ref[i * keys : (i + 1) * keys, :] = scores
            peak = jnp.max(scores, axis=0, keepdims=True) * SCALE2
            top = peak if top is None else jnp.maximum(top, peak)
        total = jnp.zeros((1, rows), F32)
        mixed_sum = jnp.zeros((1, rows), F32)
        acc = jnp.zeros((2 * HD, rows), F32)
        acc_mixed = jnp.zeros((HD, rows), F32)
        for i, (k_ref, v_ref) in enumerate(zip(k_refs, v_refs)):
            tangent = lax.dot_general(k_ref[...], q2, NT, preferred_element_type=F32)
            weights = jnp.exp2(scores_ref[i * keys : (i + 1) * keys, :] * SCALE2 - top)
            mixed = weights * tangent
            total = total + jnp.sum(weights, axis=0, keepdims=True)
            mixed_sum = mixed_sum + jnp.sum(mixed, axis=0, keepdims=True)
            vv = v_ref[...]
            acc = acc + jnp.dot(vv, weights.astype(BF16), preferred_element_type=F32)
            acc_mixed = acc_mixed + jnp.dot(
                vv[0:HD, :], mixed.astype(BF16), preferred_element_type=F32
            )
        acc_out = acc[0:HD, :]
        acc_tan = acc[HD:, :] + SCALE * acc_mixed
        mixed_sum = SCALE * mixed_sum
        if with_state:
            shrink = jnp.exp2(old_top - top)
            acc_out = acc_out + shrink * state[base : base + HD, :]
            acc_tan = acc_tan + shrink * state[base + HD : base + 2 * HD, :]
            total = total + shrink * state[base + 2 * HD + 1 : base + 2 * HD + 2, :]
            mixed_sum = mixed_sum + shrink * state[base + 2 * HD + 2 : base + 2 * HD + 3, :]
        if not final:
            out = refs[0]
            out[base : base + HD, :] = acc_out
            out[base + HD : base + 2 * HD, :] = acc_tan
            out[base + 2 * HD : base + 2 * HD + 1, :] = top
            out[base + 2 * HD + 1 : base + 2 * HD + 2, :] = total
            out[base + 2 * HD + 2 : base + 2 * HD + 3, :] = mixed_sum
            continue
        inverse = 1.0 / total
        ratio = mixed_sum * inverse
        attention = acc_out * inverse
        attention_t = acc_tan * inverse - ratio * attention
        if group == 0:
            out = refs[0]
            out[0:HD, :] = attention
            out[HD : 2 * HD, :] = attention_t
            out[2 * HD : 2 * HD + 1, :] = top
            out[2 * HD + 1 : 2 * HD + 2, :] = total
            out[2 * HD + 2 : 2 * HD + 3, :] = ratio
        else:
            out = refs[1]
            out[0:HD, :] = attention.astype(BF16)
            out[HD : 2 * HD, :] = attention_t.astype(BF16)
            stats = three_parts(top) + three_parts(total) + three_parts(ratio)
            stats = [s.astype(F32) for s in stats]
            stats.append(jnp.zeros((2 * STATS - len(stats), rows), F32))
            out[2 * HD :, :] = jnp.concatenate(stats, axis=0).astype(BF16)


def attend(first, heads, q_own, q_far, blocks, state=None, final=False):
    rows = q_own.shape[0]
    n = len(blocks)
    q_spec = pl.BlockSpec((rows, 2 * HD), lambda h: (0, first + h))
    tall, far = 2 * HD + STATS, 2 * HD + 2 * STATS
    keys, values, specs = [], [], []
    for block in blocks:
        pair = block if isinstance(block, tuple) else (block, block)
        keys.append(pair[0])
        values.append(pair[1])
    for group, part in ((keys, 0), (values, 1)):
        for array in group:
            if array.ndim == 3:
                specs.append(pl.BlockSpec((None, 2 * HD, rows), lambda h, p=part: (p, h, 0)))
            else:
                specs.append(pl.BlockSpec((2 * HD, rows), lambda h: (h, 0)))
    by_head = lambda height: pl.BlockSpec((height, rows), lambda h: (h, 0))
    extra = []
    if state is not None:
        extra.append(state)
        specs.append(by_head(2 * tall))
    if final:
        outs = [
            jax.ShapeDtypeStruct((heads * tall, rows), F32),
            jax.ShapeDtypeStruct((heads * far, rows), BF16),
        ]
        out_specs = [by_head(tall), by_head(far)]
    else:
        outs = [jax.ShapeDtypeStruct((heads * 2 * tall, rows), F32)]
        out_specs = [by_head(2 * tall)]
    result = pl.pallas_call(
        functools.partial(attend_kernel, n, state is not None, final),
        grid=(heads,),
        out_shape=outs,
        in_specs=[q_spec, q_spec] + specs,
        out_specs=out_specs,
        scratch_shapes=[pltpu.VMEM((n * rows, rows), F32)],
        compiler_params=params(),
        cost_estimate=pl.CostEstimate(
            flops=heads * 2 * 2 * rows * n * rows * HD * 8,
            bytes_accessed=heads * 2 * rows * HD * 4 * (n + 2),
            transcendentals=heads * 2 * rows * n * rows,
        ),
        name="attend",
    )(q_own, q_far, *keys, *values, *extra)
    return result if final else result[0]


def merge_kernel(own, far, out):
    rows = own.shape[1]
    stats = far[2 * HD :, :].astype(F32)
    pick = lambda i: stats[3 * i : 3 * i + 1] + stats[3 * i + 1 : 3 * i + 2] + stats[3 * i + 2 : 3 * i + 3]
    top0, total0, ratio0 = (own[2 * HD + i : 2 * HD + i + 1, :] for i in range(3))
    top1, total1, ratio1 = pick(0), pick(1), pick(2)
    top = jnp.maximum(top0, top1)
    part0 = total0 * jnp.exp2(top0 - top)
    part1 = total1 * jnp.exp2(top1 - top)
    inverse = 1.0 / (part0 + part1)
    part0, part1 = part0 * inverse, part1 * inverse
    att0, att1 = own[0:HD, :], far[0:HD, :].astype(F32)
    tan0, tan1 = own[HD : 2 * HD, :], far[HD : 2 * HD, :].astype(F32)
    attention = part0 * att0 + part1 * att1
    tangent = part0 * tan0 + part1 * tan1 + (part0 * part1 * (ratio0 - ratio1)) * (att0 - att1)
    out[0:rows, :] = attention.T.astype(BF16)
    out[rows:, :] = tangent.T.astype(BF16)


def merge(heads, own, far):
    rows = own.shape[1]
    tall, far_tall = own.shape[0] // heads, far.shape[0] // heads
    return pl.pallas_call(
        merge_kernel,
        grid=(heads,),
        out_shape=jax.ShapeDtypeStruct((2 * rows, heads * HD), BF16),
        in_specs=[
            pl.BlockSpec((tall, rows), lambda h: (h, 0)),
            pl.BlockSpec((far_tall, rows), lambda h: (h, 0)),
        ],
        out_specs=pl.BlockSpec((2 * rows, HD), lambda h: (0, h)),
        compiler_params=params(),
        cost_estimate=pl.CostEstimate(
            flops=0, bytes_accessed=heads * rows * HD * 14, transcendentals=0
        ),
        name="merge",
    )(own, far)


def project_kernel(first, heads, with_acc, *refs):
    refs = list(refs)
    out = refs.pop()
    acc = refs.pop() if with_acc else None
    shared, local = refs.pop(), refs.pop()
    left = jnp.concatenate([r[...] for r in refs], axis=1)
    rows = slice(first * HD, (first + heads) * HD)
    right = [local[rows, :]] + [shared[d, rows, :] for d in range(shared.shape[0])]
    total = jnp.dot(left, jnp.concatenate(right, axis=0), preferred_element_type=F32)
    if with_acc:
        total = total + acc[...]
    out[...] = total.astype(out.dtype)


def project(first, heads, atts, local, shared, half, acc, dtype):
    rows = atts[0].shape[0]
    quarters, others, depth, step = shared.shape
    count = quarters // 2
    whole = pl.BlockSpec((rows, heads * HD), lambda i: (0, 0))
    acc_spec = pl.BlockSpec((rows, step), lambda i: (0, i))
    extra = [] if acc is None else [acc]
    return pl.pallas_call(
        functools.partial(project_kernel, first, heads, acc is not None),
        grid=(count,),
        out_shape=jax.ShapeDtypeStruct((rows, count * step), dtype),
        in_specs=[whole] * len(atts)
        + [
            pl.BlockSpec((depth, step), lambda i: (0, half * count + i)),
            pl.BlockSpec((None, others, depth, step), lambda i: (half * count + i, 0, 0, 0)),
        ]
        + [acc_spec] * len(extra),
        out_specs=acc_spec,
        compiler_params=params(),
        cost_estimate=pl.CostEstimate(
            flops=2 * rows * count * step * HD * len(atts) * heads,
            bytes_accessed=rows * count * step * 6 + depth * count * step * 8,
            transcendentals=0,
        ),
        name="project",
    )(*atts, local, shared, *extra)


def finish_kernel(mine, other, res, res_t, gate, gate_t, out, out_t):
    rows = res.shape[0]
    projected = mine[0:rows, :] + other[0:rows, :].astype(F32)
    projected_t = mine[rows:, :] + other[rows:, :].astype(F32)
    g = gate[...]
    out[...] = (res[...].astype(F32) + g * projected).astype(out.dtype)
    out_t[...] = (res_t[...].astype(F32) + gate_t[...] * projected + g * projected_t).astype(
        out_t.dtype
    )


def finish(mine, other, res, res_t, gate, gate_t):
    rows, width = res.shape
    step = 256
    tall = pl.BlockSpec((2 * rows, step), lambda i: (0, i))
    short = pl.BlockSpec((rows, step), lambda i: (0, i))
    line = pl.BlockSpec((1, step), lambda i: (0, i))
    return pl.pallas_call(
        finish_kernel,
        grid=(width // step,),
        out_shape=[jax.ShapeDtypeStruct((rows, width), BF16)] * 2,
        in_specs=[tall, tall, short, short, line, line],
        out_specs=[short, short],
        compiler_params=params(),
        cost_estimate=pl.CostEstimate(flops=0, bytes_accessed=rows * width * 20, transcendentals=0),
        name="finish",
    )(mine, other, res, res_t, gate[None, :], gate_t[None, :])


def ring_pairs(size, shift):
    return [(i, (i + shift) % size) for i in range(size)]


def after(value, *others):
    return lax.optimization_barrier((value,) + others)[0]


def per_device(sizes, q, qt, k, kt, v, vt, residual, residual_t, weight, gate, gate_t):
    n_z, n_x = sizes
    heads = q.shape[1] // HD
    features = residual.shape[1]
    groups = [(0, heads - 1), (heads - 1, 1)]
    swap = [(0, 1), (1, 0)]
    up, down = ring_pairs(n_z, 1), ring_pairs(n_z, -1)
    packs = [pack(k, kt, v, vt, first, count) for first, count in groups]
    q_own = pack_queries(q, qt)
    q_far = lax.ppermute(q_own, "y_hi", swap)

    arrivals = []
    for place, start in enumerate(packs):
        if place > 0:
            start = after(start, arrivals[0][0][0])
        forward, backward = start, start
        steps = []
        for _ in range((n_z - 1) // 2):
            forward = lax.ppermute(forward, "z", up)
            backward = lax.ppermute(backward, "z", down)
            steps.append((forward, backward))
        last_k = lax.ppermute(forward[0], "z", up)
        last_v = lax.ppermute(backward[1], "z", down)
        steps.append((last_k, last_v))
        arrivals.append(steps)

    core = lax.axis_index("core")
    place = lax.axis_index("x")
    shares = 4
    share = 2 * lax.axis_index("y_hi") + lax.axis_index("dp")
    step = 2 * features // shares
    half = share // (shares // 2)
    inner = lax.rem(share, shares // 2) * step
    pieces = []
    for d in range(1, n_x):
        target = lax.rem(place + d, n_x)
        column = (2 * target + lax.rem(core + half, 2)) * features + inner
        piece = lax.dynamic_slice_in_dim(weight, column, step, 1)
        pieces.append(lax.ppermute(piece, "x", ring_pairs(n_x, d)))
    shared = lax.all_gather(jnp.stack(pieces), ("y_hi", "dp"), axis=0)
    local = jnp.concatenate(
        [
            lax.dynamic_slice_in_dim(weight, (2 * place + core) * features, features, 1),
            lax.dynamic_slice_in_dim(weight, (2 * place + 1 - core) * features, features, 1),
        ],
        axis=1,
    )

    gathered = []
    for (first, count), own_pack, steps in zip(groups, packs, arrivals):
        run = functools.partial(attend, first, count, q_own, q_far)
        state = run([own_pack] + [b for s in steps[:2] for b in s])
        late = list(steps[2]) + [steps[3]]
        if first > 0:
            state = run(late[:-1], state=state)
            late = late[-1:]
        own, to_far = run(late, state=state, final=True)
        att = merge(count, own, lax.ppermute(to_far, "y_hi", swap))
        gathered.append(
            [att] + [lax.ppermute(att, "x", ring_pairs(n_x, d)) for d in range(1, n_x)]
        )
    run = functools.partial(project, *groups[0], gathered[0], local, shared)
    acc_other, acc_own = run(1, None, F32), run(0, None, F32)
    run = functools.partial(project, *groups[1], gathered[1], local, shared)
    to_core = run(1, acc_other, BF16)
    from_core = lax.ppermute(to_core, "core", swap)
    mine = run(0, acc_own, F32)
    return tuple(finish(mine, from_core, residual, residual_t, gate, gate_t))


def solution(mesh):
    n_z, n_x = mesh.shape["seq"] // 2, mesh.shape["head"] // 2
    fine = Mesh(
        mesh.devices.reshape(n_z, 2, n_x, 2, mesh.shape["dp"]), ("z", "y_hi", "x", "core", "dp")
    )
    tokens, width = ("dp", "z", "y_hi"), ("x", "core")
    wide = P(tokens, width)
    gates = P(("dp", "x", "core"))
    return jax.shard_map(
        functools.partial(per_device, (n_z, n_x)),
        mesh=fine,
        in_specs=(wide,) * 8 + (P(width, None), gates, gates),
        out_specs=(wide, wide),
        check_vma=False,
    )
```

profile of v0, /device:TPU:1, one launch (start us, length us, event | category | flops | bytes accessed | tf_op | source)
XLA Modules:
  0.0 162.3 jit_solution(7053962069901274414)
XLA Ops:
  8.6 2.1 %collective-permute-start.14 = (bf16[384,384]{1,0:T(8,128)(2,1)S(1)}, bf16[384,384]{1,0:T(8,128)(2,1)S(1)}, u32[]{:S(2)}, u32[]{:S(2)}) collective-permute-start(bf16[384,384]{1,0:T(8,128)(2,1)S(1)} %get-tuple-element.12), channel_id=1, source_target_pairs={{0,4},{4,8},{8,12},{12,0},{1,5},{5,9},{9,13},{13,1},{2,6},{6,10},{... | collective-permute-start | bytes 884744 | tf_op jit(solution)/shard_map/ppermute | solution.py:360
  12.0 1.6 %collective-permute-start.15 = (bf16[384,384]{1,0:T(8,128)(2,1)S(1)}, bf16[384,384]{1,0:T(8,128)(2,1)S(1)}, u32[]{:S(2)}, u32[]{:S(2)}) collective-permute-start(bf16[384,384]{1,0:T(8,128)(2,1)S(1)} %get-tuple-element.14), channel_id=1, source_target_pairs={{0,8},{4,12},{8,0},{12,4},{1,9},{5,13},{9,1},{13,5},{2,10},{6,14},... | collective-permute-start | bytes 884744 | tf_op jit(solution)/shard_map/ppermute | solution.py:360
  13.7 2.7 %collective-permute-done.14 = bf16[384,384]{1,0:T(8,128)(2,1)S(1)} collective-permute-done((bf16[384,384]{1,0:T(8,128)(2,1)S(1)}, bf16[384,384]{1,0:T(8,128)(2,1)S(1)}, u32[]{:S(2)}, u32[]{:S(2)}) %collective-permute-start.14) | collective-permute-done | bytes 294944 | tf_op jit(solution)/shard_map/ppermute | solution.py:360
  17.9 8.0 %collective-permute-done.15 = bf16[384,384]{1,0:T(8,128)(2,1)S(1)} collective-permute-done((bf16[384,384]{1,0:T(8,128)(2,1)S(1)}, bf16[384,384]{1,0:T(8,128)(2,1)S(1)}, u32[]{:S(2)}, u32[]{:S(2)}) %collective-permute-start.15) | collective-permute-done | bytes 294944 | tf_op jit(solution)/shard_map/ppermute | solution.py:360
  27.3 5.7 %collective-permute-start.19 = (bf16[2,512,256]{2,1,0:T(8,128)(2,1)S(1)}, bf16[2,512,256]{2,1,0:T(8,128)(2,1)S(1)}, u32[]{:S(2)}, u32[]{:S(2)}) collective-permute-start(bf16[2,512,256]{2,1,0:T(8,128)(2,1)S(1)} %pack.3.refs_2_.refs_7_), channel_id=1, source_target_pairs={{0,224},{32,0},{64,32},{96,64},{128,96},{160,128},{192,160},{224,1... | collective-permute-start | bytes 1572872 | tf_op jit(solution)/shard_map/ppermute | solution.py:341
  33.0 9.7 %collective-permute-done.19.refs_4_.refs_9_ = bf16[2,512,256]{2,1,0:T(8,128)(2,1)S(1)} collective-permute-done((bf16[2,512,256]{2,1,0:T(8,128)(2,1)S(1)}, bf16[2,512,256]{2,1,0:T(8,128)(2,1)S(1)}, u32[]{:S(2)}, u32[]{:S(2)}) %collective-permute-start.19) | collective-permute-done | bytes 524320 | tf_op jit(solution)/shard_map/ppermute | solution.py:341
  42.7 3.4 %collective-permute-start.20 = (bf16[2,512,256]{2,1,0:T(8,128)(2,1)S(1)}, bf16[2,512,256]{2,1,0:T(8,128)(2,1)S(1)}, u32[]{:S(2)}, u32[]{:S(2)}) collective-permute-start(bf16[2,512,256]{2,1,0:T(8,128)(2,1)S(1)} %collective-permute-done.19.refs_4_.refs_9_), channel_id=1, source_target_pairs={{0,224},{32,0},{64,32},{96,64},{128,96},{160,128},{192,160},{224,1... | collective-permute-start | bytes 1572872 | tf_op jit(solution)/shard_map/ppermute | solution.py:341
  47.7 7.1 %collective-permute-done.20.refs_6_.refs_11_ = bf16[2,512,256]{2,1,0:T(8,128)(2,1)S(1)} collective-permute-done((bf16[2,512,256]{2,1,0:T(8,128)(2,1)S(1)}, bf16[2,512,256]{2,1,0:T(8,128)(2,1)S(1)}, u32[]{:S(2)}, u32[]{:S(2)}) %collective-permute-start.20) | collective-permute-done | bytes 524320 | tf_op jit(solution)/shard_map/ppermute | solution.py:341
  54.8 3.5 %collective-permute-start.21 = (bf16[2,512,256]{2,1,0:T(8,128)(2,1)S(1)}, bf16[2,512,256]{2,1,0:T(8,128)(2,1)S(1)}, u32[]{:S(2)}, u32[]{:S(2)}) collective-permute-start(bf16[2,512,256]{2,1,0:T(8,128)(2,1)S(1)} %collective-permute-done.20.refs_6_.refs_11_), channel_id=1, source_target_pairs={{0,224},{32,0},{64,32},{96,64},{128,96},{160,128},{192,160},{224,1... | collective-permute-start | bytes 1572872 | tf_op jit(solution)/shard_map/ppermute | solution.py:341
  59.0 2.7 %collective-permute-start.6 = (bf16[2,256,256]{2,1,0:T(8,128)(2,1)S(1)}, bf16[2,256,256]{2,1,0:T(8,128)(2,1)S(1)}, u32[]{:S(2)}, u32[]{:S(2)}) collective-permute-start(bf16[2,256,256]{2,1,0:T(8,128)(2,1)S(1)} %pack.2.refs_2_.refs_7_), channel_id=1, source_target_pairs={{0,224},{32,0},{64,32},{96,64},{128,96},{160,128},{192,160},{224,1... | collective-permute-start | bytes 786440 | tf_op jit(solution)/shard_map/ppermute | solution.py:341
  62.0 2.9 %collective-permute-start = (bf16[256,768]{1,0:T(8,128)(2,1)S(1)}, bf16[256,768]{1,0:T(8,128)(2,1)S(1)}, u32[]{:S(2)}, u32[]{:S(2)}) collective-permute-start(bf16[256,768]{1,0:T(8,128)(2,1)S(1)} %pack_queries.1.refs_0_), channel_id=1, source_target_pairs={{0,16},{16,0},{1,17},{17,1},{2,18},{18,2},{3,19},{19,3},{4,20},{20... | collective-permute-start | bytes 1179656 | tf_op jit(solution)/shard_map/ppermute | solution.py:331
  64.9 7.0 %collective-permute-done.6.refs_4_.refs_9_ = bf16[2,256,256]{2,1,0:T(8,128)(2,1)S(1)} collective-permute-done((bf16[2,256,256]{2,1,0:T(8,128)(2,1)S(1)}, bf16[2,256,256]{2,1,0:T(8,128)(2,1)S(1)}, u32[]{:S(2)}, u32[]{:S(2)}) %collective-permute-start.6) | collective-permute-done | bytes 262176 | tf_op jit(solution)/shard_map/ppermute | solution.py:341
  71.9 3.5 %collective-permute-start.7 = (bf16[2,256,256]{2,1,0:T(8,128)(2,1)S(1)}, bf16[2,256,256]{2,1,0:T(8,128)(2,1)}, u32[]{:S(2)}, u32[]{:S(2)}) collective-permute-start(bf16[2,256,256]{2,1,0:T(8,128)(2,1)S(1)} %collective-permute-done.6.refs_4_.refs_9_), channel_id=1, source_target_pairs={{0,224},{32,0},{64,32},{96,64},{128,96},{160,128},{192,160},{224,1... | collective-permute-start | bytes 786440 | tf_op jit(solution)/shard_map/ppermute | solution.py:341
  75.7 2.7 %collective-permute-start.23 = (bf16[512,256]{1,0:T(8,128)(2,1)S(1)}, bf16[512,256]{1,0:T(8,128)(2,1)}, u32[]{:S(2)}, u32[]{:S(2)}) collective-permute-start(bf16[512,256]{1,0:T(8,128)(2,1)S(1)} %slice_bitcast_fusion), channel_id=1, source_target_pairs={{0,224},{32,0},{64,32},{96,64},{128,96},{160,128},{192,160},{224,1... | collective-permute-start | bytes 786440 | tf_op jit(solution)/shard_map/ppermute | solution.py:344
  79.2 3.1 %collective-permute-start.8 = (bf16[2,256,256]{2,1,0:T(8,128)(2,1)}, bf16[2,256,256]{2,1,0:T(8,128)(2,1)S(1)}, u32[]{:S(2)}, u32[]{:S(2)}) collective-permute-start(bf16[2,256,256]{2,1,0:T(8,128)(2,1)} %collective-permute-done.7.refs_6_.refs_11_), channel_id=1, source_target_pairs={{0,224},{32,0},{64,32},{96,64},{128,96},{160,128},{192,160},{224,1... | collective-permute-start | bytes 786440 | tf_op jit(solution)/shard_map/ppermute | solution.py:341
  86.6 6.2 %attend.8.refs_8_ = f32[1056,256]{1,0:T(8,128)S(1)} custom-call(bf16[256,768]{1,0:T(8,128)(2,1)S(1)} %pack_queries.1.refs_0_, bf16[256,768]{1,0:T(8,128)(2,1)S(1)} %collective-permute-done.refs_1_, bf16[2,512,256]{2,1,0:T(8,128)(2,1)S(1)} %pack.3.refs_2_.refs_7_, bf16[2,512,256]{2,1,0:T(8,128)(2,1)S(1)} %copy-done.11, bf16[2,512,256]{2,1,0:T(8,128)(2,1)S(1)} %copy-done.9, ...), custom_call_target="tpu_custom_call" | custom-call | flops 2684354560 | bytes 3670016 | tf_op jit(solution)/shard_map/attend/pallas_call | solution.py:186
  92.9 4.6 %attend.9 = (f32[528,256]{1,0:T(8,128)S(1)}, bf16[544,256]{1,0:T(8,128)(2,1)S(1)}) custom-call(bf16[256,768]{1,0:T(8,128)(2,1)S(1)} %pack_queries.1.refs_0_, bf16[256,768]{1,0:T(8,128)(2,1)S(1)} %collective-permute-done.refs_1_, bf16[2,512,256]{2,1,0:T(8,128)(2,1)S(1)} %collective-permute-done.18.refs_2_.refs_5_, ...), custom_call_target="tpu_custom_call" | custom-call | flops 1610612736 | bytes 2621440 | tf_op jit(solution)/shard_map/attend/pallas_call | solution.py:186
  97.5 2.7 %collective-permute-start.24 = (bf16[544,256]{1,0:T(8,128)(2,1)S(1)}, bf16[544,256]{1,0:T(8,128)(2,1)S(1)}, u32[]{:S(2)}, u32[]{:S(2)}) collective-permute-start(bf16[544,256]{1,0:T(8,128)(2,1)S(1)} %get-tuple-element.11), channel_id=1, source_target_pairs={{0,16},{16,0},{1,17},{17,1},{2,18},{18,2},{3,19},{19,3},{4,20},{20... | collective-permute-start | bytes 835592 | tf_op jit(solution)/shard_map/ppermute | solution.py:379
  100.2 2.7 %collective-permute-start.9 = (bf16[256,256]{1,0:T(8,128)(2,1)S(1)}, bf16[256,256]{1,0:T(8,128)(2,1)S(1)}, u32[]{:S(2)}, u32[]{:S(2)}) collective-permute-start(bf16[256,256]{1,0:T(8,128)(2,1)S(1)} %slice_bitcast_fusion.2), channel_id=1, source_target_pairs={{0,224},{32,0},{64,32},{96,64},{128,96},{160,128},{192,160},{224,1... | collective-permute-start | bytes 393224 | tf_op jit(solution)/shard_map/ppermute | solution.py:344
  105.3 4.2 %attend.5.refs_6_ = f32[528,256]{1,0:T(8,128)S(1)} custom-call(bf16[256,768]{1,0:T(8,128)(2,1)S(1)} %pack_queries.1.refs_0_, bf16[256,768]{1,0:T(8,128)(2,1)S(1)} %collective-permute-done.refs_1_, bf16[2,256,256]{2,1,0:T(8,128)(2,1)S(1)} %pack.2.refs_2_.refs_7_, bf16[2,256,256]{2,1,0:T(8,128)(2,1)S(1)} %copy-done.19, bf16[2,256,256]{2,1,0:T(8,128)(2,1)S(1)} %copy-done.17, ...), custom_call_target="tpu_custom_call" | custom-call | flops 1342177280 | bytes 1835008 | tf_op jit(solution)/shard_map/attend/pallas_call | solution.py:186
  111.6 2.6 %collective-permute-start.10 = (bf16[272,256]{1,0:T(8,128)(2,1)S(1)}, bf16[272,256]{1,0:T(8,128)(2,1)S(1)}, u32[]{:S(2)}, u32[]{:S(2)}) collective-permute-start(bf16[272,256]{1,0:T(8,128)(2,1)S(1)} %get-tuple-element.9), channel_id=1, source_target_pairs={{0,16},{16,0},{1,17},{17,1},{2,18},{18,2},{3,19},{19,3},{4,20},{20... | collective-permute-start | bytes 417800 | tf_op jit(solution)/shard_map/ppermute | solution.py:379
  115.5 1.6 collective-permute-done.10.far
  118.0 2.4 %collective-permute-start.12 = (bf16[512,128]{1,0:T(8,128)(2,1)S(1)}, bf16[512,128]{1,0:T(8,128)(2,1)S(1)}, u32[]{:S(2)}, u32[]{:S(2)}) collective-permute-start(bf16[512,128]{1,0:T(8,128)(2,1)S(1)} %merge.2.refs_0_), channel_id=1, source_target_pairs={{0,8},{4,12},{8,0},{12,4},{1,9},{5,13},{9,1},{13,5},{2,10},{6,14},... | collective-permute-start | bytes 393224 | tf_op jit(solution)/shard_map/ppermute | solution.py:381
  120.4 1.9 %collective-permute-start.26 = (bf16[512,256]{1,0:T(8,128)(2,1)S(1)}, bf16[512,256]{1,0:T(8,128)(2,1)S(1)}, u32[]{:S(2)}, u32[]{:S(2)}) collective-permute-start(bf16[512,256]{1,0:T(8,128)(2,1)S(1)} %merge.3.refs_0_), channel_id=1, source_target_pairs={{0,8},{4,12},{8,0},{12,4},{1,9},{5,13},{9,1},{13,5},{2,10},{6,14},... | collective-permute-start | bytes 786440 | tf_op jit(solution)/shard_map/ppermute | solution.py:381
  123.8 3.9 %collective-permute-done.26.refs_2_ = bf16[512,256]{1,0:T(8,128)(2,1)S(1)} collective-permute-done((bf16[512,256]{1,0:T(8,128)(2,1)S(1)}, bf16[512,256]{1,0:T(8,128)(2,1)S(1)}, u32[]{:S(2)}, u32[]{:S(2)}) %collective-permute-start.26) | collective-permute-done | bytes 262176 | tf_op jit(solution)/shard_map/ppermute | solution.py:381
  127.6 3.4 %collective-permute-done.25.refs_1_ = bf16[512,256]{1,0:T(8,128)(2,1)S(1)} collective-permute-done((bf16[512,256]{1,0:T(8,128)(2,1)S(1)}, bf16[512,256]{1,0:T(8,128)(2,1)S(1)}, u32[]{:S(2)}, u32[]{:S(2)}) %collective-permute-start.25) | collective-permute-done | bytes 262176 | tf_op jit(solution)/shard_map/ppermute | solution.py:381
  131.1 2.7 %project.6.refs_6_ = f32[512,768]{1,0:T(8,128)S(1)} custom-call(bf16[512,256]{1,0:T(8,128)(2,1)S(1)} %merge.3.refs_0_, bf16[512,256]{1,0:T(8,128)(2,1)S(1)} %collective-permute-done.25.refs_1_, bf16[512,256]{1,0:T(8,128)(2,1)S(1)} %collective-permute-done.26.refs_2_, bf16[512,256]{1,0:T(8,128)(2,1)S(1)} %collective-permute-done.27.refs_3_, ...), custom_call_target="tpu_custom_call" | custom-call | flops 805306368 | bytes 4718592 | tf_op jit(solution)/shard_map/project/pallas_call | solution.py:264
  133.9 2.2 %project.7 = bf16[512,768]{1,0:T(8,128)(2,1)S(1)} custom-call(bf16[512,128]{1,0:T(8,128)(2,1)S(1)} %merge.2.refs_0_, bf16[512,128]{1,0:T(8,128)(2,1)S(1)} %collective-permute-done.11.refs_1_, bf16[512,128]{1,0:T(8,128)(2,1)S(1)} %collective-permute-done.12.refs_2_, bf16[512,128]{1,0:T(8,128)(2,1)S(1)} %collective-permute-done.13.refs_3_, ...), custom_call_target="tpu_custom_call" | custom-call | flops 402653184 | bytes 4718592 | tf_op jit(solution)/shard_map/project/pallas_call | solution.py:264
  136.1 12.5 %collective-permute-start.28 = (bf16[512,768]{1,0:T(8,128)(2,1)S(1)}, bf16[512,768]{1,0:T(8,128)(2,1)S(1)}, u32[]{:S(2)}, u32[]{:S(2)}) collective-permute-start(bf16[512,768]{1,0:T(8,128)(2,1)S(1)} %project.7), channel_id=1, source_target_pairs={{0,2},{2,0},{1,3},{3,1},{4,6},{6,4},{5,7},{7,5},{8,10},{10,8},{9,1... | collective-permute-start | bytes 2359304 | tf_op jit(solution)/shard_map/ppermute | solution.py:387
  148.6 2.7 %project.4.refs_6_ = f32[512,768]{1,0:T(8,128)S(1)} custom-call(bf16[512,256]{1,0:T(8,128)(2,1)S(1)} %merge.3.refs_0_, bf16[512,256]{1,0:T(8,128)(2,1)S(1)} %collective-permute-done.25.refs_1_, bf16[512,256]{1,0:T(8,128)(2,1)S(1)} %collective-permute-done.26.refs_2_, bf16[512,256]{1,0:T(8,128)(2,1)S(1)} %collective-permute-done.27.refs_3_, ...), custom_call_target="tpu_custom_call" | custom-call | flops 805306368 | bytes 4718592 | tf_op jit(solution)/shard_map/project/pallas_call | solution.py:264
  151.3 2.4 %project.5.mine = f32[512,768]{1,0:T(8,128)S(1)} custom-call(bf16[512,128]{1,0:T(8,128)(2,1)S(1)} %merge.2.refs_0_, bf16[512,128]{1,0:T(8,128)(2,1)S(1)} %collective-permute-done.11.refs_1_, bf16[512,128]{1,0:T(8,128)(2,1)S(1)} %collective-permute-done.12.refs_2_, bf16[512,128]{1,0:T(8,128)(2,1)S(1)} %collective-permute-done.13.refs_3_, ...), custom_call_target="tpu_custom_call" | custom-call | flops 402653184 | bytes 4718592 | tf_op jit(solution)/shard_map/project/pallas_call | solution.py:264
  153.7 1.7 %finish.1 = (bf16[256,768]{1,0:T(8,128)(2,1)}, bf16[256,768]{1,0:T(8,128)(2,1)}) custom-call(f32[512,768]{1,0:T(8,128)S(1)} %project.5.mine, bf16[512,768]{1,0:T(8,128)(2,1)S(1)} %collective-permute-done.28.other, bf16[256,768]{1,0:T(8,128)(2,1)S(1)} %copy-done.4, bf16[256,768]{1,0:T(8,128)(2,1)S(1)} %copy-done.5, f32[1,768]{1,0:T(1,128)S(1)} %broadcast_in_dim.6.gate, ...), custom_call_target="tpu_custom_call" | custom-call | bytes 3932160 | tf_op jit(solution)/shard_map/finish/pallas_call | solution.py:302
  (98 shorter events, 21.6 us)
Async XLA Ops:
  7.2 123.9 %all-gather.3.cloned.1.call-start = ((), (), s32[]{:S(2)}) async-start(), calls=%async_computation | async-start | bytes 4423680 | tf_op jit(solution)/shard_map/all_gather | solution.py:361
  8.6 7.8 %collective-permute-start.14 = (bf16[384,384]{1,0:T(8,128)(2,1)S(1)}, bf16[384,384]{1,0:T(8,128)(2,1)S(1)}, u32[]{:S(2)}, u32[]{:S(2)}) collective-permute-start(bf16[384,384]{1,0:T(8,128)(2,1)S(1)} %get-tuple-element.12), channel_id=1, source_target_pairs={{0,4},{4,8},{8,12},{12,0},{1,5},{5,9},{9,13},{13,1},{2,6},{6,10},{... | collective-permute-start | bytes 884744 | tf_op jit(solution)/shard_map/ppermute | solution.py:360
  10.7 7.2 %collective-permute-start.16 = (bf16[384,384]{1,0:T(8,128)(2,1)S(1)}, bf16[384,384]{1,0:T(8,128)(2,1)S(1)}, u32[]{:S(2)}, u32[]{:S(2)}) collective-permute-start(bf16[384,384]{1,0:T(8,128)(2,1)S(1)} %get-tuple-element.13), channel_id=1, source_target_pairs={{0,12},{4,0},{8,4},{12,8},{1,13},{5,1},{9,5},{13,9},{2,14},{6,2},{... | collective-permute-start | bytes 884744 | tf_op jit(solution)/shard_map/ppermute | solution.py:360
  12.0 13.8 %collective-permute-start.15 = (bf16[384,384]{1,0:T(8,128)(2,1)S(1)}, bf16[384,384]{1,0:T(8,128)(2,1)S(1)}, u32[]{:S(2)}, u32[]{:S(2)}) collective-permute-start(bf16[384,384]{1,0:T(8,128)(2,1)S(1)} %get-tuple-element.14), channel_id=1, source_target_pairs={{0,8},{4,12},{8,0},{12,4},{1,9},{5,13},{9,1},{13,5},{2,10},{6,14},... | collective-permute-start | bytes 884744 | tf_op jit(solution)/shard_map/ppermute | solution.py:360
  26.9 34.8 %copy-start.6 = (bf16[256,384]{1,0:T(8,128)(2,1)S(1)}, bf16[256,384]{1,0:T(8,128)(2,1)}, u32[]{:S(2)}) copy-start(bf16[256,384]{1,0:T(8,128)(2,1)} %q.1) | copy-start | bytes 589828
  26.9 34.8 %copy-start.7 = (bf16[256,384]{1,0:T(8,128)(2,1)S(1)}, bf16[256,384]{1,0:T(8,128)(2,1)}, u32[]{:S(2)}) copy-start(bf16[256,384]{1,0:T(8,128)(2,1)} %qt.1) | copy-start | bytes 589828
  27.3 15.3 %collective-permute-start.19 = (bf16[2,512,256]{2,1,0:T(8,128)(2,1)S(1)}, bf16[2,512,256]{2,1,0:T(8,128)(2,1)S(1)}, u32[]{:S(2)}, u32[]{:S(2)}) collective-permute-start(bf16[2,512,256]{2,1,0:T(8,128)(2,1)S(1)} %pack.3.refs_2_.refs_7_), channel_id=1, source_target_pairs={{0,224},{32,0},{64,32},{96,64},{128,96},{160,128},{192,160},{224,1... | collective-permute-start | bytes 1572872 | tf_op jit(solution)/shard_map/ppermute | solution.py:341
  33.0 13.9 %collective-permute-start.1 = (bf16[2,512,256]{2,1,0:T(8,128)(2,1)S(1)}, bf16[2,512,256]{2,1,0:T(8,128)(2,1)S(1)}, u32[]{:S(2)}, u32[]{:S(2)}) collective-permute-start(bf16[2,512,256]{2,1,0:T(8,128)(2,1)S(1)} %pack.3.refs_2_.refs_7_), channel_id=1, source_target_pairs={{0,32},{32,64},{64,96},{96,128},{128,160},{160,192},{192,224},{224... | collective-permute-start | bytes 1572872 | tf_op jit(solution)/shard_map/ppermute | solution.py:340
  42.7 12.2 %collective-permute-start.20 = (bf16[2,512,256]{2,1,0:T(8,128)(2,1)S(1)}, bf16[2,512,256]{2,1,0:T(8,128)(2,1)S(1)}, u32[]{:S(2)}, u32[]{:S(2)}) collective-permute-start(bf16[2,512,256]{2,1,0:T(8,128)(2,1)S(1)} %collective-permute-done.19.refs_4_.refs_9_), channel_id=1, source_target_pairs={{0,224},{32,0},{64,32},{96,64},{128,96},{160,128},{192,160},{224,1... | collective-permute-start | bytes 1572872 | tf_op jit(solution)/shard_map/ppermute | solution.py:341
  46.9 12.0 %collective-permute-start.17 = (bf16[2,512,256]{2,1,0:T(8,128)(2,1)S(1)}, bf16[2,512,256]{2,1,0:T(8,128)(2,1)S(1)}, u32[]{:S(2)}, u32[]{:S(2)}) collective-permute-start(bf16[2,512,256]{2,1,0:T(8,128)(2,1)S(1)} %collective-permute-done.1.refs_3_.refs_8_), channel_id=1, source_target_pairs={{0,32},{32,64},{64,96},{96,128},{128,160},{160,192},{192,224},{224... | collective-permute-start | bytes 1572872 | tf_op jit(solution)/shard_map/ppermute | solution.py:340
  54.8 20.8 %collective-permute-start.21 = (bf16[2,512,256]{2,1,0:T(8,128)(2,1)S(1)}, bf16[2,512,256]{2,1,0:T(8,128)(2,1)S(1)}, u32[]{:S(2)}, u32[]{:S(2)}) collective-permute-start(bf16[2,512,256]{2,1,0:T(8,128)(2,1)S(1)} %collective-permute-done.20.refs_6_.refs_11_), channel_id=1, source_target_pairs={{0,224},{32,0},{64,32},{96,64},{128,96},{160,128},{192,160},{224,1... | collective-permute-start | bytes 1572872 | tf_op jit(solution)/shard_map/ppermute | solution.py:341
  58.9 19.6 %collective-permute-start.18 = (bf16[2,512,256]{2,1,0:T(8,128)(2,1)S(1)}, bf16[2,512,256]{2,1,0:T(8,128)(2,1)S(1)}, u32[]{:S(2)}, u32[]{:S(2)}) collective-permute-start(bf16[2,512,256]{2,1,0:T(8,128)(2,1)S(1)} %collective-permute-done.17.refs_5_.refs_10_), channel_id=1, source_target_pairs={{0,32},{32,64},{64,96},{96,128},{128,160},{160,192},{192,224},{224... | collective-permute-start | bytes 1572872 | tf_op jit(solution)/shard_map/ppermute | solution.py:340
  59.0 12.9 %collective-permute-start.6 = (bf16[2,256,256]{2,1,0:T(8,128)(2,1)S(1)}, bf16[2,256,256]{2,1,0:T(8,128)(2,1)S(1)}, u32[]{:S(2)}, u32[]{:S(2)}) collective-permute-start(bf16[2,256,256]{2,1,0:T(8,128)(2,1)S(1)} %pack.2.refs_2_.refs_7_), channel_id=1, source_target_pairs={{0,224},{32,0},{64,32},{96,64},{128,96},{160,128},{192,160},{224,1... | collective-permute-start | bytes 786440 | tf_op jit(solution)/shard_map/ppermute | solution.py:341
  61.7 13.9 %collective-permute-start.2 = (bf16[2,256,256]{2,1,0:T(8,128)(2,1)S(1)}, bf16[2,256,256]{2,1,0:T(8,128)(2,1)S(1)}, u32[]{:S(2)}, u32[]{:S(2)}) collective-permute-start(bf16[2,256,256]{2,1,0:T(8,128)(2,1)S(1)} %pack.2.refs_2_.refs_7_), channel_id=1, source_target_pairs={{0,32},{32,64},{64,96},{96,128},{128,160},{160,192},{192,224},{224... | collective-permute-start | bytes 786440 | tf_op jit(solution)/shard_map/ppermute | solution.py:340
  62.0 20.5 %collective-permute-start = (bf16[256,768]{1,0:T(8,128)(2,1)S(1)}, bf16[256,768]{1,0:T(8,128)(2,1)S(1)}, u32[]{:S(2)}, u32[]{:S(2)}) collective-permute-start(bf16[256,768]{1,0:T(8,128)(2,1)S(1)} %pack_queries.1.refs_0_), channel_id=1, source_target_pairs={{0,16},{16,0},{1,17},{17,1},{2,18},{18,2},{3,19},{19,3},{4,20},{20... | collective-permute-start | bytes 1179656 | tf_op jit(solution)/shard_map/ppermute | solution.py:331
  71.9 7.3 %collective-permute-start.7 = (bf16[2,256,256]{2,1,0:T(8,128)(2,1)S(1)}, bf16[2,256,256]{2,1,0:T(8,128)(2,1)}, u32[]{:S(2)}, u32[]{:S(2)}) collective-permute-start(bf16[2,256,256]{2,1,0:T(8,128)(2,1)S(1)} %collective-permute-done.6.refs_4_.refs_9_), channel_id=1, source_target_pairs={{0,224},{32,0},{64,32},{96,64},{128,96},{160,128},{192,160},{224,1... | collective-permute-start | bytes 786440 | tf_op jit(solution)/shard_map/ppermute | solution.py:341
  75.6 6.8 %collective-permute-start.3 = (bf16[2,256,256]{2,1,0:T(8,128)(2,1)S(1)}, bf16[2,256,256]{2,1,0:T(8,128)(2,1)}, u32[]{:S(2)}, u32[]{:S(2)}) collective-permute-start(bf16[2,256,256]{2,1,0:T(8,128)(2,1)S(1)} %collective-permute-done.2.refs_3_.refs_8_), channel_id=1, source_target_pairs={{0,32},{32,64},{64,96},{96,128},{128,160},{160,192},{192,224},{224... | collective-permute-start | bytes 786440 | tf_op jit(solution)/shard_map/ppermute | solution.py:340
  75.7 17.2 %collective-permute-start.23 = (bf16[512,256]{1,0:T(8,128)(2,1)S(1)}, bf16[512,256]{1,0:T(8,128)(2,1)}, u32[]{:S(2)}, u32[]{:S(2)}) collective-permute-start(bf16[512,256]{1,0:T(8,128)(2,1)S(1)} %slice_bitcast_fusion), channel_id=1, source_target_pairs={{0,224},{32,0},{64,32},{96,64},{128,96},{160,128},{192,160},{224,1... | collective-permute-start | bytes 786440 | tf_op jit(solution)/shard_map/ppermute | solution.py:344
  79.2 13.7 %collective-permute-start.22 = (bf16[512,256]{1,0:T(8,128)(2,1)}, bf16[512,256]{1,0:T(8,128)(2,1)}, u32[]{:S(2)}, u32[]{:S(2)}) collective-permute-start(bf16[512,256]{1,0:T(8,128)(2,1)} %slice_bitcast_fusion.1), channel_id=1, source_target_pairs={{0,32},{32,64},{64,96},{96,128},{128,160},{160,192},{192,224},{224... | collective-permute-start | bytes 786440 | tf_op jit(solution)/shard_map/ppermute | solution.py:343
  79.2 21.0 %collective-permute-start.8 = (bf16[2,256,256]{2,1,0:T(8,128)(2,1)}, bf16[2,256,256]{2,1,0:T(8,128)(2,1)S(1)}, u32[]{:S(2)}, u32[]{:S(2)}) collective-permute-start(bf16[2,256,256]{2,1,0:T(8,128)(2,1)} %collective-permute-done.7.refs_6_.refs_11_), channel_id=1, source_target_pairs={{0,224},{32,0},{64,32},{96,64},{128,96},{160,128},{192,160},{224,1... | collective-permute-start | bytes 786440 | tf_op jit(solution)/shard_map/ppermute | solution.py:341
  82.5 20.5 %collective-permute-start.4 = (bf16[2,256,256]{2,1,0:T(8,128)(2,1)}, bf16[2,256,256]{2,1,0:T(8,128)(2,1)S(1)}, u32[]{:S(2)}, u32[]{:S(2)}) collective-permute-start(bf16[2,256,256]{2,1,0:T(8,128)(2,1)} %collective-permute-done.3.refs_5_.refs_10_), channel_id=1, source_target_pairs={{0,32},{32,64},{64,96},{96,128},{128,160},{160,192},{192,224},{224... | collective-permute-start | bytes 786440 | tf_op jit(solution)/shard_map/ppermute | solution.py:340
  97.5 7.0 %collective-permute-start.24 = (bf16[544,256]{1,0:T(8,128)(2,1)S(1)}, bf16[544,256]{1,0:T(8,128)(2,1)S(1)}, u32[]{:S(2)}, u32[]{:S(2)}) collective-permute-start(bf16[544,256]{1,0:T(8,128)(2,1)S(1)} %get-tuple-element.11), channel_id=1, source_target_pairs={{0,16},{16,0},{1,17},{17,1},{2,18},{18,2},{3,19},{19,3},{4,20},{20... | collective-permute-start | bytes 835592 | tf_op jit(solution)/shard_map/ppermute | solution.py:379
  100.2 10.4 %collective-permute-start.9 = (bf16[256,256]{1,0:T(8,128)(2,1)S(1)}, bf16[256,256]{1,0:T(8,128)(2,1)S(1)}, u32[]{:S(2)}, u32[]{:S(2)}) collective-permute-start(bf16[256,256]{1,0:T(8,128)(2,1)S(1)} %slice_bitcast_fusion.2), channel_id=1, source_target_pairs={{0,224},{32,0},{64,32},{96,64},{128,96},{160,128},{192,160},{224,1... | collective-permute-start | bytes 393224 | tf_op jit(solution)/shard_map/ppermute | solution.py:344
  103.0 7.7 %collective-permute-start.5 = (bf16[256,256]{1,0:T(8,128)(2,1)S(1)}, bf16[256,256]{1,0:T(8,128)(2,1)S(1)}, u32[]{:S(2)}, u32[]{:S(2)}) collective-permute-start(bf16[256,256]{1,0:T(8,128)(2,1)S(1)} %slice_bitcast_fusion.3), channel_id=1, source_target_pairs={{0,32},{32,64},{64,96},{96,128},{128,160},{160,192},{192,224},{224... | collective-permute-start | bytes 393224 | tf_op jit(solution)/shard_map/ppermute | solution.py:343
  104.9 17.4 %collective-permute-start.27 = (bf16[512,256]{1,0:T(8,128)(2,1)S(1)}, bf16[512,256]{1,0:T(8,128)(2,1)S(1)}, u32[]{:S(2)}, u32[]{:S(2)}) collective-permute-start(bf16[512,256]{1,0:T(8,128)(2,1)S(1)} %merge.3.refs_0_), channel_id=1, source_target_pairs={{0,12},{4,0},{8,4},{12,8},{1,13},{5,1},{9,5},{13,9},{2,14},{6,2},{... | collective-permute-start | bytes 786440 | tf_op jit(solution)/shard_map/ppermute | solution.py:381
  111.6 5.5 %collective-permute-start.10 = (bf16[272,256]{1,0:T(8,128)(2,1)S(1)}, bf16[272,256]{1,0:T(8,128)(2,1)S(1)}, u32[]{:S(2)}, u32[]{:S(2)}) collective-permute-start(bf16[272,256]{1,0:T(8,128)(2,1)S(1)} %get-tuple-element.9), channel_id=1, source_target_pairs={{0,16},{16,0},{1,17},{17,1},{2,18},{18,2},{3,19},{19,3},{4,20},{20... | collective-permute-start | bytes 417800 | tf_op jit(solution)/shard_map/ppermute | solution.py:379
  117.2 16.6 %collective-permute-start.13 = (bf16[512,128]{1,0:T(8,128)(2,1)S(1)}, bf16[512,128]{1,0:T(8,128)(2,1)S(1)}, u32[]{:S(2)}, u32[]{:S(2)}) collective-permute-start(bf16[512,128]{1,0:T(8,128)(2,1)S(1)} %merge.2.refs_0_), channel_id=1, source_target_pairs={{0,12},{4,0},{8,4},{12,8},{1,13},{5,1},{9,5},{13,9},{2,14},{6,2},{... | collective-permute-start | bytes 393224 | tf_op jit(solution)/shard_map/ppermute | solution.py:381
  118.0 15.8 %collective-permute-start.12 = (bf16[512,128]{1,0:T(8,128)(2,1)S(1)}, bf16[512,128]{1,0:T(8,128)(2,1)S(1)}, u32[]{:S(2)}, u32[]{:S(2)}) collective-permute-start(bf16[512,128]{1,0:T(8,128)(2,1)S(1)} %merge.2.refs_0_), channel_id=1, source_target_pairs={{0,8},{4,12},{8,0},{12,4},{1,9},{5,13},{9,1},{13,5},{2,10},{6,14},... | collective-permute-start | bytes 393224 | tf_op jit(solution)/shard_map/ppermute | solution.py:381
  120.4 13.4 %collective-permute-start.11 = (bf16[512,128]{1,0:T(8,128)(2,1)S(1)}, bf16[512,128]{1,0:T(8,128)(2,1)S(1)}, u32[]{:S(2)}, u32[]{:S(2)}) collective-permute-start(bf16[512,128]{1,0:T(8,128)(2,1)S(1)} %merge.2.refs_0_), channel_id=1, source_target_pairs={{0,4},{4,8},{8,12},{12,0},{1,5},{5,9},{9,13},{13,1},{2,6},{6,10},{... | collective-permute-start | bytes 393224 | tf_op jit(solution)/shard_map/ppermute | solution.py:381
  120.4 7.2 %collective-permute-start.26 = (bf16[512,256]{1,0:T(8,128)(2,1)S(1)}, bf16[512,256]{1,0:T(8,128)(2,1)S(1)}, u32[]{:S(2)}, u32[]{:S(2)}) collective-permute-start(bf16[512,256]{1,0:T(8,128)(2,1)S(1)} %merge.3.refs_0_), channel_id=1, source_target_pairs={{0,8},{4,12},{8,0},{12,4},{1,9},{5,13},{9,1},{13,5},{2,10},{6,14},... | collective-permute-start | bytes 786440 | tf_op jit(solution)/shard_map/ppermute | solution.py:381
  122.3 8.7 %collective-permute-start.25 = (bf16[512,256]{1,0:T(8,128)(2,1)S(1)}, bf16[512,256]{1,0:T(8,128)(2,1)S(1)}, u32[]{:S(2)}, u32[]{:S(2)}) collective-permute-start(bf16[512,256]{1,0:T(8,128)(2,1)S(1)} %merge.3.refs_0_), channel_id=1, source_target_pairs={{0,4},{4,8},{8,12},{12,0},{1,5},{5,9},{9,13},{13,1},{2,6},{6,10},{... | collective-permute-start | bytes 786440 | tf_op jit(solution)/shard_map/ppermute | solution.py:381
  136.1 17.6 %collective-permute-start.28 = (bf16[512,768]{1,0:T(8,128)(2,1)S(1)}, bf16[512,768]{1,0:T(8,128)(2,1)S(1)}, u32[]{:S(2)}, u32[]{:S(2)}) collective-permute-start(bf16[512,768]{1,0:T(8,128)(2,1)S(1)} %project.7), channel_id=1, source_target_pairs={{0,2},{2,0},{1,3},{3,1},{4,6},{6,4},{5,7},{7,5},{8,10},{10,8},{9,1... | collective-permute-start | bytes 2359304 | tf_op jit(solution)/shard_map/ppermute | solution.py:387
  (20 other events, 211.4 us)
Sparse Core Ops, SparseCore 0:
  27.0 55.1 all-gather.2
where the time goes:
time: 163 us; the launch traced here: 162 us
  starting transfers between devices  60.2 us (37%)
  waiting for transfers between devices  47.3 us (29%)
  Pallas kernels  30 us (18%)
  between operations  14.5 us (9%)
  local copies, waits for them, and re-layouts  9.2 us (6%)
    ppermute x6, waiting for transfers between devices, per_device(): backward = lax.ppermute(backward, 'z', down)  23.8 us
    ppermute x6, starting transfers between devices, per_device(): backward = lax.ppermute(backward, 'z', down)  21.9 us
    pallas_call x5, Pallas kernels, attend(): pl.pallas_call(functools.partial(attend_kernel, n, state is not None, fin...  17 us
    ppermute x1, starting transfers between devices, per_device(): from_core = lax.ppermute(to_core, 'core', swap)  12.5 us
    ppermute x3, waiting for transfers between devices, per_device(): pieces.append(lax.ppermute(piece, 'x', ring_pairs(n_x, d)))  12.2 us
    pallas_call x4, Pallas kernels, project(): pl.pallas_call(functools.partial(project_kernel, first, heads, acc is not...  10 us
    ppermute x6, waiting for transfers between devices, per_device(): lax.ppermute(att, 'x', ring_pairs(n_x, d))  7.31 us
    ppermute x6, starting transfers between devices, per_device(): lax.ppermute(att, 'x', ring_pairs(n_x, d))  6.88 us
  transfers between devices with their start and end apart: 30, of which 13 were waited for; matrix products, arithmetic and copies ran while one was open for 1% of the time, Pallas kernels for 16%

commit v1 on v0

v1 whole, which is shorter than its diff:
```python
import functools

import jax
import jax.numpy as jnp
from jax import lax
from jax.experimental import pallas as pl
from jax.experimental.pallas import tpu as pltpu
from jax.sharding import Mesh
from jax.sharding import PartitionSpec as P

HD = 128
SCALE = HD ** (-0.5)
SCALE2 = SCALE * 1.4426950408889634
NT = (((1,), (1,)), ((), ()))
BF16 = jnp.bfloat16
F32 = jnp.float32
STATS = 8


def spec_whole():
    return pl.BlockSpec(memory_space=pltpu.VMEM)


def params(mib=12):
    return pltpu.CompilerParams(vmem_limit_bytes=mib * 1024 * 1024)


def query_kernel(q, qt, out, sems):
    copies = []
    for h in range(q.shape[1] // HD):
        for i, ref in enumerate((qt, q)):
            copies.append(
                pltpu.make_async_copy(
                    ref.at[:, h * HD : (h + 1) * HD],
                    out.at[:, (2 * h + i) * HD : (2 * h + i + 1) * HD],
                    sems.at[2 * h + i],
                )
            )
    for copy in copies:
        copy.start()
    for copy in copies:
        copy.wait()


def pack_queries(q, qt):
    rows, width = q.shape
    return pl.pallas_call(
        query_kernel,
        out_shape=jax.ShapeDtypeStruct((rows, 2 * width), BF16),
        in_specs=[pl.BlockSpec(memory_space=pltpu.HBM)] * 2,
        out_specs=spec_whole(),
        scratch_shapes=[pltpu.SemaphoreType.DMA((2 * width // HD,))],
        compiler_params=params(),
        cost_estimate=pl.CostEstimate(flops=0, bytes_accessed=8 * rows * width, transcendentals=0),
        name="pack_queries",
    )(q, qt)


def pack_kernel(k, kt, v, vt, out, scratch, sems):
    heads = k.shape[1] // HD
    values = [
        pltpu.make_async_copy(ref, scratch.at[i], sems.at[2 * heads + i])
        for i, ref in enumerate((v, vt))
    ]
    copies = []
    for h in range(heads):
        for i, ref in enumerate((k, kt)):
            copies.append(
                pltpu.make_async_copy(
                    ref.at[:, h * HD : (h + 1) * HD],
                    out.at[0, 2 * h * HD : 2 * (h + 1) * HD, i * HD : (i + 1) * HD],
                    sems.at[2 * h + i],
                )
            )
    for copy in values + copies:
        copy.start()
    for i, copy in enumerate(values):
        copy.wait()
        for h in range(heads):
            part = scratch[i, :, h * HD : (h + 1) * HD].T
            out[1, (2 * h + i) * HD : (2 * h + i + 1) * HD, :] = part
    for copy in copies:
        copy.wait()


def pack(k, kt, v, vt):
    rows, width = k.shape
    return pl.pallas_call(
        pack_kernel,
        out_shape=jax.ShapeDtypeStruct((2, 2 * width, rows), BF16),
        in_specs=[pl.BlockSpec(memory_space=pltpu.HBM)] * 4,
        out_specs=spec_whole(),
        scratch_shapes=[
            pltpu.VMEM((2, rows, width), BF16),
            pltpu.SemaphoreType.DMA((2 * width // HD + 2,)),
        ],
        compiler_params=params(),
        cost_estimate=pl.CostEstimate(flops=0, bytes_accessed=16 * rows * width, transcendentals=0),
        name="pack",
    )(k, kt, v, vt)


def three_parts(value):
    high = value.astype(BF16)
    rest = value - high.astype(F32)
    middle = rest.astype(BF16)
    low = (rest - middle.astype(F32)).astype(BF16)
    return [high, middle, low]


def attend_kernel(kinds, groups, with_state, final, *refs):
    refs = list(refs)
    scores_ref = refs.pop()
    q_refs = [refs.pop(0), refs.pop(0)]
    pairs = []
    for halves in kinds:
        if halves:
            pairs.append((refs.pop(0), refs.pop(0)))
        else:
            both = refs.pop(0)
            pairs.append((both.at[0], both.at[1]))
    state = refs.pop(0) if with_state else None
    keys = q_refs[0].shape[0]
    tall, far_tall = 2 * HD + STATS, 2 * HD + 2 * STATS
    where = [(g, i) for g, (_, count) in enumerate(groups) for i in range(count)]
    for h, (group, inner) in enumerate(where):
        place = pl.ds(2 * h * HD, 2 * HD)
        q2 = jnp.concatenate([r[:, place] for r in q_refs], axis=0)
        old = state.at[pl.ds(h * tall, tall), :] if with_state else None
        sums = attend_blocks(
            q2, [(k.at[place, :], v.at[place, :]) for k, v in pairs], old, scores_ref
        )
        acc_out, acc_tan, top, total, mixed_sum = sums
        if not final:
            put(refs[0], h * tall, *sums)
            continue
        inverse = 1.0 / total
        ratio = mixed_sum * inverse
        attention = acc_out * inverse
        attention_t = acc_tan * inverse - ratio * attention
        parts = (attention, attention_t, top, total, ratio)
        own, far = refs[0], refs[1 + group]
        put(own, h * tall, *(p[:, :keys] for p in parts))
        base = inner * far_tall
        far[base : base + HD, :] = attention[:, keys:].astype(BF16)
        far[base + HD : base + 2 * HD, :] = attention_t[:, keys:].astype(BF16)
        stats = three_parts(top) + three_parts(total) + three_parts(ratio)
        stats = [s[:, keys:].astype(F32) for s in stats]
        stats.append(jnp.zeros((2 * STATS - len(stats), keys), F32))
        far[base + 2 * HD : base + far_tall, :] = jnp.concatenate(stats, axis=0).astype(BF16)


def put(out, base, upper, lower, *lines):
    out[base : base + HD, :] = upper
    out[base + HD : base + 2 * HD, :] = lower
    for i, line in enumerate(lines):
        out[base + 2 * HD + i : base + 2 * HD + i + 1, :] = line


def attend_blocks(q2, pairs, state, scores_ref):
    rows = q2.shape[0]
    keys = rows // 2
    q = q2[:, HD:]
    top = state[2 * HD : 2 * HD + 1, :] if state is not None else None
    old_top = top
    for i, (k_ref, _) in enumerate(pairs):
        scores = lax.dot_general(k_ref[:, 0:HD], q, NT, preferred_element_type=F32)
        scores_ref[i * keys : (i + 1) * keys, :] = scores
        peak = jnp.max(scores, axis=0, keepdims=True) * SCALE2
        top = peak if top is None else jnp.maximum(top, peak)
    total = jnp.zeros((1, rows), F32)
    mixed_sum = jnp.zeros((1, rows), F32)
    all_weights, all_mixed = [], []
    for i, (k_ref, _) in enumerate(pairs):
        tangent = lax.dot_general(k_ref[...], q2, NT, preferred_element_type=F32)
        weights = jnp.exp2(scores_ref[i * keys : (i + 1) * keys, :] * SCALE2 - top)
        mixed = weights * tangent
        total = total + jnp.sum(weights, axis=0, keepdims=True)
        mixed_sum = mixed_sum + jnp.sum(mixed, axis=0, keepdims=True)
        all_weights.append(weights.astype(BF16))
        all_mixed.append(mixed.astype(BF16))
    values = jnp.concatenate([v_ref[...] for _, v_ref in pairs], axis=1)
    acc = jnp.dot(values, jnp.concatenate(all_weights, axis=0), preferred_element_type=F32)
    acc_mixed = jnp.dot(
        values[0:HD, :], jnp.concatenate(all_mixed, axis=0), preferred_element_type=F32
    )
    acc_out = acc[0:HD, :]
    acc_tan = acc[HD:, :] + SCALE * acc_mixed
    mixed_sum = SCALE * mixed_sum
    if state is not None:
        shrink = jnp.exp2(old_top - top)
        acc_out = acc_out + shrink * state[0:HD, :]
        acc_tan = acc_tan + shrink * state[HD : 2 * HD, :]
        total = total + shrink * state[2 * HD + 1 : 2 * HD + 2, :]
        mixed_sum = mixed_sum + shrink * state[2 * HD + 2 : 2 * HD + 3, :]
    return acc_out, acc_tan, top, total, mixed_sum


def attend(q_own, q_far, groups, blocks, state=None, final=False):
    rows = q_own.shape[0]
    heads = sum(count for _, count in groups)
    n = len(blocks)
    tall, far = 2 * HD + STATS, 2 * HD + 2 * STATS
    kinds = [isinstance(block, tuple) for block in blocks]
    arrays = [q_own, q_far]
    for block in blocks:
        arrays.extend(block if isinstance(block, tuple) else (block,))
    if state is not None:
        arrays.append(state)
    if final:
        outs = [
            jax.ShapeDtypeStruct((heads * tall, rows), F32),
            *(jax.ShapeDtypeStruct((count * far, rows), BF16) for _, count in groups),
        ]
    else:
        outs = [jax.ShapeDtypeStruct((heads * tall, 2 * rows), F32)]
    result = pl.pallas_call(
        functools.partial(attend_kernel, kinds, groups, state is not None, final),
        out_shape=outs,
        in_specs=[spec_whole()] * len(arrays),
        out_specs=[spec_whole()] * len(outs),
        scratch_shapes=[pltpu.VMEM((n * rows, 2 * rows), F32)],
        compiler_params=params(20),
        cost_estimate=pl.CostEstimate(
            flops=4 * heads * 2 * 2 * rows * n * rows * HD * 8,
            bytes_accessed=heads * 2 * rows * HD * 4 * (n + 2),
            transcendentals=heads * 2 * rows * n * rows,
        ),
        name="attend",
    )(*arrays)
    return result if final else result[0]


def merge_kernel(first, own_ref, far_ref, out):
    rows = own_ref.shape[1]
    tall, far_tall = 2 * HD + STATS, 2 * HD + 2 * STATS
    for h in range(far_ref.shape[0] // far_tall):
        own = own_ref[(first + h) * tall : (first + h + 1) * tall, :]
        far = far_ref[h * far_tall : (h + 1) * far_tall, :]
        attention, tangent = merge_parts(own, far)
        out[0:rows, h * HD : (h + 1) * HD] = attention.T.astype(BF16)
        out[rows:, h * HD : (h + 1) * HD] = tangent.T.astype(BF16)


def merge_parts(own, far):
    stats = far[2 * HD :, :].astype(F32)
    pick = lambda i: stats[3 * i : 3 * i + 1] + stats[3 * i + 1 : 3 * i + 2] + stats[3 * i + 2 : 3 * i + 3]
    top0, total0, ratio0 = (own[2 * HD + i : 2 * HD + i + 1, :] for i in range(3))
    top1, total1, ratio1 = pick(0), pick(1), pick(2)
    top = jnp.maximum(top0, top1)
    part0 = total0 * jnp.exp2(top0 - top)
    part1 = total1 * jnp.exp2(top1 - top)
    inverse = 1.0 / (part0 + part1)
    part0, part1 = part0 * inverse, part1 * inverse
    att0, att1 = own[0:HD, :], far[0:HD, :].astype(F32)
    tan0, tan1 = own[HD : 2 * HD, :], far[HD : 2 * HD, :].astype(F32)
    attention = part0 * att0 + part1 * att1
    tangent = part0 * tan0 + part1 * tan1 + (part0 * part1 * (ratio0 - ratio1)) * (att0 - att1)
    return attention, tangent


def merge(first, heads, own, far, cost):
    rows = own.shape[1]
    return pl.pallas_call(
        functools.partial(merge_kernel, first),
        out_shape=jax.ShapeDtypeStruct((2 * rows, heads * HD), BF16),
        in_specs=[spec_whole()] * 2,
        out_specs=spec_whole(),
        compiler_params=params(),
        cost_estimate=pl.CostEstimate(
            flops=cost, bytes_accessed=heads * rows * HD * 14, transcendentals=0
        ),
        name="merge",
    )(own, far)


def stage_kernel(groups, place, weight, *refs):
    count = (len(refs) - 1 - len(groups)) + 1
    pieces, outs, sems = refs[: count - 1], refs[count - 1 : -1], refs[-1]
    width = outs[0].shape[1] // 2
    copies = []
    for (first, heads), out in zip(groups, outs):
        tall = heads * HD
        for d in range(count):
            for half in range(2):
                start = lax.rem(place[1] + half, 2) * width
                if d == 0:
                    start = start + place[0] * (2 * width)
                source = pieces[d - 1] if d else weight
                copies.append(
                    pltpu.make_async_copy(
                        source.at[
                            pl.ds(first * HD, tall), pl.ds(pl.multiple_of(start, HD), width)
                        ],
                        out.at[pl.ds(d * tall, tall), pl.ds(half * width, width)],
                        sems.at[len(copies)],
                    )
                )
    for copy in copies:
        copy.start()
    for copy in copies:
        copy.wait()


def stage(groups, place, weight, pieces):
    depth, width = pieces[0].shape
    count = len(pieces) + 1
    return pl.pallas_call(
        functools.partial(stage_kernel, groups),
        out_shape=[jax.ShapeDtypeStruct((count * n * HD, width), BF16) for _, n in groups],
        in_specs=[pl.BlockSpec(memory_space=pltpu.SMEM)]
        + [pl.BlockSpec(memory_space=pltpu.HBM)] * count,
        out_specs=[spec_whole()] * len(groups),
        scratch_shapes=[pltpu.SemaphoreType.DMA((2 * count * len(groups),))],
        compiler_params=params(),
        cost_estimate=pl.CostEstimate(
            flops=0, bytes_accessed=4 * count * depth * width, transcendentals=0
        ),
        name="stage",
    )(place, weight, *pieces)


def project_kernel(halves, with_acc, *refs):
    refs = list(refs)
    out = refs.pop()
    acc = refs.pop() if with_acc else None
    weight = refs.pop()
    width = weight.shape[1] // 2
    step = width // 2
    left = jnp.concatenate([r[...] for r in refs], axis=1)
    for i, half in enumerate(halves):
        for j in range(2):
            columns = slice(half * width + j * step, half * width + (j + 1) * step)
            total = jnp.dot(left, weight[:, columns], preferred_element_type=F32)
            if with_acc:
                total = total + acc[:, columns]
            to = i * width + j * step
            out[:, to : to + step] = total.astype(out.dtype)


def project(atts, weight, halves, acc, dtype):
    rows = atts[0].shape[0]
    depth, width = weight.shape[0], len(halves) * weight.shape[1] // 2
    arrays = [*atts, weight] + ([] if acc is None else [acc])
    return pl.pallas_call(
        functools.partial(project_kernel, halves, acc is not None),
        out_shape=jax.ShapeDtypeStruct((rows, width), dtype),
        in_specs=[spec_whole()] * len(arrays),
        out_specs=spec_whole(),
        compiler_params=params(16),
        cost_estimate=pl.CostEstimate(
            flops=rows * width * depth,
            bytes_accessed=width * (rows * 6 + depth * 2),
            transcendentals=0,
        ),
        name="project",
    )(*arrays)


def finish_kernel(mine, other, res, res_t, gate, gate_t, out, out_t):
    rows = res.shape[0]
    projected = mine[0:rows, :] + other[0:rows, :].astype(F32)
    projected_t = mine[rows:, :] + other[rows:, :].astype(F32)
    g = gate[...]
    out[...] = (res[...].astype(F32) + g * projected).astype(out.dtype)
    out_t[...] = (res_t[...].astype(F32) + gate_t[...] * projected + g * projected_t).astype(
        out_t.dtype
    )


def finish(mine, other, res, res_t, gate, gate_t):
    rows, width = res.shape
    step = width // 2
    tall = pl.BlockSpec((2 * rows, step), lambda i: (0, i))
    short = pl.BlockSpec((rows, step), lambda i: (0, i))
    line = pl.BlockSpec((1, step), lambda i: (0, i))
    return pl.pallas_call(
        finish_kernel,
        grid=(width // step,),
        out_shape=[jax.ShapeDtypeStruct((rows, width), BF16)] * 2,
        in_specs=[tall, tall, short, short, line, line],
        out_specs=[short, short],
        compiler_params=params(),
        cost_estimate=pl.CostEstimate(flops=0, bytes_accessed=rows * width * 20, transcendentals=0),
        name="finish",
    )(mine, other, res, res_t, gate[None, :], gate_t[None, :])


def in_hbm(value):
    return pltpu.with_memory_space_constraint(value, pltpu.HBM)


def ring_pairs(size, shift):
    return [(i, (i + shift) % size) for i in range(size)]


def after(value, *others):
    return lax.optimization_barrier((value, others))[0]


def each(values, *others):
    return tuple(after(value, *others) for value in values)


def per_device(sizes, q, qt, k, kt, v, vt, residual, residual_t, weight, gate, gate_t):
    n_z, n_x = sizes
    heads = q.shape[1] // HD
    features = residual.shape[1]
    groups = [(0, 1), (1, heads - 1)]
    swap = [(0, 1), (1, 0)]
    up, down = ring_pairs(n_z, 1), ring_pairs(n_z, -1)
    q, qt, k, kt, v, vt = (in_hbm(item) for item in (q, qt, k, kt, v, vt))
    packed = pack(k, kt, v, vt)
    q_own = pack_queries(q, qt)
    q_far = lax.ppermute(q_own, "y_hi", swap)

    x = lax.axis_index("x")
    here = jnp.stack([x, lax.axis_index("core")]).astype(jnp.int32)

    def piece(d, *others):
        corner = lax.rem(x + d, n_x) * (2 * features)
        part = lax.dynamic_slice_in_dim(weight, corner, 2 * features, 1)
        return lax.ppermute(after(part, *others), "x", ring_pairs(n_x, d))

    near = [piece(1), piece(n_x - 1)]
    pieces = [near[0]] + [piece(d, *near) for d in range(2, n_x - 1)] + [near[1]]

    def hop(pair):
        return lax.ppermute(pair[0], "z", up), lax.ppermute(pair[1], "z", down)

    def turn(pair):
        return hop((pair[0][0], pair[1][1]))

    run = functools.partial(attend, q_own, q_far, groups)
    step1 = hop((packed, packed))
    step2 = hop(each(step1, q_far))
    state = run([packed, *step1])
    step3 = hop(each(step2, state, *near))
    state = run([*step2], state=state)
    step4 = turn(each(step3, state))
    state = run([*step3], state=state)
    own, *far = run([step4], state=state, final=True)
    staged = stage(groups, here, in_hbm(weight), [in_hbm(item) for item in after(pieces, own)])

    gathered, arrived = [], own
    for group, item in zip(groups, far):
        waits = (arrived, staged) if group[0] else ()
        arrived = lax.ppermute(after(item, *waits), "y_hi", swap)
        att = merge(*group, own, arrived, 10**10 if group[0] else 0)
        gathered.append(
            [att] + [lax.ppermute(att, "x", ring_pairs(n_x, d)) for d in range(1, n_x)]
        )
    acc = project(gathered[0], staged[0], (0, 1), None, F32)
    run = functools.partial(project, gathered[1], staged[1])
    to_core = run((1,), acc, BF16)
    from_core = lax.ppermute(to_core, "core", swap)
    mine = run((0,), acc, F32)
    return tuple(finish(mine, from_core, residual, residual_t, gate, gate_t))


def solution(mesh):
    n_z, n_x = mesh.shape["seq"] // 2, mesh.shape["head"] // 2
    fine = Mesh(
        mesh.devices.reshape(n_z, 2, n_x, 2, mesh.shape["dp"]), ("z", "y_hi", "x", "core", "dp")
    )
    tokens, width = ("dp", "z", "y_hi"), ("x", "core")
    wide = P(tokens, width)
    gates = P(("dp", "x", "core"))
    return jax.shard_map(
        functools.partial(per_device, (n_z, n_x)),
        mesh=fine,
        in_specs=(wide,) * 8 + (P(width, None), gates, gates),
        out_specs=(wide, wide),
        check_vma=False,
    )
```

time: 163 us -> 117 us (0.72)
  starting transfers between devices: 60.2 us -> 41.5 us
  between operations: 14.5 us -> 0.83 us
  Pallas kernels: 30 us -> 20.5 us
  local copies, waits for them, and re-layouts: 9.2 us -> 4.31 us
  waiting for transfers between devices: 47.3 us -> 49.4 us
    ppermute x21 -> x13, starting transfers between devices: 37.9 us -> 25.4 us  [the longest x8 15.8 us: hop(): return (lax.ppermute(pair[0], 'z', up), lax.ppermute(pair[1], 'z', down))]
    pallas_call x14 -> x12, Pallas kernels: 28.3 us -> 19.2 us  [the longest x4 9.71 us: attend(): pl.pallas_call(functools.partial(attend_kernel, kinds, groups, state is n...]
    ppermute x1, starting transfers between devices: 12.5 us -> 6.2 us  [per_device(): from_core = lax.ppermute(to_core, 'core', swap)]
    unnamed x44 -> x14, local copies, waits for them, and re-layouts: 5.85 us -> 1.03 us
    ppermute x21 -> x13, waiting for transfers between devices: 40 us -> 37 us  [the longest x8 20.2 us: hop(): return (lax.ppermute(pair[0], 'z', up), lax.ppermute(pair[1], 'z', down))]
    ppermute x1, waiting for transfers between devices: 0.01 us -> 2.36 us  [per_device(): q_far = lax.ppermute(q_own, 'y_hi', swap)]
    ppermute x6, waiting for transfers between devices: 7.31 us -> 9.35 us  [per_device(): lax.ppermute(att, 'x', ring_pairs(n_x, d))]
  transfers between devices with their start and end apart: 30 -> 21, of which waited for: 13 -> 12; matrix products, arithmetic and copies ran while one was open for 1% -> 3% of each run, Pallas kernels for 16% -> 14%
where the time goes in v1:
time: 117 us
  waiting for transfers between devices  49.4 us (42%)
  starting transfers between devices  41.5 us (35%)
  Pallas kernels  20.5 us (18%)
  local copies, waits for them, and re-layouts  4.31 us (4%)
    ppermute x8, waiting for transfers between devices, hop(): return (lax.ppermute(pair[0], 'z', up), lax.ppermute(pair[1], 'z', down))  20.2 us
    ppermute x8, starting transfers between devices, hop(): return (lax.ppermute(pair[0], 'z', up), lax.ppermute(pair[1], 'z', down))  15.8 us
    ppermute x3, waiting for transfers between devices, piece(): return lax.ppermute(after(part, *others), 'x', ring_pairs(n_x, d))  11.6 us
    pallas_call x4, Pallas kernels, attend(): pl.pallas_call(functools.partial(attend_kernel, kinds, groups, state is n...  9.71 us
    ppermute x6, waiting for transfers between devices, per_device(): lax.ppermute(att, 'x', ring_pairs(n_x, d))  9.35 us
    ppermute x6, starting transfers between devices, per_device(): lax.ppermute(att, 'x', ring_pairs(n_x, d))  6.9 us
    ppermute x1, starting transfers between devices, per_device(): from_core = lax.ppermute(to_core, 'core', swap)  6.2 us
    ppermute x3, starting transfers between devices, piece(): return lax.ppermute(after(part, *others), 'x', ring_pairs(n_x, d))  5.42 us
  transfers between devices with their start and end apart: 21, of which 12 were waited for; matrix products, arithmetic and copies ran while one was open for 3% of the time, Pallas kernels for 14%

profile of v1, /device:TPU:1, one launch (start us, length us, event | category | flops | bytes accessed | tf_op | source)
XLA Modules:
  0.0 116.6 jit_solution(185061614076318638)
XLA Ops:
  1.9 2.5 %collective-permute-start.1 = (bf16[2,768,256]{2,1,0:T(8,128)(2,1)S(1)}, bf16[2,768,256]{2,1,0:T(8,128)(2,1)S(1)}, u32[]{:S(2)}, u32[]{:S(2)}) collective-permute-start(bf16[2,768,256]{2,1,0:T(8,128)(2,1)S(1)} %pack.1.refs_2_), channel_id=1, source_target_pairs={{0,32},{32,64},{64,96},{96,128},{128,160},{160,192},{192,224},{224... | collective-permute-start | bytes 2359304 | tf_op jit(solution)/shard_map/ppermute | solution.py:429
  4.4 4.0 %collective-permute-start.3 = (bf16[2,768,256]{2,1,0:T(8,128)(2,1)S(1)}, bf16[2,768,256]{2,1,0:T(8,128)(2,1)S(1)}, u32[]{:S(2)}, u32[]{:S(2)}) collective-permute-start(bf16[2,768,256]{2,1,0:T(8,128)(2,1)S(1)} %pack.1.refs_2_), channel_id=1, source_target_pairs={{0,224},{32,0},{64,32},{96,64},{128,96},{160,128},{192,160},{224,1... | collective-permute-start | bytes 2359304 | tf_op jit(solution)/shard_map/ppermute | solution.py:429
  9.5 3.0 %collective-permute-start = (bf16[256,768]{1,0:T(8,128)(2,1)S(1)}, bf16[256,768]{1,0:T(8,128)(2,1)S(1)}, u32[]{:S(2)}, u32[]{:S(2)}) collective-permute-start(bf16[256,768]{1,0:T(8,128)(2,1)S(1)} %pack_queries.1.refs_0_), channel_id=1, source_target_pairs={{0,16},{16,0},{1,17},{17,1},{2,18},{18,2},{3,19},{19,3},{4,20},{20... | collective-permute-start | bytes 1179656 | tf_op jit(solution)/shard_map/ppermute | solution.py:415
  12.5 3.2 %constant_dynamic-slice_fusion = (bf16[384,1536]{1,0:T(8,128)(2,1)}, bf16[384,1536]{1,0:T(8,128)(2,1)S(1)}, bf16[384,1536]{1,0:T(8,128)(2,1)S(1)}) fusion(bf16[384,6144]{1,0:T(8,128)(2,1)} %weight.1, s32[]{:T(128)S(6)} %select_n.11, s32[]{:T(128)S(6)} %select_n.10, s32[]{:T(128)S(6)} %select_n.9), kind=kLoop, calls=%fused_computation.2 | loop fusion | bytes 7077900 | tf_op jit(solution)/shard_map/dynamic_slice | solution.py:422
  16.9 1.5 %collective-permute-start.5 = (bf16[384,1536]{1,0:T(8,128)(2,1)S(1)}, bf16[384,1536]{1,0:T(8,128)(2,1)S(1)}, u32[]{:S(2)}, u32[]{:S(2)}) collective-permute-start(bf16[384,1536]{1,0:T(8,128)(2,1)S(1)} %get-tuple-element.35), channel_id=1, source_target_pairs={{0,12},{4,0},{8,4},{12,8},{1,13},{5,1},{9,5},{13,9},{2,14},{6,2},{... | collective-permute-start | bytes 3538952 | tf_op jit(solution)/shard_map/ppermute | solution.py:423
  18.4 2.4 %collective-permute-done.refs_1_ = bf16[256,768]{1,0:T(8,128)(2,1)S(1)} collective-permute-done((bf16[256,768]{1,0:T(8,128)(2,1)S(1)}, bf16[256,768]{1,0:T(8,128)(2,1)S(1)}, u32[]{:S(2)}, u32[]{:S(2)}) %collective-permute-start) | collective-permute-done | bytes 393248 | tf_op jit(solution)/shard_map/ppermute | solution.py:415
  20.7 4.9 %collective-permute-done.1.refs_3_ = bf16[2,768,256]{2,1,0:T(8,128)(2,1)S(1)} collective-permute-done((bf16[2,768,256]{2,1,0:T(8,128)(2,1)S(1)}, bf16[2,768,256]{2,1,0:T(8,128)(2,1)S(1)}, u32[]{:S(2)}, u32[]{:S(2)}) %collective-permute-start.1) | collective-permute-done | bytes 786464 | tf_op jit(solution)/shard_map/ppermute | solution.py:429
  25.6 2.7 %collective-permute-start.7 = (bf16[2,768,256]{2,1,0:T(8,128)(2,1)S(1)}, bf16[2,768,256]{2,1,0:T(8,128)(2,1)S(1)}, u32[]{:S(2)}, u32[]{:S(2)}) collective-permute-start(bf16[2,768,256]{2,1,0:T(8,128)(2,1)S(1)} %collective-permute-done.3.refs_4_), channel_id=1, source_target_pairs={{0,224},{32,0},{64,32},{96,64},{128,96},{160,128},{192,160},{224,1... | collective-permute-start | bytes 2359304 | tf_op jit(solution)/shard_map/ppermute | solution.py:429
  28.3 3.2 %attend.4.refs_4_ = f32[792,512]{1,0:T(8,128)S(1)} custom-call(bf16[256,768]{1,0:T(8,128)(2,1)S(1)} %pack_queries.1.refs_0_, bf16[256,768]{1,0:T(8,128)(2,1)S(1)} %collective-permute-done.refs_1_, bf16[2,768,256]{2,1,0:T(8,128)(2,1)S(1)} %pack.1.refs_2_, bf16[2,768,256]{2,1,0:T(8,128)(2,1)S(1)} %collective-permute-done.1.refs_3_, ...), custom_call_target="tpu_custom_call" | custom-call | flops 9663676416 | bytes 3932160 | tf_op jit(solution)/shard_map/attend/pallas_call | solution.py:217
  31.5 11.6 %collective-permute-done.4.refs_0_ = bf16[384,1536]{1,0:T(8,128)(2,1)S(1)} collective-permute-done((bf16[384,1536]{1,0:T(8,128)(2,1)S(1)}, bf16[384,1536]{1,0:T(8,128)(2,1)S(1)}, u32[]{:S(2)}, u32[]{:S(2)}) %collective-permute-start.4) | collective-permute-done | bytes 1179680 | tf_op jit(solution)/shard_map/ppermute | solution.py:423
  43.1 1.5 %collective-permute-done.2.refs_2_ = bf16[2,768,256]{2,1,0:T(8,128)(2,1)S(1)} collective-permute-done((bf16[2,768,256]{2,1,0:T(8,128)(2,1)S(1)}, bf16[2,768,256]{2,1,0:T(8,128)(2,1)S(1)}, u32[]{:S(2)}, u32[]{:S(2)}) %collective-permute-start.2) | collective-permute-done | bytes 786464 | tf_op jit(solution)/shard_map/ppermute | solution.py:429
  44.6 2.7 %collective-permute-start.12 = (bf16[384,1536]{1,0:T(8,128)(2,1)}, bf16[384,1536]{1,0:T(8,128)(2,1)S(1)}, u32[]{:S(2)}, u32[]{:S(2)}) collective-permute-start(bf16[384,1536]{1,0:T(8,128)(2,1)} %get-tuple-element.27), channel_id=1, source_target_pairs={{0,8},{4,12},{8,0},{12,4},{1,9},{5,13},{9,1},{13,5},{2,10},{6,14},... | collective-permute-start | bytes 3538952 | tf_op jit(solution)/shard_map/ppermute | solution.py:423
  47.4 2.9 %collective-permute-start.9 = (bf16[2,768,256]{2,1,0:T(8,128)(2,1)S(1)}, bf16[2,768,256]{2,1,0:T(8,128)(2,1)S(1)}, u32[]{:S(2)}, u32[]{:S(2)}) collective-permute-start(bf16[2,768,256]{2,1,0:T(8,128)(2,1)S(1)} %collective-permute-done.7.refs_3_), channel_id=1, source_target_pairs={{0,224},{32,0},{64,32},{96,64},{128,96},{160,128},{192,160},{224,1... | collective-permute-start | bytes 2359304 | tf_op jit(solution)/shard_map/ppermute | solution.py:429
  50.3 2.4 %attend.5.refs_4_ = f32[792,512]{1,0:T(8,128)S(1)} custom-call(bf16[256,768]{1,0:T(8,128)(2,1)S(1)} %pack_queries.1.refs_0_, bf16[256,768]{1,0:T(8,128)(2,1)S(1)} %collective-permute-done.refs_1_, bf16[2,768,256]{2,1,0:T(8,128)(2,1)S(1)} %collective-permute-done.2.refs_2_, bf16[2,768,256]{2,1,0:T(8,128)(2,1)S(1)} %collective-permute-done.7.refs_3_, ...), custom_call_target="tpu_custom_call" | custom-call | flops 6442450944 | bytes 3145728 | tf_op jit(solution)/shard_map/attend/pallas_call | solution.py:217
  52.8 9.9 %collective-permute-done.6.refs_2_ = bf16[2,768,256]{2,1,0:T(8,128)(2,1)S(1)} collective-permute-done((bf16[2,768,256]{2,1,0:T(8,128)(2,1)S(1)}, bf16[2,768,256]{2,1,0:T(8,128)(2,1)S(1)}, u32[]{:S(2)}, u32[]{:S(2)}) %collective-permute-start.6) | collective-permute-done | bytes 786464 | tf_op jit(solution)/shard_map/ppermute | solution.py:429
  62.8 1.6 %collective-permute-done.9.refs_3_ = bf16[2,768,256]{2,1,0:T(8,128)(2,1)S(1)} collective-permute-done((bf16[2,768,256]{2,1,0:T(8,128)(2,1)S(1)}, bf16[2,768,256]{2,1,0:T(8,128)(2,1)S(1)}, u32[]{:S(2)}, u32[]{:S(2)}) %collective-permute-start.9) | collective-permute-done | bytes 786464 | tf_op jit(solution)/shard_map/ppermute | solution.py:429
  64.5 3.5 %collective-permute-start.10 = (bf16[768,256]{1,0:T(8,128)(2,1)S(1)}, bf16[768,256]{1,0:T(8,128)(2,1)S(1)}, u32[]{:S(2)}, u32[]{:S(2)}) collective-permute-start(bf16[768,256]{1,0:T(8,128)(2,1)S(1)} %slice_bitcast_fusion), channel_id=1, source_target_pairs={{0,224},{32,0},{64,32},{96,64},{128,96},{160,128},{192,160},{224,1... | collective-permute-start | bytes 1179656 | tf_op jit(solution)/shard_map/ppermute | solution.py:429
  68.0 2.4 %attend.6.refs_4_ = f32[792,512]{1,0:T(8,128)S(1)} custom-call(bf16[256,768]{1,0:T(8,128)(2,1)S(1)} %pack_queries.1.refs_0_, bf16[256,768]{1,0:T(8,128)(2,1)S(1)} %collective-permute-done.refs_1_, bf16[2,768,256]{2,1,0:T(8,128)(2,1)S(1)} %collective-permute-done.6.refs_2_, bf16[2,768,256]{2,1,0:T(8,128)(2,1)S(1)} %collective-permute-done.9.refs_3_, ...), custom_call_target="tpu_custom_call" | custom-call | flops 6442450944 | bytes 3145728 | tf_op jit(solution)/shard_map/attend/pallas_call | solution.py:217
  72.7 1.6 %attend.7 = (f32[792,256]{1,0:T(8,128)S(1)}, bf16[272,256]{1,0:T(8,128)(2,1)S(1)}, bf16[544,256]{1,0:T(8,128)(2,1)S(1)}) custom-call(bf16[256,768]{1,0:T(8,128)(2,1)S(1)} %pack_queries.1.refs_0_, bf16[256,768]{1,0:T(8,128)(2,1)S(1)} %collective-permute-done.refs_1_, bf16[768,256]{1,0:T(8,128)(2,1)S(1)} %collective-permute-done.8.refs_2_, ...), custom_call_target="tpu_custom_call" | custom-call | flops 3221225472 | bytes 2359296 | tf_op jit(solution)/shard_map/attend/pallas_call | solution.py:217
  74.3 3.0 %collective-permute-start.11 = (bf16[272,256]{1,0:T(8,128)(2,1)S(1)}, bf16[272,256]{1,0:T(8,128)(2,1)S(1)}, u32[]{:S(2)}, u32[]{:S(2)}) collective-permute-start(bf16[272,256]{1,0:T(8,128)(2,1)S(1)} %get-tuple-element.26), channel_id=1, source_target_pairs={{0,16},{16,0},{1,17},{17,1},{2,18},{18,2},{3,19},{19,3},{4,20},{20... | collective-permute-start | bytes 417800 | tf_op jit(solution)/shard_map/ppermute | solution.py:448
  78.4 3.1 %stage.1 = (bf16[512,1536]{1,0:T(8,128)(2,1)S(1)}, bf16[1024,1536]{1,0:T(8,128)(2,1)S(1)}) custom-call(s32[2]{0:T(128)S(1)} %pad_add_fusion.place, bf16[384,6144]{1,0:T(8,128)(2,1)} %weight.1, bf16[384,1536]{1,0:T(8,128)(2,1)} %copy-done.2, bf16[384,1536]{1,0:T(8,128)(2,1)} %copy-done.4, bf16[384,1536]{1,0:T(8,128)(2,1)} %copy-done.3), custom_call_target="tpu_custom_call" | custom-call | bytes 9437184 | tf_op jit(solution)/shard_map/stage/pallas_call | solution.py:308
  83.2 5.2 %collective-permute-done.13.far_ref = bf16[544,256]{1,0:T(8,128)(2,1)S(1)} collective-permute-done((bf16[544,256]{1,0:T(8,128)(2,1)S(1)}, bf16[544,256]{1,0:T(8,128)(2,1)S(1)}, u32[]{:S(2)}, u32[]{:S(2)}) %collective-permute-start.13) | collective-permute-done | bytes 278560 | tf_op jit(solution)/shard_map/ppermute | solution.py:448
  89.1 2.3 %collective-permute-start.15 = (bf16[512,256]{1,0:T(8,128)(2,1)S(1)}, bf16[512,256]{1,0:T(8,128)(2,1)S(1)}, u32[]{:S(2)}, u32[]{:S(2)}) collective-permute-start(bf16[512,256]{1,0:T(8,128)(2,1)S(1)} %merge.2.refs_0_), channel_id=1, source_target_pairs={{0,8},{4,12},{8,0},{12,4},{1,9},{5,13},{9,1},{13,5},{2,10},{6,14},... | collective-permute-start | bytes 786440 | tf_op jit(solution)/shard_map/ppermute | solution.py:451
  92.5 1.3 %collective-permute-start.18 = (bf16[512,128]{1,0:T(8,128)(2,1)S(1)}, bf16[512,128]{1,0:T(8,128)(2,1)S(1)}, u32[]{:S(2)}, u32[]{:S(2)}) collective-permute-start(bf16[512,128]{1,0:T(8,128)(2,1)S(1)} %merge.3.refs_0_), channel_id=1, source_target_pairs={{0,8},{4,12},{8,0},{12,4},{1,9},{5,13},{9,1},{13,5},{2,10},{6,14},... | collective-permute-start | bytes 393224 | tf_op jit(solution)/shard_map/ppermute | solution.py:451
  93.8 1.4 %collective-permute-start.19 = (bf16[512,128]{1,0:T(8,128)(2,1)S(1)}, bf16[512,128]{1,0:T(8,128)(2,1)S(1)}, u32[]{:S(2)}, u32[]{:S(2)}) collective-permute-start(bf16[512,128]{1,0:T(8,128)(2,1)S(1)} %merge.3.refs_0_), channel_id=1, source_target_pairs={{0,12},{4,0},{8,4},{12,8},{1,13},{5,1},{9,5},{13,9},{2,14},{6,2},{... | collective-permute-start | bytes 393224 | tf_op jit(solution)/shard_map/ppermute | solution.py:451
  95.2 8.0 %collective-permute-done.18.refs_2_ = bf16[512,128]{1,0:T(8,128)(2,1)S(1)} collective-permute-done((bf16[512,128]{1,0:T(8,128)(2,1)S(1)}, bf16[512,128]{1,0:T(8,128)(2,1)S(1)}, u32[]{:S(2)}, u32[]{:S(2)}) %collective-permute-start.18) | collective-permute-done | bytes 131104 | tf_op jit(solution)/shard_map/ppermute | solution.py:451
  103.2 1.3 %collective-permute-done.19.refs_3_ = bf16[512,128]{1,0:T(8,128)(2,1)S(1)} collective-permute-done((bf16[512,128]{1,0:T(8,128)(2,1)S(1)}, bf16[512,128]{1,0:T(8,128)(2,1)S(1)}, u32[]{:S(2)}, u32[]{:S(2)}) %collective-permute-start.19) | collective-permute-done | bytes 131104 | tf_op jit(solution)/shard_map/ppermute | solution.py:451
  104.6 1.3 %project.3.refs_5_ = f32[512,1536]{1,0:T(8,128)S(1)} custom-call(bf16[512,128]{1,0:T(8,128)(2,1)S(1)} %merge.3.refs_0_, bf16[512,128]{1,0:T(8,128)(2,1)S(1)} %collective-permute-done.17.refs_1_, bf16[512,128]{1,0:T(8,128)(2,1)S(1)} %collective-permute-done.18.refs_2_, bf16[512,128]{1,0:T(8,128)(2,1)S(1)} %collective-permute-done.19.refs_3_, ...), custom_call_target="tpu_custom_call" | custom-call | flops 402653184 | bytes 6291456 | tf_op jit(solution)/shard_map/project/pallas_call | solution.py:345
  105.9 1.3 %project.5 = bf16[512,768]{1,0:T(8,128)(2,1)S(1)} custom-call(bf16[512,256]{1,0:T(8,128)(2,1)S(1)} %merge.2.refs_0_, bf16[512,256]{1,0:T(8,128)(2,1)S(1)} %collective-permute-done.14.refs_1_, bf16[512,256]{1,0:T(8,128)(2,1)S(1)} %collective-permute-done.15.refs_2_, bf16[512,256]{1,0:T(8,128)(2,1)S(1)} %collective-permute-done.16.refs_3_, ...), custom_call_target="tpu_custom_call" | custom-call | flops 402653184 | bytes 3932160 | tf_op jit(solution)/shard_map/project/pallas_call | solution.py:345
  107.1 6.2 %collective-permute-start.20 = (bf16[512,768]{1,0:T(8,128)(2,1)S(1)}, bf16[512,768]{1,0:T(8,128)(2,1)S(1)}, u32[]{:S(2)}, u32[]{:S(2)}) collective-permute-start(bf16[512,768]{1,0:T(8,128)(2,1)S(1)} %project.5), channel_id=1, source_target_pairs={{0,2},{2,0},{1,3},{3,1},{4,6},{6,4},{5,7},{7,5},{8,10},{10,8},{9,1... | collective-permute-start | bytes 2359304 | tf_op jit(solution)/shard_map/ppermute | solution.py:456
  113.4 1.3 %project.4.mine = f32[512,768]{1,0:T(8,128)S(1)} custom-call(bf16[512,256]{1,0:T(8,128)(2,1)S(1)} %merge.2.refs_0_, bf16[512,256]{1,0:T(8,128)(2,1)S(1)} %collective-permute-done.14.refs_1_, bf16[512,256]{1,0:T(8,128)(2,1)S(1)} %collective-permute-done.15.refs_2_, bf16[512,256]{1,0:T(8,128)(2,1)S(1)} %collective-permute-done.16.refs_3_, ...), custom_call_target="tpu_custom_call" | custom-call | flops 402653184 | bytes 3932160 | tf_op jit(solution)/shard_map/project/pallas_call | solution.py:345
  115.2 1.3 %finish.1 = (bf16[256,768]{1,0:T(8,128)(2,1)}, bf16[256,768]{1,0:T(8,128)(2,1)}) custom-call(f32[512,768]{1,0:T(8,128)S(1)} %project.4.mine, bf16[512,768]{1,0:T(8,128)(2,1)S(1)} %collective-permute-done.20.other, bf16[256,768]{1,0:T(8,128)(2,1)S(1)} %copy-done, bf16[256,768]{1,0:T(8,128)(2,1)S(1)} %copy-done.1, f32[1,768]{1,0:T(1,128)S(1)} %broadcast_in_dim.6.gate, ...), custom_call_target="tpu_custom_call" | custom-call | bytes 3932160 | tf_op jit(solution)/shard_map/finish/pallas_call | solution.py:377
  (43 shorter events, 11.2 us)
Async XLA Ops:
  1.9 23.8 %collective-permute-start.1 = (bf16[2,768,256]{2,1,0:T(8,128)(2,1)S(1)}, bf16[2,768,256]{2,1,0:T(8,128)(2,1)S(1)}, u32[]{:S(2)}, u32[]{:S(2)}) collective-permute-start(bf16[2,768,256]{2,1,0:T(8,128)(2,1)S(1)} %pack.1.refs_2_), channel_id=1, source_target_pairs={{0,32},{32,64},{64,96},{96,128},{128,160},{160,192},{192,224},{224... | collective-permute-start | bytes 2359304 | tf_op jit(solution)/shard_map/ppermute | solution.py:429
  4.4 21.2 %collective-permute-start.3 = (bf16[2,768,256]{2,1,0:T(8,128)(2,1)S(1)}, bf16[2,768,256]{2,1,0:T(8,128)(2,1)S(1)}, u32[]{:S(2)}, u32[]{:S(2)}) collective-permute-start(bf16[2,768,256]{2,1,0:T(8,128)(2,1)S(1)} %pack.1.refs_2_), channel_id=1, source_target_pairs={{0,224},{32,0},{64,32},{96,64},{128,96},{160,128},{192,160},{224,1... | collective-permute-start | bytes 2359304 | tf_op jit(solution)/shard_map/ppermute | solution.py:429
  9.5 11.3 %collective-permute-start = (bf16[256,768]{1,0:T(8,128)(2,1)S(1)}, bf16[256,768]{1,0:T(8,128)(2,1)S(1)}, u32[]{:S(2)}, u32[]{:S(2)}) collective-permute-start(bf16[256,768]{1,0:T(8,128)(2,1)S(1)} %pack_queries.1.refs_0_), channel_id=1, source_target_pairs={{0,16},{16,0},{1,17},{17,1},{2,18},{18,2},{3,19},{19,3},{4,20},{20... | collective-permute-start | bytes 1179656 | tf_op jit(solution)/shard_map/ppermute | solution.py:415
  15.7 27.4 %collective-permute-start.4 = (bf16[384,1536]{1,0:T(8,128)(2,1)S(1)}, bf16[384,1536]{1,0:T(8,128)(2,1)S(1)}, u32[]{:S(2)}, u32[]{:S(2)}) collective-permute-start(bf16[384,1536]{1,0:T(8,128)(2,1)S(1)} %get-tuple-element.36), channel_id=1, source_target_pairs={{0,4},{4,8},{8,12},{12,0},{1,5},{5,9},{9,13},{13,1},{2,6},{6,10},{... | collective-permute-start | bytes 3538952 | tf_op jit(solution)/shard_map/ppermute | solution.py:423
  16.9 26.2 %collective-permute-start.5 = (bf16[384,1536]{1,0:T(8,128)(2,1)S(1)}, bf16[384,1536]{1,0:T(8,128)(2,1)S(1)}, u32[]{:S(2)}, u32[]{:S(2)}) collective-permute-start(bf16[384,1536]{1,0:T(8,128)(2,1)S(1)} %get-tuple-element.35), channel_id=1, source_target_pairs={{0,12},{4,0},{8,4},{12,8},{1,13},{5,1},{9,5},{13,9},{2,14},{6,2},{... | collective-permute-start | bytes 3538952 | tf_op jit(solution)/shard_map/ppermute | solution.py:423
  25.6 19.0 %collective-permute-start.2 = (bf16[2,768,256]{2,1,0:T(8,128)(2,1)S(1)}, bf16[2,768,256]{2,1,0:T(8,128)(2,1)S(1)}, u32[]{:S(2)}, u32[]{:S(2)}) collective-permute-start(bf16[2,768,256]{2,1,0:T(8,128)(2,1)S(1)} %collective-permute-done.1.refs_3_), channel_id=1, source_target_pairs={{0,32},{32,64},{64,96},{96,128},{128,160},{160,192},{192,224},{224... | collective-permute-start | bytes 2359304 | tf_op jit(solution)/shard_map/ppermute | solution.py:429
  25.6 21.8 %collective-permute-start.7 = (bf16[2,768,256]{2,1,0:T(8,128)(2,1)S(1)}, bf16[2,768,256]{2,1,0:T(8,128)(2,1)S(1)}, u32[]{:S(2)}, u32[]{:S(2)}) collective-permute-start(bf16[2,768,256]{2,1,0:T(8,128)(2,1)S(1)} %collective-permute-done.3.refs_4_), channel_id=1, source_target_pairs={{0,224},{32,0},{64,32},{96,64},{128,96},{160,128},{192,160},{224,1... | collective-permute-start | bytes 2359304 | tf_op jit(solution)/shard_map/ppermute | solution.py:429
  43.1 4.2 %copy-start.2 = (bf16[384,1536]{1,0:T(8,128)(2,1)}, bf16[384,1536]{1,0:T(8,128)(2,1)S(1)}, u32[]{:S(2)}) copy-start(bf16[384,1536]{1,0:T(8,128)(2,1)S(1)} %collective-permute-done.4.refs_0_) | copy-start | bytes 3538948
  43.1 4.2 %copy-start.3 = (bf16[384,1536]{1,0:T(8,128)(2,1)}, bf16[384,1536]{1,0:T(8,128)(2,1)S(1)}, u32[]{:S(2)}) copy-start(bf16[384,1536]{1,0:T(8,128)(2,1)S(1)} %collective-permute-done.5.refs_2_) | copy-start | bytes 3538948
  44.6 18.1 %collective-permute-start.6 = (bf16[2,768,256]{2,1,0:T(8,128)(2,1)S(1)}, bf16[2,768,256]{2,1,0:T(8,128)(2,1)S(1)}, u32[]{:S(2)}, u32[]{:S(2)}) collective-permute-start(bf16[2,768,256]{2,1,0:T(8,128)(2,1)S(1)} %collective-permute-done.2.refs_2_), channel_id=1, source_target_pairs={{0,32},{32,64},{64,96},{96,128},{128,160},{160,192},{192,224},{224... | collective-permute-start | bytes 2359304 | tf_op jit(solution)/shard_map/ppermute | solution.py:429
  44.6 32.7 %collective-permute-start.12 = (bf16[384,1536]{1,0:T(8,128)(2,1)}, bf16[384,1536]{1,0:T(8,128)(2,1)S(1)}, u32[]{:S(2)}, u32[]{:S(2)}) collective-permute-start(bf16[384,1536]{1,0:T(8,128)(2,1)} %get-tuple-element.27), channel_id=1, source_target_pairs={{0,8},{4,12},{8,0},{12,4},{1,9},{5,13},{9,1},{13,5},{2,10},{6,14},... | collective-permute-start | bytes 3538952 | tf_op jit(solution)/shard_map/ppermute | solution.py:423
  47.4 17.1 %collective-permute-start.9 = (bf16[2,768,256]{2,1,0:T(8,128)(2,1)S(1)}, bf16[2,768,256]{2,1,0:T(8,128)(2,1)S(1)}, u32[]{:S(2)}, u32[]{:S(2)}) collective-permute-start(bf16[2,768,256]{2,1,0:T(8,128)(2,1)S(1)} %collective-permute-done.7.refs_3_), channel_id=1, source_target_pairs={{0,224},{32,0},{64,32},{96,64},{128,96},{160,128},{192,160},{224,1... | collective-permute-start | bytes 2359304 | tf_op jit(solution)/shard_map/ppermute | solution.py:429
  62.8 8.8 %collective-permute-start.8 = (bf16[768,256]{1,0:T(8,128)(2,1)S(1)}, bf16[768,256]{1,0:T(8,128)(2,1)S(1)}, u32[]{:S(2)}, u32[]{:S(2)}) collective-permute-start(bf16[768,256]{1,0:T(8,128)(2,1)S(1)} %slice_bitcast_fusion.1), channel_id=1, source_target_pairs={{0,32},{32,64},{64,96},{96,128},{128,160},{160,192},{192,224},{224... | collective-permute-start | bytes 1179656 | tf_op jit(solution)/shard_map/ppermute | solution.py:429
  64.5 8.2 %collective-permute-start.10 = (bf16[768,256]{1,0:T(8,128)(2,1)S(1)}, bf16[768,256]{1,0:T(8,128)(2,1)S(1)}, u32[]{:S(2)}, u32[]{:S(2)}) collective-permute-start(bf16[768,256]{1,0:T(8,128)(2,1)S(1)} %slice_bitcast_fusion), channel_id=1, source_target_pairs={{0,224},{32,0},{64,32},{96,64},{128,96},{160,128},{192,160},{224,1... | collective-permute-start | bytes 1179656 | tf_op jit(solution)/shard_map/ppermute | solution.py:429
  74.3 7.2 %collective-permute-start.11 = (bf16[272,256]{1,0:T(8,128)(2,1)S(1)}, bf16[272,256]{1,0:T(8,128)(2,1)S(1)}, u32[]{:S(2)}, u32[]{:S(2)}) collective-permute-start(bf16[272,256]{1,0:T(8,128)(2,1)S(1)} %get-tuple-element.26), channel_id=1, source_target_pairs={{0,16},{16,0},{1,17},{17,1},{2,18},{18,2},{3,19},{19,3},{4,20},{20... | collective-permute-start | bytes 417800 | tf_op jit(solution)/shard_map/ppermute | solution.py:448
  77.4 1.0 copy-start.4
  81.5 7.0 %collective-permute-start.13 = (bf16[544,256]{1,0:T(8,128)(2,1)S(1)}, bf16[544,256]{1,0:T(8,128)(2,1)S(1)}, u32[]{:S(2)}, u32[]{:S(2)}) collective-permute-start(bf16[544,256]{1,0:T(8,128)(2,1)S(1)} %get-tuple-element.33), channel_id=1, source_target_pairs={{0,16},{16,0},{1,17},{17,1},{2,18},{18,2},{3,19},{19,3},{4,20},{20... | collective-permute-start | bytes 835592 | tf_op jit(solution)/shard_map/ppermute | solution.py:448
  82.8 11.0 %collective-permute-start.17 = (bf16[512,128]{1,0:T(8,128)(2,1)S(1)}, bf16[512,128]{1,0:T(8,128)(2,1)S(1)}, u32[]{:S(2)}, u32[]{:S(2)}) collective-permute-start(bf16[512,128]{1,0:T(8,128)(2,1)S(1)} %merge.3.refs_0_), channel_id=1, source_target_pairs={{0,4},{4,8},{8,12},{12,0},{1,5},{5,9},{9,13},{13,1},{2,6},{6,10},{... | collective-permute-start | bytes 393224 | tf_op jit(solution)/shard_map/ppermute | solution.py:451
  88.7 17.1 %collective-permute-start.14 = (bf16[512,256]{1,0:T(8,128)(2,1)S(1)}, bf16[512,256]{1,0:T(8,128)(2,1)S(1)}, u32[]{:S(2)}, u32[]{:S(2)}) collective-permute-start(bf16[512,256]{1,0:T(8,128)(2,1)S(1)} %merge.2.refs_0_), channel_id=1, source_target_pairs={{0,4},{4,8},{8,12},{12,0},{1,5},{5,9},{9,13},{13,1},{2,6},{6,10},{... | collective-permute-start | bytes 786440 | tf_op jit(solution)/shard_map/ppermute | solution.py:451
  89.1 16.7 %collective-permute-start.15 = (bf16[512,256]{1,0:T(8,128)(2,1)S(1)}, bf16[512,256]{1,0:T(8,128)(2,1)S(1)}, u32[]{:S(2)}, u32[]{:S(2)}) collective-permute-start(bf16[512,256]{1,0:T(8,128)(2,1)S(1)} %merge.2.refs_0_), channel_id=1, source_target_pairs={{0,8},{4,12},{8,0},{12,4},{1,9},{5,13},{9,1},{13,5},{2,10},{6,14},... | collective-permute-start | bytes 786440 | tf_op jit(solution)/shard_map/ppermute | solution.py:451
  91.4 14.5 %collective-permute-start.16 = (bf16[512,256]{1,0:T(8,128)(2,1)S(1)}, bf16[512,256]{1,0:T(8,128)(2,1)S(1)}, u32[]{:S(2)}, u32[]{:S(2)}) collective-permute-start(bf16[512,256]{1,0:T(8,128)(2,1)S(1)} %merge.2.refs_0_), channel_id=1, source_target_pairs={{0,12},{4,0},{8,4},{12,8},{1,13},{5,1},{9,5},{13,9},{2,14},{6,2},{... | collective-permute-start | bytes 786440 | tf_op jit(solution)/shard_map/ppermute | solution.py:451
  92.5 10.7 %collective-permute-start.18 = (bf16[512,128]{1,0:T(8,128)(2,1)S(1)}, bf16[512,128]{1,0:T(8,128)(2,1)S(1)}, u32[]{:S(2)}, u32[]{:S(2)}) collective-permute-start(bf16[512,128]{1,0:T(8,128)(2,1)S(1)} %merge.3.refs_0_), channel_id=1, source_target_pairs={{0,8},{4,12},{8,0},{12,4},{1,9},{5,13},{9,1},{13,5},{2,10},{6,14},... | collective-permute-start | bytes 393224 | tf_op jit(solution)/shard_map/ppermute | solution.py:451
  93.8 10.7 %collective-permute-start.19 = (bf16[512,128]{1,0:T(8,128)(2,1)S(1)}, bf16[512,128]{1,0:T(8,128)(2,1)S(1)}, u32[]{:S(2)}, u32[]{:S(2)}) collective-permute-start(bf16[512,128]{1,0:T(8,128)(2,1)S(1)} %merge.3.refs_0_), channel_id=1, source_target_pairs={{0,12},{4,0},{8,4},{12,8},{1,13},{5,1},{9,5},{13,9},{2,14},{6,2},{... | collective-permute-start | bytes 393224 | tf_op jit(solution)/shard_map/ppermute | solution.py:451
  105.8 7.5 %copy-start.5 = (f32[768]{0:T(1024)S(1)}, f32[768]{0:T(1024)}, u32[]{:S(2)}) copy-start(f32[768]{0:T(1024)} %param.20) | copy-start | bytes 9220
  105.8 7.5 %copy-start.6 = (f32[768]{0:T(1024)S(1)}, f32[768]{0:T(1024)}, u32[]{:S(2)}) copy-start(f32[768]{0:T(1024)} %param.21) | copy-start | bytes 9220
  107.1 8.1 %collective-permute-start.20 = (bf16[512,768]{1,0:T(8,128)(2,1)S(1)}, bf16[512,768]{1,0:T(8,128)(2,1)S(1)}, u32[]{:S(2)}, u32[]{:S(2)}) collective-permute-start(bf16[512,768]{1,0:T(8,128)(2,1)S(1)} %project.5), channel_id=1, source_target_pairs={{0,2},{2,0},{1,3},{3,1},{4,6},{6,4},{5,7},{7,5},{8,10},{10,8},{9,1... | collective-permute-start | bytes 2359304 | tf_op jit(solution)/shard_map/ppermute | solution.py:456
  113.3 1.9 %copy-start = (bf16[256,768]{1,0:T(8,128)(2,1)S(1)}, bf16[256,768]{1,0:T(8,128)(2,1)}, u32[]{:S(2)}) copy-start(bf16[256,768]{1,0:T(8,128)(2,1)} %res.1) | copy-start | bytes 1179652
  113.4 1.9 %copy-start.1 = (bf16[256,768]{1,0:T(8,128)(2,1)S(1)}, bf16[256,768]{1,0:T(8,128)(2,1)}, u32[]{:S(2)}) copy-start(bf16[256,768]{1,0:T(8,128)(2,1)} %res_t.1) | copy-start | bytes 1179652

commit v2 on v1

--- a/solution.py
+++ b/solution.py
@@ -220,7 +220,7 @@
         in_specs=[spec_whole()] * len(arrays),
         out_specs=[spec_whole()] * len(outs),
         scratch_shapes=[pltpu.VMEM((n * rows, 2 * rows), F32)],
-        compiler_params=params(20),
+        compiler_params=params(8),
         cost_estimate=pl.CostEstimate(
             flops=4 * heads * 2 * 2 * rows * n * rows * HD * 8,
             bytes_accessed=heads * 2 * rows * HD * 4 * (n + 2),
@@ -309,7 +309,7 @@
         functools.partial(stage_kernel, groups),
         out_shape=[jax.ShapeDtypeStruct((count * n * HD, width), BF16) for _, n in groups],
         in_specs=[pl.BlockSpec(memory_space=pltpu.SMEM)]
-        + [pl.BlockSpec(memory_space=pltpu.HBM)] * count,
+        + [pl.BlockSpec(memory_space=pl.ANY)] * count,
         out_specs=[spec_whole()] * len(groups),
         scratch_shapes=[pltpu.SemaphoreType.DMA((2 * count * len(groups),))],
         compiler_params=params(),
@@ -338,7 +338,7 @@
             out[:, to : to + step] = total.astype(out.dtype)
 
 
-def project(atts, weight, halves, acc, dtype):
+def project(atts, weight, halves, acc, dtype, cost=0):
     rows = atts[0].shape[0]
     depth, width = weight.shape[0], len(halves) * weight.shape[1] // 2
     arrays = [*atts, weight] + ([] if acc is None else [acc])
@@ -349,7 +349,7 @@
         out_specs=spec_whole(),
         compiler_params=params(16),
         cost_estimate=pl.CostEstimate(
-            flops=rows * width * depth,
+            flops=max(cost, rows * width * depth),
             bytes_accessed=width * (rows * 6 + depth * 2),
             transcendentals=0,
         ),
@@ -423,7 +423,6 @@
         return lax.ppermute(after(part, *others), "x", ring_pairs(n_x, d))
 
     near = [piece(1), piece(n_x - 1)]
-    pieces = [near[0]] + [piece(d, *near) for d in range(2, n_x - 1)] + [near[1]]
 
     def hop(pair):
         return lax.ppermute(pair[0], "z", up), lax.ppermute(pair[1], "z", down)
@@ -437,20 +436,21 @@
     state = run([packed, *step1])
     step3 = hop(each(step2, state, *near))
     state = run([*step2], state=state)
+    far_pieces = [piece(d, *near, state) for d in range(2, n_x - 1)]
+    pieces = [near[0], *far_pieces, near[1]]
     step4 = turn(each(step3, state))
     state = run([*step3], state=state)
     own, *far = run([step4], state=state, final=True)
     staged = stage(groups, here, in_hbm(weight), [in_hbm(item) for item in after(pieces, own)])
-
-    gathered, arrived = [], own
-    for group, item in zip(groups, far):
-        waits = (arrived, staged) if group[0] else ()
-        arrived = lax.ppermute(after(item, *waits), "y_hi", swap)
-        att = merge(*group, own, arrived, 10**10 if group[0] else 0)
+    arrived = [lax.ppermute(item, "y_hi", swap) for item in far]
+    arrived[0] = after(arrived[0], staged)
+    gathered = []
+    for group, item in zip(groups, arrived):
+        att = merge(*group, own, item, 10**10 if group[0] else 0)
         gathered.append(
             [att] + [lax.ppermute(att, "x", ring_pairs(n_x, d)) for d in range(1, n_x)]
         )
-    acc = project(gathered[0], staged[0], (0, 1), None, F32)
+    acc = project(gathered[0], staged[0], (0, 1), None, F32, 10**10)
     run = functools.partial(project, gathered[1], staged[1])
     to_core = run((1,), acc, BF16)
     from_core = lax.ppermute(to_core, "core", swap)

time: 117 us -> 111 us (0.949)
  waiting for transfers between devices: 49.4 us -> 45 us
  starting transfers between devices: 41.5 us -> 39 us
    ppermute x2, waiting for transfers between devices: 5.25 us -> 1.19 us  [per_device(): arrived = [lax.ppermute(item, 'y_hi', swap) for item in far]]
    ppermute x1, starting transfers between devices: 6.2 us -> 4.67 us  [per_device(): from_core = lax.ppermute(to_core, 'core', swap)]
    ppermute x8, waiting for transfers between devices: 20.2 us -> 18.9 us  [hop(): return (lax.ppermute(pair[0], 'z', up), lax.ppermute(pair[1], 'z', down))]
  transfers between devices with their start and end apart: 21 -> 21, of which waited for: 12 -> 10; matrix products, arithmetic and copies ran while one was open for 3% -> 3% of each run, Pallas kernels for 14% -> 15%
where the time goes in v2:
time: 111 us
  waiting for transfers between devices  45 us (41%)
  starting transfers between devices  39 us (35%)
  Pallas kernels  20.6 us (19%)
  local copies, waits for them, and re-layouts  5.35 us (5%)
    ppermute x8, waiting for transfers between devices, hop(): return (lax.ppermute(pair[0], 'z', up), lax.ppermute(pair[1], 'z', down))  18.9 us
    ppermute x8, starting transfers between devices, hop(): return (lax.ppermute(pair[0], 'z', up), lax.ppermute(pair[1], 'z', down))  14.7 us
    ppermute x3, waiting for transfers between devices, piece(): return lax.ppermute(after(part, *others), 'x', ring_pairs(n_x, d))  11.6 us
    ppermute x6, waiting for transfers between devices, per_device(): lax.ppermute(att, 'x', ring_pairs(n_x, d))  10.3 us
    pallas_call x4, Pallas kernels, attend(): pl.pallas_call(functools.partial(attend_kernel, kinds, groups, state is n...  9.76 us
    ppermute x6, starting transfers between devices, per_device(): lax.ppermute(att, 'x', ring_pairs(n_x, d))  7.99 us
    ppermute x3, starting transfers between devices, piece(): return lax.ppermute(after(part, *others), 'x', ring_pairs(n_x, d))  5.51 us
    ppermute x1, starting transfers between devices, per_device(): from_core = lax.ppermute(to_core, 'core', swap)  4.67 us
  transfers between devices with their start and end apart: 21, of which 10 were waited for; matrix products, arithmetic and copies ran while one was open for 3% of the time, Pallas kernels for 15%

profile of v2, /device:TPU:1, one launch (start us, length us, event | category | flops | bytes accessed | tf_op | source)
XLA Modules:
  0.0 110.9 jit_solution(2279079612549672929)
XLA Ops:
  0.6 1.2 %pack.1.refs_2_ = bf16[2,768,256]{2,1,0:T(8,128)(2,1)S(1)} custom-call(bf16[256,384]{1,0:T(8,128)(2,1)} %k.1, bf16[256,384]{1,0:T(8,128)(2,1)} %kt.1, bf16[256,384]{1,0:T(8,128)(2,1)} %v.1, bf16[256,384]{1,0:T(8,128)(2,1)} %vt.1), custom_call_target="tpu_custom_call" | custom-call | bytes 1572864 | tf_op jit(solution)/shard_map/pack/pallas_call | solution.py:88
  1.9 2.5 %collective-permute-start.1 = (bf16[2,768,256]{2,1,0:T(8,128)(2,1)S(1)}, bf16[2,768,256]{2,1,0:T(8,128)(2,1)S(1)}, u32[]{:S(2)}, u32[]{:S(2)}) collective-permute-start(bf16[2,768,256]{2,1,0:T(8,128)(2,1)S(1)} %pack.1.refs_2_), channel_id=1, source_target_pairs={{0,32},{32,64},{64,96},{96,128},{128,160},{160,192},{192,224},{224... | collective-permute-start | bytes 2359304 | tf_op jit(solution)/shard_map/ppermute | solution.py:428
  4.4 4.0 %collective-permute-start.3 = (bf16[2,768,256]{2,1,0:T(8,128)(2,1)S(1)}, bf16[2,768,256]{2,1,0:T(8,128)(2,1)S(1)}, u32[]{:S(2)}, u32[]{:S(2)}) collective-permute-start(bf16[2,768,256]{2,1,0:T(8,128)(2,1)S(1)} %pack.1.refs_2_), channel_id=1, source_target_pairs={{0,224},{32,0},{64,32},{96,64},{128,96},{160,128},{192,160},{224,1... | collective-permute-start | bytes 2359304 | tf_op jit(solution)/shard_map/ppermute | solution.py:428
  9.5 3.0 %collective-permute-start = (bf16[256,768]{1,0:T(8,128)(2,1)S(1)}, bf16[256,768]{1,0:T(8,128)(2,1)S(1)}, u32[]{:S(2)}, u32[]{:S(2)}) collective-permute-start(bf16[256,768]{1,0:T(8,128)(2,1)S(1)} %pack_queries.1.refs_0_), channel_id=1, source_target_pairs={{0,16},{16,0},{1,17},{17,1},{2,18},{18,2},{3,19},{19,3},{4,20},{20... | collective-permute-start | bytes 1179656 | tf_op jit(solution)/shard_map/ppermute | solution.py:415
  12.5 3.2 %constant_dynamic-slice_fusion = (bf16[384,1536]{1,0:T(8,128)(2,1)}, bf16[384,1536]{1,0:T(8,128)(2,1)S(1)}, bf16[384,1536]{1,0:T(8,128)(2,1)S(1)}) fusion(bf16[384,6144]{1,0:T(8,128)(2,1)} %weight.1, s32[]{:T(128)S(6)} %select_n.11, s32[]{:T(128)S(6)} %select_n.10, s32[]{:T(128)S(6)} %select_n.9), kind=kLoop, calls=%fused_computation.2 | loop fusion | bytes 7077900 | tf_op jit(solution)/shard_map/dynamic_slice | solution.py:422
  15.7 1.2 %collective-permute-start.4 = (bf16[384,1536]{1,0:T(8,128)(2,1)S(1)}, bf16[384,1536]{1,0:T(8,128)(2,1)S(1)}, u32[]{:S(2)}, u32[]{:S(2)}) collective-permute-start(bf16[384,1536]{1,0:T(8,128)(2,1)S(1)} %get-tuple-element.36), channel_id=1, source_target_pairs={{0,4},{4,8},{8,12},{12,0},{1,5},{5,9},{9,13},{13,1},{2,6},{6,10},{... | collective-permute-start | bytes 3538952 | tf_op jit(solution)/shard_map/ppermute | solution.py:423
  16.9 1.5 %collective-permute-start.5 = (bf16[384,1536]{1,0:T(8,128)(2,1)S(1)}, bf16[384,1536]{1,0:T(8,128)(2,1)S(1)}, u32[]{:S(2)}, u32[]{:S(2)}) collective-permute-start(bf16[384,1536]{1,0:T(8,128)(2,1)S(1)} %get-tuple-element.35), channel_id=1, source_target_pairs={{0,12},{4,0},{8,4},{12,8},{1,13},{5,1},{9,5},{13,9},{2,14},{6,2},{... | collective-permute-start | bytes 3538952 | tf_op jit(solution)/shard_map/ppermute | solution.py:423
  18.4 2.4 %collective-permute-done.refs_1_ = bf16[256,768]{1,0:T(8,128)(2,1)S(1)} collective-permute-done((bf16[256,768]{1,0:T(8,128)(2,1)S(1)}, bf16[256,768]{1,0:T(8,128)(2,1)S(1)}, u32[]{:S(2)}, u32[]{:S(2)}) %collective-permute-start) | collective-permute-done | bytes 393248 | tf_op jit(solution)/shard_map/ppermute | solution.py:415
  20.7 4.9 %collective-permute-done.1.refs_3_ = bf16[2,768,256]{2,1,0:T(8,128)(2,1)S(1)} collective-permute-done((bf16[2,768,256]{2,1,0:T(8,128)(2,1)S(1)}, bf16[2,768,256]{2,1,0:T(8,128)(2,1)S(1)}, u32[]{:S(2)}, u32[]{:S(2)}) %collective-permute-start.1) | collective-permute-done | bytes 786464 | tf_op jit(solution)/shard_map/ppermute | solution.py:428
  25.6 2.7 %collective-permute-start.7 = (bf16[2,768,256]{2,1,0:T(8,128)(2,1)S(1)}, bf16[2,768,256]{2,1,0:T(8,128)(2,1)S(1)}, u32[]{:S(2)}, u32[]{:S(2)}) collective-permute-start(bf16[2,768,256]{2,1,0:T(8,128)(2,1)S(1)} %collective-permute-done.3.refs_4_), channel_id=1, source_target_pairs={{0,224},{32,0},{64,32},{96,64},{128,96},{160,128},{192,160},{224,1... | collective-permute-start | bytes 2359304 | tf_op jit(solution)/shard_map/ppermute | solution.py:428
  28.3 3.2 %attend.4.refs_4_ = f32[792,512]{1,0:T(8,128)S(1)} custom-call(bf16[256,768]{1,0:T(8,128)(2,1)S(1)} %pack_queries.1.refs_0_, bf16[256,768]{1,0:T(8,128)(2,1)S(1)} %collective-permute-done.refs_1_, bf16[2,768,256]{2,1,0:T(8,128)(2,1)S(1)} %pack.1.refs_2_, bf16[2,768,256]{2,1,0:T(8,128)(2,1)S(1)} %collective-permute-done.1.refs_3_, ...), custom_call_target="tpu_custom_call" | custom-call | flops 9663676416 | bytes 3932160 | tf_op jit(solution)/shard_map/attend/pallas_call | solution.py:217
  31.5 11.6 %collective-permute-done.4.refs_0_ = bf16[384,1536]{1,0:T(8,128)(2,1)S(1)} collective-permute-done((bf16[384,1536]{1,0:T(8,128)(2,1)S(1)}, bf16[384,1536]{1,0:T(8,128)(2,1)S(1)}, u32[]{:S(2)}, u32[]{:S(2)}) %collective-permute-start.4) | collective-permute-done | bytes 1179680 | tf_op jit(solution)/shard_map/ppermute | solution.py:423
  44.6 2.7 %collective-permute-start.9 = (bf16[2,768,256]{2,1,0:T(8,128)(2,1)S(1)}, bf16[2,768,256]{2,1,0:T(8,128)(2,1)S(1)}, u32[]{:S(2)}, u32[]{:S(2)}) collective-permute-start(bf16[2,768,256]{2,1,0:T(8,128)(2,1)S(1)} %collective-permute-done.7.refs_3_), channel_id=1, source_target_pairs={{0,224},{32,0},{64,32},{96,64},{128,96},{160,128},{192,160},{224,1... | collective-permute-start | bytes 2359304 | tf_op jit(solution)/shard_map/ppermute | solution.py:428
  47.3 2.5 %attend.5.refs_4_ = f32[792,512]{1,0:T(8,128)S(1)} custom-call(bf16[256,768]{1,0:T(8,128)(2,1)S(1)} %pack_queries.1.refs_0_, bf16[256,768]{1,0:T(8,128)(2,1)S(1)} %collective-permute-done.refs_1_, bf16[2,768,256]{2,1,0:T(8,128)(2,1)S(1)} %collective-permute-done.2.refs_2_, bf16[2,768,256]{2,1,0:T(8,128)(2,1)S(1)} %collective-permute-done.7.refs_3_, ...), custom_call_target="tpu_custom_call" | custom-call | flops 6442450944 | bytes 3145728 | tf_op jit(solution)/shard_map/attend/pallas_call | solution.py:217
  49.8 2.8 %collective-permute-start.15 = (bf16[384,1536]{1,0:T(8,128)(2,1)}, bf16[384,1536]{1,0:T(8,128)(2,1)S(1)}, u32[]{:S(2)}, u32[]{:S(2)}) collective-permute-start(bf16[384,1536]{1,0:T(8,128)(2,1)} %get-tuple-element.26), channel_id=1, source_target_pairs={{0,8},{4,12},{8,0},{12,4},{1,9},{5,13},{9,1},{13,5},{2,10},{6,14},... | collective-permute-start | bytes 3538952 | tf_op jit(solution)/shard_map/ppermute | solution.py:423
  52.6 10.1 %collective-permute-done.6.refs_2_ = bf16[2,768,256]{2,1,0:T(8,128)(2,1)S(1)} collective-permute-done((bf16[2,768,256]{2,1,0:T(8,128)(2,1)S(1)}, bf16[2,768,256]{2,1,0:T(8,128)(2,1)S(1)}, u32[]{:S(2)}, u32[]{:S(2)}) %collective-permute-start.6) | collective-permute-done | bytes 786464 | tf_op jit(solution)/shard_map/ppermute | solution.py:428
  62.9 2.7 %collective-permute-start.10 = (bf16[768,256]{1,0:T(8,128)(2,1)S(1)}, bf16[768,256]{1,0:T(8,128)(2,1)S(1)}, u32[]{:S(2)}, u32[]{:S(2)}) collective-permute-start(bf16[768,256]{1,0:T(8,128)(2,1)S(1)} %slice_bitcast_fusion), channel_id=1, source_target_pairs={{0,224},{32,0},{64,32},{96,64},{128,96},{160,128},{192,160},{224,1... | collective-permute-start | bytes 1179656 | tf_op jit(solution)/shard_map/ppermute | solution.py:428
  65.6 2.5 %attend.6.refs_4_ = f32[792,512]{1,0:T(8,128)S(1)} custom-call(bf16[256,768]{1,0:T(8,128)(2,1)S(1)} %pack_queries.1.refs_0_, bf16[256,768]{1,0:T(8,128)(2,1)S(1)} %collective-permute-done.refs_1_, bf16[2,768,256]{2,1,0:T(8,128)(2,1)S(1)} %collective-permute-done.6.refs_2_, bf16[2,768,256]{2,1,0:T(8,128)(2,1)S(1)} %collective-permute-done.9.refs_3_, ...), custom_call_target="tpu_custom_call" | custom-call | flops 6442450944 | bytes 3145728 | tf_op jit(solution)/shard_map/attend/pallas_call | solution.py:217
  68.1 3.5 %collective-permute-done.8.refs_2_ = bf16[768,256]{1,0:T(8,128)(2,1)S(1)} collective-permute-done((bf16[768,256]{1,0:T(8,128)(2,1)S(1)}, bf16[768,256]{1,0:T(8,128)(2,1)S(1)}, u32[]{:S(2)}, u32[]{:S(2)}) %collective-permute-start.8) | collective-permute-done | bytes 393248 | tf_op jit(solution)/shard_map/ppermute | solution.py:428
  71.6 1.6 %attend.7 = (f32[792,256]{1,0:T(8,128)S(1)}, bf16[272,256]{1,0:T(8,128)(2,1)S(1)}, bf16[544,256]{1,0:T(8,128)(2,1)S(1)}) custom-call(bf16[256,768]{1,0:T(8,128)(2,1)S(1)} %pack_queries.1.refs_0_, bf16[256,768]{1,0:T(8,128)(2,1)S(1)} %collective-permute-done.refs_1_, bf16[768,256]{1,0:T(8,128)(2,1)S(1)} %collective-permute-done.8.refs_2_, ...), custom_call_target="tpu_custom_call" | custom-call | flops 3221225472 | bytes 2359296 | tf_op jit(solution)/shard_map/attend/pallas_call | solution.py:217
  73.2 3.0 %collective-permute-start.11 = (bf16[544,256]{1,0:T(8,128)(2,1)S(1)}, bf16[544,256]{1,0:T(8,128)(2,1)S(1)}, u32[]{:S(2)}, u32[]{:S(2)}) collective-permute-start(bf16[544,256]{1,0:T(8,128)(2,1)S(1)} %get-tuple-element.25), channel_id=1, source_target_pairs={{0,16},{16,0},{1,17},{17,1},{2,18},{18,2},{3,19},{19,3},{4,20},{20... | collective-permute-start | bytes 835592 | tf_op jit(solution)/shard_map/ppermute | solution.py:445
  77.4 3.1 %stage.1 = (bf16[512,1536]{1,0:T(8,128)(2,1)S(1)}, bf16[1024,1536]{1,0:T(8,128)(2,1)S(1)}) custom-call(s32[2]{0:T(128)S(1)} %pad_add_fusion.place, bf16[384,6144]{1,0:T(8,128)(2,1)} %weight.1, bf16[384,1536]{1,0:T(8,128)(2,1)} %copy-done.2, bf16[384,1536]{1,0:T(8,128)(2,1)} %copy-done.4, bf16[384,1536]{1,0:T(8,128)(2,1)} %copy-done.3), custom_call_target="tpu_custom_call" | custom-call | bytes 9437184 | tf_op jit(solution)/shard_map/stage/pallas_call | solution.py:308
  80.5 1.2 %collective-permute-done.16.far_ref = bf16[272,256]{1,0:T(8,128)(2,1)S(1)} collective-permute-done((bf16[272,256]{1,0:T(8,128)(2,1)S(1)}, bf16[272,256]{1,0:T(8,128)(2,1)S(1)}, u32[]{:S(2)}, u32[]{:S(2)}) %collective-permute-start.16) | collective-permute-done | bytes 139296 | tf_op jit(solution)/shard_map/ppermute | solution.py:445
  81.8 1.3 %collective-permute-start.17 = (bf16[512,128]{1,0:T(8,128)(2,1)S(1)}, bf16[512,128]{1,0:T(8,128)(2,1)S(1)}, u32[]{:S(2)}, u32[]{:S(2)}) collective-permute-start(bf16[512,128]{1,0:T(8,128)(2,1)S(1)} %merge.3.refs_0_), channel_id=1, source_target_pairs={{0,4},{4,8},{8,12},{12,0},{1,5},{5,9},{9,13},{13,1},{2,6},{6,10},{... | collective-permute-start | bytes 393224 | tf_op jit(solution)/shard_map/ppermute | solution.py:451
  83.1 2.5 %collective-permute-start.18 = (bf16[512,128]{1,0:T(8,128)(2,1)S(1)}, bf16[512,128]{1,0:T(8,128)(2,1)S(1)}, u32[]{:S(2)}, u32[]{:S(2)}) collective-permute-start(bf16[512,128]{1,0:T(8,128)(2,1)S(1)} %merge.3.refs_0_), channel_id=1, source_target_pairs={{0,8},{4,12},{8,0},{12,4},{1,9},{5,13},{9,1},{13,5},{2,10},{6,14},... | collective-permute-start | bytes 393224 | tf_op jit(solution)/shard_map/ppermute | solution.py:451
  88.4 1.6 %collective-permute-start.14 = (bf16[512,256]{1,0:T(8,128)(2,1)S(1)}, bf16[512,256]{1,0:T(8,128)(2,1)S(1)}, u32[]{:S(2)}, u32[]{:S(2)}) collective-permute-start(bf16[512,256]{1,0:T(8,128)(2,1)S(1)} %merge.2.refs_0_), channel_id=1, source_target_pairs={{0,12},{4,0},{8,4},{12,8},{1,13},{5,1},{9,5},{13,9},{2,14},{6,2},{... | collective-permute-start | bytes 786440 | tf_op jit(solution)/shard_map/ppermute | solution.py:451
  90.1 1.3 %project.3.refs_5_ = f32[512,1536]{1,0:T(8,128)S(1)} custom-call(bf16[512,128]{1,0:T(8,128)(2,1)S(1)} %merge.3.refs_0_, bf16[512,128]{1,0:T(8,128)(2,1)S(1)} %collective-permute-done.17.refs_1_, bf16[512,128]{1,0:T(8,128)(2,1)S(1)} %collective-permute-done.18.refs_2_, bf16[512,128]{1,0:T(8,128)(2,1)S(1)} %collective-permute-done.19.refs_3_, ...), custom_call_target="tpu_custom_call" | custom-call | flops 10000000000 | bytes 6291456 | tf_op jit(solution)/shard_map/project/pallas_call | solution.py:345
  91.3 9.2 %collective-permute-done.12.refs_1_ = bf16[512,256]{1,0:T(8,128)(2,1)S(1)} collective-permute-done((bf16[512,256]{1,0:T(8,128)(2,1)S(1)}, bf16[512,256]{1,0:T(8,128)(2,1)S(1)}, u32[]{:S(2)}, u32[]{:S(2)}) %collective-permute-start.12) | collective-permute-done | bytes 262176 | tf_op jit(solution)/shard_map/ppermute | solution.py:451
  101.7 1.2 %project.5 = bf16[512,768]{1,0:T(8,128)(2,1)S(1)} custom-call(bf16[512,256]{1,0:T(8,128)(2,1)S(1)} %merge.2.refs_0_, bf16[512,256]{1,0:T(8,128)(2,1)S(1)} %collective-permute-done.12.refs_1_, bf16[512,256]{1,0:T(8,128)(2,1)S(1)} %collective-permute-done.13.refs_2_, bf16[512,256]{1,0:T(8,128)(2,1)S(1)} %collective-permute-done.14.refs_3_, ...), custom_call_target="tpu_custom_call" | custom-call | flops 402653184 | bytes 3932160 | tf_op jit(solution)/shard_map/project/pallas_call | solution.py:345
  102.9 4.7 %collective-permute-start.20 = (bf16[512,768]{1,0:T(8,128)(2,1)S(1)}, bf16[512,768]{1,0:T(8,128)(2,1)S(1)}, u32[]{:S(2)}, u32[]{:S(2)}) collective-permute-start(bf16[512,768]{1,0:T(8,128)(2,1)S(1)} %project.5), channel_id=1, source_target_pairs={{0,2},{2,0},{1,3},{3,1},{4,6},{6,4},{5,7},{7,5},{8,10},{10,8},{9,1... | collective-permute-start | bytes 2359304 | tf_op jit(solution)/shard_map/ppermute | solution.py:456
  107.7 1.3 %project.4.mine = f32[512,768]{1,0:T(8,128)S(1)} custom-call(bf16[512,256]{1,0:T(8,128)(2,1)S(1)} %merge.2.refs_0_, bf16[512,256]{1,0:T(8,128)(2,1)S(1)} %collective-permute-done.12.refs_1_, bf16[512,256]{1,0:T(8,128)(2,1)S(1)} %collective-permute-done.13.refs_2_, bf16[512,256]{1,0:T(8,128)(2,1)S(1)} %collective-permute-done.14.refs_3_, ...), custom_call_target="tpu_custom_call" | custom-call | flops 402653184 | bytes 3932160 | tf_op jit(solution)/shard_map/project/pallas_call | solution.py:345
  109.5 1.3 %finish.1 = (bf16[256,768]{1,0:T(8,128)(2,1)}, bf16[256,768]{1,0:T(8,128)(2,1)}) custom-call(f32[512,768]{1,0:T(8,128)S(1)} %project.4.mine, bf16[512,768]{1,0:T(8,128)(2,1)S(1)} %collective-permute-done.20.other, bf16[256,768]{1,0:T(8,128)(2,1)S(1)} %copy-done, bf16[256,768]{1,0:T(8,128)(2,1)S(1)} %copy-done.1, f32[1,768]{1,0:T(1,128)S(1)} %broadcast_in_dim.6.gate, ...), custom_call_target="tpu_custom_call" | custom-call | bytes 3932160 | tf_op jit(solution)/shard_map/finish/pallas_call | solution.py:377
  (43 shorter events, 8.6 us)
Async XLA Ops:
  1.9 23.8 %collective-permute-start.1 = (bf16[2,768,256]{2,1,0:T(8,128)(2,1)S(1)}, bf16[2,768,256]{2,1,0:T(8,128)(2,1)S(1)}, u32[]{:S(2)}, u32[]{:S(2)}) collective-permute-start(bf16[2,768,256]{2,1,0:T(8,128)(2,1)S(1)} %pack.1.refs_2_), channel_id=1, source_target_pairs={{0,32},{32,64},{64,96},{96,128},{128,160},{160,192},{192,224},{224... | collective-permute-start | bytes 2359304 | tf_op jit(solution)/shard_map/ppermute | solution.py:428
  4.4 21.2 %collective-permute-start.3 = (bf16[2,768,256]{2,1,0:T(8,128)(2,1)S(1)}, bf16[2,768,256]{2,1,0:T(8,128)(2,1)S(1)}, u32[]{:S(2)}, u32[]{:S(2)}) collective-permute-start(bf16[2,768,256]{2,1,0:T(8,128)(2,1)S(1)} %pack.1.refs_2_), channel_id=1, source_target_pairs={{0,224},{32,0},{64,32},{96,64},{128,96},{160,128},{192,160},{224,1... | collective-permute-start | bytes 2359304 | tf_op jit(solution)/shard_map/ppermute | solution.py:428
  9.5 11.3 %collective-permute-start = (bf16[256,768]{1,0:T(8,128)(2,1)S(1)}, bf16[256,768]{1,0:T(8,128)(2,1)S(1)}, u32[]{:S(2)}, u32[]{:S(2)}) collective-permute-start(bf16[256,768]{1,0:T(8,128)(2,1)S(1)} %pack_queries.1.refs_0_), channel_id=1, source_target_pairs={{0,16},{16,0},{1,17},{17,1},{2,18},{18,2},{3,19},{19,3},{4,20},{20... | collective-permute-start | bytes 1179656 | tf_op jit(solution)/shard_map/ppermute | solution.py:415
  15.7 27.4 %collective-permute-start.4 = (bf16[384,1536]{1,0:T(8,128)(2,1)S(1)}, bf16[384,1536]{1,0:T(8,128)(2,1)S(1)}, u32[]{:S(2)}, u32[]{:S(2)}) collective-permute-start(bf16[384,1536]{1,0:T(8,128)(2,1)S(1)} %get-tuple-element.36), channel_id=1, source_target_pairs={{0,4},{4,8},{8,12},{12,0},{1,5},{5,9},{9,13},{13,1},{2,6},{6,10},{... | collective-permute-start | bytes 3538952 | tf_op jit(solution)/shard_map/ppermute | solution.py:423
  16.9 26.2 %collective-permute-start.5 = (bf16[384,1536]{1,0:T(8,128)(2,1)S(1)}, bf16[384,1536]{1,0:T(8,128)(2,1)S(1)}, u32[]{:S(2)}, u32[]{:S(2)}) collective-permute-start(bf16[384,1536]{1,0:T(8,128)(2,1)S(1)} %get-tuple-element.35), channel_id=1, source_target_pairs={{0,12},{4,0},{8,4},{12,8},{1,13},{5,1},{9,5},{13,9},{2,14},{6,2},{... | collective-permute-start | bytes 3538952 | tf_op jit(solution)/shard_map/ppermute | solution.py:423
  25.6 19.0 %collective-permute-start.2 = (bf16[2,768,256]{2,1,0:T(8,128)(2,1)S(1)}, bf16[2,768,256]{2,1,0:T(8,128)(2,1)S(1)}, u32[]{:S(2)}, u32[]{:S(2)}) collective-permute-start(bf16[2,768,256]{2,1,0:T(8,128)(2,1)S(1)} %collective-permute-done.1.refs_3_), channel_id=1, source_target_pairs={{0,32},{32,64},{64,96},{96,128},{128,160},{160,192},{192,224},{224... | collective-permute-start | bytes 2359304 | tf_op jit(solution)/shard_map/ppermute | solution.py:428
  25.6 19.0 %collective-permute-start.7 = (bf16[2,768,256]{2,1,0:T(8,128)(2,1)S(1)}, bf16[2,768,256]{2,1,0:T(8,128)(2,1)S(1)}, u32[]{:S(2)}, u32[]{:S(2)}) collective-permute-start(bf16[2,768,256]{2,1,0:T(8,128)(2,1)S(1)} %collective-permute-done.3.refs_4_), channel_id=1, source_target_pairs={{0,224},{32,0},{64,32},{96,64},{128,96},{160,128},{192,160},{224,1... | collective-permute-start | bytes 2359304 | tf_op jit(solution)/shard_map/ppermute | solution.py:428
  43.1 6.6 %copy-start.2 = (bf16[384,1536]{1,0:T(8,128)(2,1)}, bf16[384,1536]{1,0:T(8,128)(2,1)S(1)}, u32[]{:S(2)}) copy-start(bf16[384,1536]{1,0:T(8,128)(2,1)S(1)} %collective-permute-done.4.refs_0_) | copy-start | bytes 3538948
  43.1 1.0 copy-start.3
  44.6 18.1 %collective-permute-start.6 = (bf16[2,768,256]{2,1,0:T(8,128)(2,1)S(1)}, bf16[2,768,256]{2,1,0:T(8,128)(2,1)S(1)}, u32[]{:S(2)}, u32[]{:S(2)}) collective-permute-start(bf16[2,768,256]{2,1,0:T(8,128)(2,1)S(1)} %collective-permute-done.2.refs_2_), channel_id=1, source_target_pairs={{0,32},{32,64},{64,96},{96,128},{128,160},{160,192},{192,224},{224... | collective-permute-start | bytes 2359304 | tf_op jit(solution)/shard_map/ppermute | solution.py:428
  44.6 18.2 %collective-permute-start.9 = (bf16[2,768,256]{2,1,0:T(8,128)(2,1)S(1)}, bf16[2,768,256]{2,1,0:T(8,128)(2,1)S(1)}, u32[]{:S(2)}, u32[]{:S(2)}) collective-permute-start(bf16[2,768,256]{2,1,0:T(8,128)(2,1)S(1)} %collective-permute-done.7.refs_3_), channel_id=1, source_target_pairs={{0,224},{32,0},{64,32},{96,64},{128,96},{160,128},{192,160},{224,1... | collective-permute-start | bytes 2359304 | tf_op jit(solution)/shard_map/ppermute | solution.py:428
  49.8 26.6 %collective-permute-start.15 = (bf16[384,1536]{1,0:T(8,128)(2,1)}, bf16[384,1536]{1,0:T(8,128)(2,1)S(1)}, u32[]{:S(2)}, u32[]{:S(2)}) collective-permute-start(bf16[384,1536]{1,0:T(8,128)(2,1)} %get-tuple-element.26), channel_id=1, source_target_pairs={{0,8},{4,12},{8,0},{12,4},{1,9},{5,13},{9,1},{13,5},{2,10},{6,14},... | collective-permute-start | bytes 3538952 | tf_op jit(solution)/shard_map/ppermute | solution.py:423
  62.8 8.8 %collective-permute-start.8 = (bf16[768,256]{1,0:T(8,128)(2,1)S(1)}, bf16[768,256]{1,0:T(8,128)(2,1)S(1)}, u32[]{:S(2)}, u32[]{:S(2)}) collective-permute-start(bf16[768,256]{1,0:T(8,128)(2,1)S(1)} %slice_bitcast_fusion.1), channel_id=1, source_target_pairs={{0,32},{32,64},{64,96},{96,128},{128,160},{160,192},{192,224},{224... | collective-permute-start | bytes 1179656 | tf_op jit(solution)/shard_map/ppermute | solution.py:428
  62.9 8.7 %collective-permute-start.10 = (bf16[768,256]{1,0:T(8,128)(2,1)S(1)}, bf16[768,256]{1,0:T(8,128)(2,1)S(1)}, u32[]{:S(2)}, u32[]{:S(2)}) collective-permute-start(bf16[768,256]{1,0:T(8,128)(2,1)S(1)} %slice_bitcast_fusion), channel_id=1, source_target_pairs={{0,224},{32,0},{64,32},{96,64},{128,96},{160,128},{192,160},{224,1... | collective-permute-start | bytes 1179656 | tf_op jit(solution)/shard_map/ppermute | solution.py:428
  73.2 13.5 %collective-permute-start.11 = (bf16[544,256]{1,0:T(8,128)(2,1)S(1)}, bf16[544,256]{1,0:T(8,128)(2,1)S(1)}, u32[]{:S(2)}, u32[]{:S(2)}) collective-permute-start(bf16[544,256]{1,0:T(8,128)(2,1)S(1)} %get-tuple-element.25), channel_id=1, source_target_pairs={{0,16},{16,0},{1,17},{17,1},{2,18},{18,2},{3,19},{19,3},{4,20},{20... | collective-permute-start | bytes 835592 | tf_op jit(solution)/shard_map/ppermute | solution.py:445
  76.2 5.5 %collective-permute-start.16 = (bf16[272,256]{1,0:T(8,128)(2,1)S(1)}, bf16[272,256]{1,0:T(8,128)(2,1)S(1)}, u32[]{:S(2)}, u32[]{:S(2)}) collective-permute-start(bf16[272,256]{1,0:T(8,128)(2,1)S(1)} %get-tuple-element.31), channel_id=1, source_target_pairs={{0,16},{16,0},{1,17},{17,1},{2,18},{18,2},{3,19},{19,3},{4,20},{20... | collective-permute-start | bytes 417800 | tf_op jit(solution)/shard_map/ppermute | solution.py:445
  76.4 1.0 copy-start.4
  81.8 6.6 %collective-permute-start.17 = (bf16[512,128]{1,0:T(8,128)(2,1)S(1)}, bf16[512,128]{1,0:T(8,128)(2,1)S(1)}, u32[]{:S(2)}, u32[]{:S(2)}) collective-permute-start(bf16[512,128]{1,0:T(8,128)(2,1)S(1)} %merge.3.refs_0_), channel_id=1, source_target_pairs={{0,4},{4,8},{8,12},{12,0},{1,5},{5,9},{9,13},{13,1},{2,6},{6,10},{... | collective-permute-start | bytes 393224 | tf_op jit(solution)/shard_map/ppermute | solution.py:451
  83.1 6.9 %collective-permute-start.18 = (bf16[512,128]{1,0:T(8,128)(2,1)S(1)}, bf16[512,128]{1,0:T(8,128)(2,1)S(1)}, u32[]{:S(2)}, u32[]{:S(2)}) collective-permute-start(bf16[512,128]{1,0:T(8,128)(2,1)S(1)} %merge.3.refs_0_), channel_id=1, source_target_pairs={{0,8},{4,12},{8,0},{12,4},{1,9},{5,13},{9,1},{13,5},{2,10},{6,14},... | collective-permute-start | bytes 393224 | tf_op jit(solution)/shard_map/ppermute | solution.py:451
  85.6 4.5 %collective-permute-start.19 = (bf16[512,128]{1,0:T(8,128)(2,1)S(1)}, bf16[512,128]{1,0:T(8,128)(2,1)S(1)}, u32[]{:S(2)}, u32[]{:S(2)}) collective-permute-start(bf16[512,128]{1,0:T(8,128)(2,1)S(1)} %merge.3.refs_0_), channel_id=1, source_target_pairs={{0,12},{4,0},{8,4},{12,8},{1,13},{5,1},{9,5},{13,9},{2,14},{6,2},{... | collective-permute-start | bytes 393224 | tf_op jit(solution)/shard_map/ppermute | solution.py:451
  86.9 13.6 %collective-permute-start.12 = (bf16[512,256]{1,0:T(8,128)(2,1)S(1)}, bf16[512,256]{1,0:T(8,128)(2,1)S(1)}, u32[]{:S(2)}, u32[]{:S(2)}) collective-permute-start(bf16[512,256]{1,0:T(8,128)(2,1)S(1)} %merge.2.refs_0_), channel_id=1, source_target_pairs={{0,4},{4,8},{8,12},{12,0},{1,5},{5,9},{9,13},{13,1},{2,6},{6,10},{... | collective-permute-start | bytes 786440 | tf_op jit(solution)/shard_map/ppermute | solution.py:451
  87.6 13.0 %collective-permute-start.13 = (bf16[512,256]{1,0:T(8,128)(2,1)S(1)}, bf16[512,256]{1,0:T(8,128)(2,1)S(1)}, u32[]{:S(2)}, u32[]{:S(2)}) collective-permute-start(bf16[512,256]{1,0:T(8,128)(2,1)S(1)} %merge.2.refs_0_), channel_id=1, source_target_pairs={{0,8},{4,12},{8,0},{12,4},{1,9},{5,13},{9,1},{13,5},{2,10},{6,14},... | collective-permute-start | bytes 786440 | tf_op jit(solution)/shard_map/ppermute | solution.py:451
  88.4 13.2 %collective-permute-start.14 = (bf16[512,256]{1,0:T(8,128)(2,1)S(1)}, bf16[512,256]{1,0:T(8,128)(2,1)S(1)}, u32[]{:S(2)}, u32[]{:S(2)}) collective-permute-start(bf16[512,256]{1,0:T(8,128)(2,1)S(1)} %merge.2.refs_0_), channel_id=1, source_target_pairs={{0,12},{4,0},{8,4},{12,8},{1,13},{5,1},{9,5},{13,9},{2,14},{6,2},{... | collective-permute-start | bytes 786440 | tf_op jit(solution)/shard_map/ppermute | solution.py:451
  91.3 16.3 %copy-start.5 = (f32[768]{0:T(1024)S(1)}, f32[768]{0:T(1024)}, u32[]{:S(2)}) copy-start(f32[768]{0:T(1024)} %param.20) | copy-start | bytes 9220
  91.3 16.3 %copy-start.6 = (f32[768]{0:T(1024)S(1)}, f32[768]{0:T(1024)}, u32[]{:S(2)}) copy-start(f32[768]{0:T(1024)} %param.21) | copy-start | bytes 9220
  102.9 6.6 %collective-permute-start.20 = (bf16[512,768]{1,0:T(8,128)(2,1)S(1)}, bf16[512,768]{1,0:T(8,128)(2,1)S(1)}, u32[]{:S(2)}, u32[]{:S(2)}) collective-permute-start(bf16[512,768]{1,0:T(8,128)(2,1)S(1)} %project.5), channel_id=1, source_target_pairs={{0,2},{2,0},{1,3},{3,1},{4,6},{6,4},{5,7},{7,5},{8,10},{10,8},{9,1... | collective-permute-start | bytes 2359304 | tf_op jit(solution)/shard_map/ppermute | solution.py:456
  107.6 1.9 %copy-start = (bf16[256,768]{1,0:T(8,128)(2,1)S(1)}, bf16[256,768]{1,0:T(8,128)(2,1)}, u32[]{:S(2)}) copy-start(bf16[256,768]{1,0:T(8,128)(2,1)} %res.1) | copy-start | bytes 1179652
  107.6 1.9 %copy-start.1 = (bf16[256,768]{1,0:T(8,128)(2,1)S(1)}, bf16[256,768]{1,0:T(8,128)(2,1)}, u32[]{:S(2)}) copy-start(bf16[256,768]{1,0:T(8,128)(2,1)} %res_t.1) | copy-start | bytes 1179652

commit v3 on v2

--- a/solution.py
+++ b/solution.py
@@ -406,7 +406,7 @@
     n_z, n_x = sizes
     heads = q.shape[1] // HD
     features = residual.shape[1]
-    groups = [(0, 1), (1, heads - 1)]
+    groups = [(0, heads - 1), (heads - 1, 1)]
     swap = [(0, 1), (1, 0)]
     up, down = ring_pairs(n_z, 1), ring_pairs(n_z, -1)
     q, qt, k, kt, v, vt = (in_hbm(item) for item in (q, qt, k, kt, v, vt))

time: 111 us -> 107 us (0.964)
  waiting for transfers between devices: 45 us -> 39.9 us
  starting transfers between devices: 39 us -> 40.4 us
    ppermute x6, waiting for transfers between devices: 10.3 us -> 5.82 us  [per_device(): lax.ppermute(att, 'x', ring_pairs(n_x, d))]
    ppermute x1, starting transfers between devices: 4.67 us -> 6.03 us  [per_device(): from_core = lax.ppermute(to_core, 'core', swap)]
    ppermute x2, waiting for transfers between devices: 1.19 us -> 0.01 us  [per_device(): arrived = [lax.ppermute(item, 'y_hi', swap) for item in far]]
  transfers between devices with their start and end apart: 21 -> 21, of which waited for: 10 -> 10; matrix products, arithmetic and copies ran while one was open for 3% -> 3% of each run, Pallas kernels for 15% -> 16%
where the time goes in v3:
time: 107 us
  starting transfers between devices  40.4 us (38%)
  waiting for transfers between devices  39.9 us (37%)
  Pallas kernels  20.5 us (19%)
  local copies, waits for them, and re-layouts  5.35 us (5%)
    ppermute x8, waiting for transfers between devices, hop(): return (lax.ppermute(pair[0], 'z', up), lax.ppermute(pair[1], 'z', down))  18.9 us
    ppermute x8, starting transfers between devices, hop(): return (lax.ppermute(pair[0], 'z', up), lax.ppermute(pair[1], 'z', down))  14.7 us
    ppermute x3, waiting for transfers between devices, piece(): return lax.ppermute(after(part, *others), 'x', ring_pairs(n_x, d))  11.6 us
    pallas_call x4, Pallas kernels, attend(): pl.pallas_call(functools.partial(attend_kernel, kinds, groups, state is n...  9.77 us
    ppermute x6, starting transfers between devices, per_device(): lax.ppermute(att, 'x', ring_pairs(n_x, d))  8 us
    ppermute x1, starting transfers between devices, per_device(): from_core = lax.ppermute(to_core, 'core', swap)  6.03 us
    ppermute x6, waiting for transfers between devices, per_device(): lax.ppermute(att, 'x', ring_pairs(n_x, d))  5.82 us
    ppermute x3, starting transfers between devices, piece(): return lax.ppermute(after(part, *others), 'x', ring_pairs(n_x, d))  5.51 us
  transfers between devices with their start and end apart: 21, of which 10 were waited for; matrix products, arithmetic and copies ran while one was open for 3% of the time, Pallas kernels for 16%

profile of v3, /device:TPU:1, one launch (start us, length us, event | category | flops | bytes accessed | tf_op | source)
XLA Modules:
  0.0 107.0 jit_solution(4217767349671000612)
XLA Ops:
  0.6 1.2 %pack.1.refs_2_ = bf16[2,768,256]{2,1,0:T(8,128)(2,1)S(1)} custom-call(bf16[256,384]{1,0:T(8,128)(2,1)} %k.1, bf16[256,384]{1,0:T(8,128)(2,1)} %kt.1, bf16[256,384]{1,0:T(8,128)(2,1)} %v.1, bf16[256,384]{1,0:T(8,128)(2,1)} %vt.1), custom_call_target="tpu_custom_call" | custom-call | bytes 1572864 | tf_op jit(solution)/shard_map/pack/pallas_call | solution.py:88
  1.9 2.5 %collective-permute-start.1 = (bf16[2,768,256]{2,1,0:T(8,128)(2,1)S(1)}, bf16[2,768,256]{2,1,0:T(8,128)(2,1)S(1)}, u32[]{:S(2)}, u32[]{:S(2)}) collective-permute-start(bf16[2,768,256]{2,1,0:T(8,128)(2,1)S(1)} %pack.1.refs_2_), channel_id=1, source_target_pairs={{0,32},{32,64},{64,96},{96,128},{128,160},{160,192},{192,224},{224... | collective-permute-start | bytes 2359304 | tf_op jit(solution)/shard_map/ppermute | solution.py:428
  4.4 4.0 %collective-permute-start.3 = (bf16[2,768,256]{2,1,0:T(8,128)(2,1)S(1)}, bf16[2,768,256]{2,1,0:T(8,128)(2,1)S(1)}, u32[]{:S(2)}, u32[]{:S(2)}) collective-permute-start(bf16[2,768,256]{2,1,0:T(8,128)(2,1)S(1)} %pack.1.refs_2_), channel_id=1, source_target_pairs={{0,224},{32,0},{64,32},{96,64},{128,96},{160,128},{192,160},{224,1... | collective-permute-start | bytes 2359304 | tf_op jit(solution)/shard_map/ppermute | solution.py:428
  9.5 3.0 %collective-permute-start = (bf16[256,768]{1,0:T(8,128)(2,1)S(1)}, bf16[256,768]{1,0:T(8,128)(2,1)S(1)}, u32[]{:S(2)}, u32[]{:S(2)}) collective-permute-start(bf16[256,768]{1,0:T(8,128)(2,1)S(1)} %pack_queries.1.refs_0_), channel_id=1, source_target_pairs={{0,16},{16,0},{1,17},{17,1},{2,18},{18,2},{3,19},{19,3},{4,20},{20... | collective-permute-start | bytes 1179656 | tf_op jit(solution)/shard_map/ppermute | solution.py:415
  12.5 3.2 %constant_dynamic-slice_fusion = (bf16[384,1536]{1,0:T(8,128)(2,1)}, bf16[384,1536]{1,0:T(8,128)(2,1)S(1)}, bf16[384,1536]{1,0:T(8,128)(2,1)S(1)}) fusion(bf16[384,6144]{1,0:T(8,128)(2,1)} %weight.1, s32[]{:T(128)S(6)} %select_n.11, s32[]{:T(128)S(6)} %select_n.10, s32[]{:T(128)S(6)} %select_n.9), kind=kLoop, calls=%fused_computation.2 | loop fusion | bytes 7077900 | tf_op jit(solution)/shard_map/dynamic_slice | solution.py:422
  15.7 1.2 %collective-permute-start.4 = (bf16[384,1536]{1,0:T(8,128)(2,1)S(1)}, bf16[384,1536]{1,0:T(8,128)(2,1)S(1)}, u32[]{:S(2)}, u32[]{:S(2)}) collective-permute-start(bf16[384,1536]{1,0:T(8,128)(2,1)S(1)} %get-tuple-element.36), channel_id=1, source_target_pairs={{0,4},{4,8},{8,12},{12,0},{1,5},{5,9},{9,13},{13,1},{2,6},{6,10},{... | collective-permute-start | bytes 3538952 | tf_op jit(solution)/shard_map/ppermute | solution.py:423
  16.9 1.5 %collective-permute-start.5 = (bf16[384,1536]{1,0:T(8,128)(2,1)S(1)}, bf16[384,1536]{1,0:T(8,128)(2,1)S(1)}, u32[]{:S(2)}, u32[]{:S(2)}) collective-permute-start(bf16[384,1536]{1,0:T(8,128)(2,1)S(1)} %get-tuple-element.35), channel_id=1, source_target_pairs={{0,12},{4,0},{8,4},{12,8},{1,13},{5,1},{9,5},{13,9},{2,14},{6,2},{... | collective-permute-start | bytes 3538952 | tf_op jit(solution)/shard_map/ppermute | solution.py:423
  18.4 2.4 %collective-permute-done.refs_1_ = bf16[256,768]{1,0:T(8,128)(2,1)S(1)} collective-permute-done((bf16[256,768]{1,0:T(8,128)(2,1)S(1)}, bf16[256,768]{1,0:T(8,128)(2,1)S(1)}, u32[]{:S(2)}, u32[]{:S(2)}) %collective-permute-start) | collective-permute-done | bytes 393248 | tf_op jit(solution)/shard_map/ppermute | solution.py:415
  20.7 4.9 %collective-permute-done.1.refs_3_ = bf16[2,768,256]{2,1,0:T(8,128)(2,1)S(1)} collective-permute-done((bf16[2,768,256]{2,1,0:T(8,128)(2,1)S(1)}, bf16[2,768,256]{2,1,0:T(8,128)(2,1)S(1)}, u32[]{:S(2)}, u32[]{:S(2)}) %collective-permute-start.1) | collective-permute-done | bytes 786464 | tf_op jit(solution)/shard_map/ppermute | solution.py:428
  25.6 2.7 %collective-permute-start.7 = (bf16[2,768,256]{2,1,0:T(8,128)(2,1)S(1)}, bf16[2,768,256]{2,1,0:T(8,128)(2,1)S(1)}, u32[]{:S(2)}, u32[]{:S(2)}) collective-permute-start(bf16[2,768,256]{2,1,0:T(8,128)(2,1)S(1)} %collective-permute-done.3.refs_4_), channel_id=1, source_target_pairs={{0,224},{32,0},{64,32},{96,64},{128,96},{160,128},{192,160},{224,1... | collective-permute-start | bytes 2359304 | tf_op jit(solution)/shard_map/ppermute | solution.py:428
  28.3 3.2 %attend.4.refs_4_ = f32[792,512]{1,0:T(8,128)S(1)} custom-call(bf16[256,768]{1,0:T(8,128)(2,1)S(1)} %pack_queries.1.refs_0_, bf16[256,768]{1,0:T(8,128)(2,1)S(1)} %collective-permute-done.refs_1_, bf16[2,768,256]{2,1,0:T(8,128)(2,1)S(1)} %pack.1.refs_2_, bf16[2,768,256]{2,1,0:T(8,128)(2,1)S(1)} %collective-permute-done.1.refs_3_, ...), custom_call_target="tpu_custom_call" | custom-call | flops 9663676416 | bytes 3932160 | tf_op jit(solution)/shard_map/attend/pallas_call | solution.py:217
  31.5 11.6 %collective-permute-done.4.refs_0_ = bf16[384,1536]{1,0:T(8,128)(2,1)S(1)} collective-permute-done((bf16[384,1536]{1,0:T(8,128)(2,1)S(1)}, bf16[384,1536]{1,0:T(8,128)(2,1)S(1)}, u32[]{:S(2)}, u32[]{:S(2)}) %collective-permute-start.4) | collective-permute-done | bytes 1179680 | tf_op jit(solution)/shard_map/ppermute | solution.py:423
  44.6 2.7 %collective-permute-start.9 = (bf16[2,768,256]{2,1,0:T(8,128)(2,1)S(1)}, bf16[2,768,256]{2,1,0:T(8,128)(2,1)S(1)}, u32[]{:S(2)}, u32[]{:S(2)}) collective-permute-start(bf16[2,768,256]{2,1,0:T(8,128)(2,1)S(1)} %collective-permute-done.7.refs_3_), channel_id=1, source_target_pairs={{0,224},{32,0},{64,32},{96,64},{128,96},{160,128},{192,160},{224,1... | collective-permute-start | bytes 2359304 | tf_op jit(solution)/shard_map/ppermute | solution.py:428
  47.3 2.5 %attend.5.refs_4_ = f32[792,512]{1,0:T(8,128)S(1)} custom-call(bf16[256,768]{1,0:T(8,128)(2,1)S(1)} %pack_queries.1.refs_0_, bf16[256,768]{1,0:T(8,128)(2,1)S(1)} %collective-permute-done.refs_1_, bf16[2,768,256]{2,1,0:T(8,128)(2,1)S(1)} %collective-permute-done.2.refs_2_, bf16[2,768,256]{2,1,0:T(8,128)(2,1)S(1)} %collective-permute-done.7.refs_3_, ...), custom_call_target="tpu_custom_call" | custom-call | flops 6442450944 | bytes 3145728 | tf_op jit(solution)/shard_map/attend/pallas_call | solution.py:217
  49.8 2.8 %collective-permute-start.15 = (bf16[384,1536]{1,0:T(8,128)(2,1)}, bf16[384,1536]{1,0:T(8,128)(2,1)S(1)}, u32[]{:S(2)}, u32[]{:S(2)}) collective-permute-start(bf16[384,1536]{1,0:T(8,128)(2,1)} %get-tuple-element.26), channel_id=1, source_target_pairs={{0,8},{4,12},{8,0},{12,4},{1,9},{5,13},{9,1},{13,5},{2,10},{6,14},... | collective-permute-start | bytes 3538952 | tf_op jit(solution)/shard_map/ppermute | solution.py:423
  52.6 10.1 %collective-permute-done.6.refs_2_ = bf16[2,768,256]{2,1,0:T(8,128)(2,1)S(1)} collective-permute-done((bf16[2,768,256]{2,1,0:T(8,128)(2,1)S(1)}, bf16[2,768,256]{2,1,0:T(8,128)(2,1)S(1)}, u32[]{:S(2)}, u32[]{:S(2)}) %collective-permute-start.6) | collective-permute-done | bytes 786464 | tf_op jit(solution)/shard_map/ppermute | solution.py:428
  62.9 2.7 %collective-permute-start.10 = (bf16[768,256]{1,0:T(8,128)(2,1)S(1)}, bf16[768,256]{1,0:T(8,128)(2,1)S(1)}, u32[]{:S(2)}, u32[]{:S(2)}) collective-permute-start(bf16[768,256]{1,0:T(8,128)(2,1)S(1)} %slice_bitcast_fusion), channel_id=1, source_target_pairs={{0,224},{32,0},{64,32},{96,64},{128,96},{160,128},{192,160},{224,1... | collective-permute-start | bytes 1179656 | tf_op jit(solution)/shard_map/ppermute | solution.py:428
  65.6 2.5 %attend.6.refs_4_ = f32[792,512]{1,0:T(8,128)S(1)} custom-call(bf16[256,768]{1,0:T(8,128)(2,1)S(1)} %pack_queries.1.refs_0_, bf16[256,768]{1,0:T(8,128)(2,1)S(1)} %collective-permute-done.refs_1_, bf16[2,768,256]{2,1,0:T(8,128)(2,1)S(1)} %collective-permute-done.6.refs_2_, bf16[2,768,256]{2,1,0:T(8,128)(2,1)S(1)} %collective-permute-done.9.refs_3_, ...), custom_call_target="tpu_custom_call" | custom-call | flops 6442450944 | bytes 3145728 | tf_op jit(solution)/shard_map/attend/pallas_call | solution.py:217
  68.1 3.5 %collective-permute-done.8.refs_2_ = bf16[768,256]{1,0:T(8,128)(2,1)S(1)} collective-permute-done((bf16[768,256]{1,0:T(8,128)(2,1)S(1)}, bf16[768,256]{1,0:T(8,128)(2,1)S(1)}, u32[]{:S(2)}, u32[]{:S(2)}) %collective-permute-start.8) | collective-permute-done | bytes 393248 | tf_op jit(solution)/shard_map/ppermute | solution.py:428
  71.6 1.6 %attend.7 = (f32[792,256]{1,0:T(8,128)S(1)}, bf16[544,256]{1,0:T(8,128)(2,1)S(1)}, bf16[272,256]{1,0:T(8,128)(2,1)S(1)}) custom-call(bf16[256,768]{1,0:T(8,128)(2,1)S(1)} %pack_queries.1.refs_0_, bf16[256,768]{1,0:T(8,128)(2,1)S(1)} %collective-permute-done.refs_1_, bf16[768,256]{1,0:T(8,128)(2,1)S(1)} %collective-permute-done.8.refs_2_, ...), custom_call_target="tpu_custom_call" | custom-call | flops 3221225472 | bytes 2359296 | tf_op jit(solution)/shard_map/attend/pallas_call | solution.py:217
  73.2 3.0 %collective-permute-start.16 = (bf16[544,256]{1,0:T(8,128)(2,1)S(1)}, bf16[544,256]{1,0:T(8,128)(2,1)S(1)}, u32[]{:S(2)}, u32[]{:S(2)}) collective-permute-start(bf16[544,256]{1,0:T(8,128)(2,1)S(1)} %get-tuple-element.31), channel_id=1, source_target_pairs={{0,16},{16,0},{1,17},{17,1},{2,18},{18,2},{3,19},{19,3},{4,20},{20... | collective-permute-start | bytes 835592 | tf_op jit(solution)/shard_map/ppermute | solution.py:445
  77.4 3.0 %stage.1 = (bf16[1024,1536]{1,0:T(8,128)(2,1)S(1)}, bf16[512,1536]{1,0:T(8,128)(2,1)S(1)}) custom-call(s32[2]{0:T(128)S(1)} %pad_add_fusion.place, bf16[384,6144]{1,0:T(8,128)(2,1)} %weight.1, bf16[384,1536]{1,0:T(8,128)(2,1)} %copy-done.2, bf16[384,1536]{1,0:T(8,128)(2,1)} %copy-done.4, bf16[384,1536]{1,0:T(8,128)(2,1)} %copy-done.3), custom_call_target="tpu_custom_call" | custom-call | bytes 9437184 | tf_op jit(solution)/shard_map/stage/pallas_call | solution.py:308
  80.6 1.3 %collective-permute-start.17 = (bf16[512,256]{1,0:T(8,128)(2,1)S(1)}, bf16[512,256]{1,0:T(8,128)(2,1)S(1)}, u32[]{:S(2)}, u32[]{:S(2)}) collective-permute-start(bf16[512,256]{1,0:T(8,128)(2,1)S(1)} %merge.3.refs_0_), channel_id=1, source_target_pairs={{0,4},{4,8},{8,12},{12,0},{1,5},{5,9},{9,13},{13,1},{2,6},{6,10},{... | collective-permute-start | bytes 786440 | tf_op jit(solution)/shard_map/ppermute | solution.py:451
  81.9 2.5 %collective-permute-start.18 = (bf16[512,256]{1,0:T(8,128)(2,1)S(1)}, bf16[512,256]{1,0:T(8,128)(2,1)S(1)}, u32[]{:S(2)}, u32[]{:S(2)}) collective-permute-start(bf16[512,256]{1,0:T(8,128)(2,1)S(1)} %merge.3.refs_0_), channel_id=1, source_target_pairs={{0,8},{4,12},{8,0},{12,4},{1,9},{5,13},{9,1},{13,5},{2,10},{6,14},... | collective-permute-start | bytes 786440 | tf_op jit(solution)/shard_map/ppermute | solution.py:451
  84.4 1.2 %collective-permute-start.19 = (bf16[512,256]{1,0:T(8,128)(2,1)S(1)}, bf16[512,256]{1,0:T(8,128)(2,1)S(1)}, u32[]{:S(2)}, u32[]{:S(2)}) collective-permute-start(bf16[512,256]{1,0:T(8,128)(2,1)S(1)} %merge.3.refs_0_), channel_id=1, source_target_pairs={{0,12},{4,0},{8,4},{12,8},{1,13},{5,1},{9,5},{13,9},{2,14},{6,2},{... | collective-permute-start | bytes 786440 | tf_op jit(solution)/shard_map/ppermute | solution.py:451
  87.2 1.6 %collective-permute-start.14 = (bf16[512,128]{1,0:T(8,128)(2,1)S(1)}, bf16[512,128]{1,0:T(8,128)(2,1)S(1)}, u32[]{:S(2)}, u32[]{:S(2)}) collective-permute-start(bf16[512,128]{1,0:T(8,128)(2,1)S(1)} %merge.2.refs_0_), channel_id=1, source_target_pairs={{0,12},{4,0},{8,4},{12,8},{1,13},{5,1},{9,5},{13,9},{2,14},{6,2},{... | collective-permute-start | bytes 393224 | tf_op jit(solution)/shard_map/ppermute | solution.py:451
  88.8 2.3 %collective-permute-done.18.refs_2_ = bf16[512,256]{1,0:T(8,128)(2,1)S(1)} collective-permute-done((bf16[512,256]{1,0:T(8,128)(2,1)S(1)}, bf16[512,256]{1,0:T(8,128)(2,1)S(1)}, u32[]{:S(2)}, u32[]{:S(2)}) %collective-permute-start.18) | collective-permute-done | bytes 262176 | tf_op jit(solution)/shard_map/ppermute | solution.py:451
  91.0 2.3 %project.3.refs_5_ = f32[512,1536]{1,0:T(8,128)S(1)} custom-call(bf16[512,256]{1,0:T(8,128)(2,1)S(1)} %merge.3.refs_0_, bf16[512,256]{1,0:T(8,128)(2,1)S(1)} %collective-permute-done.17.refs_1_, bf16[512,256]{1,0:T(8,128)(2,1)S(1)} %collective-permute-done.18.refs_2_, bf16[512,256]{1,0:T(8,128)(2,1)S(1)} %collective-permute-done.19.refs_3_, ...), custom_call_target="tpu_custom_call" | custom-call | flops 10000000000 | bytes 7864320 | tf_op jit(solution)/shard_map/project/pallas_call | solution.py:345
  94.0 2.9 %collective-permute-done.13.refs_2_ = bf16[512,128]{1,0:T(8,128)(2,1)S(1)} collective-permute-done((bf16[512,128]{1,0:T(8,128)(2,1)S(1)}, bf16[512,128]{1,0:T(8,128)(2,1)S(1)}, u32[]{:S(2)}, u32[]{:S(2)}) %collective-permute-start.13) | collective-permute-done | bytes 131104 | tf_op jit(solution)/shard_map/ppermute | solution.py:451
  97.7 6.0 %collective-permute-start.20 = (bf16[512,768]{1,0:T(8,128)(2,1)S(1)}, bf16[512,768]{1,0:T(8,128)(2,1)S(1)}, u32[]{:S(2)}, u32[]{:S(2)}) collective-permute-start(bf16[512,768]{1,0:T(8,128)(2,1)S(1)} %project.5), channel_id=1, source_target_pairs={{0,2},{2,0},{1,3},{3,1},{4,6},{6,4},{5,7},{7,5},{8,10},{10,8},{9,1... | collective-permute-start | bytes 2359304 | tf_op jit(solution)/shard_map/ppermute | solution.py:456
  104.5 1.1 %collective-permute-done.20.other = bf16[512,768]{1,0:T(8,128)(2,1)S(1)} collective-permute-done((bf16[512,768]{1,0:T(8,128)(2,1)S(1)}, bf16[512,768]{1,0:T(8,128)(2,1)S(1)}, u32[]{:S(2)}, u32[]{:S(2)}) %collective-permute-start.20) | collective-permute-done | bytes 786464 | tf_op jit(solution)/shard_map/ppermute | solution.py:456
  105.6 1.3 %finish.1 = (bf16[256,768]{1,0:T(8,128)(2,1)}, bf16[256,768]{1,0:T(8,128)(2,1)}) custom-call(f32[512,768]{1,0:T(8,128)S(1)} %project.4.mine, bf16[512,768]{1,0:T(8,128)(2,1)S(1)} %collective-permute-done.20.other, bf16[256,768]{1,0:T(8,128)(2,1)S(1)} %copy-done, bf16[256,768]{1,0:T(8,128)(2,1)S(1)} %copy-done.1, f32[1,768]{1,0:T(1,128)S(1)} %broadcast_in_dim.6.gate, ...), custom_call_target="tpu_custom_call" | custom-call | bytes 3932160 | tf_op jit(solution)/shard_map/finish/pallas_call | solution.py:377
  (43 shorter events, 7.8 us)
Async XLA Ops:
  1.9 23.8 %collective-permute-start.1 = (bf16[2,768,256]{2,1,0:T(8,128)(2,1)S(1)}, bf16[2,768,256]{2,1,0:T(8,128)(2,1)S(1)}, u32[]{:S(2)}, u32[]{:S(2)}) collective-permute-start(bf16[2,768,256]{2,1,0:T(8,128)(2,1)S(1)} %pack.1.refs_2_), channel_id=1, source_target_pairs={{0,32},{32,64},{64,96},{96,128},{128,160},{160,192},{192,224},{224... | collective-permute-start | bytes 2359304 | tf_op jit(solution)/shard_map/ppermute | solution.py:428
  4.4 21.2 %collective-permute-start.3 = (bf16[2,768,256]{2,1,0:T(8,128)(2,1)S(1)}, bf16[2,768,256]{2,1,0:T(8,128)(2,1)S(1)}, u32[]{:S(2)}, u32[]{:S(2)}) collective-permute-start(bf16[2,768,256]{2,1,0:T(8,128)(2,1)S(1)} %pack.1.refs_2_), channel_id=1, source_target_pairs={{0,224},{32,0},{64,32},{96,64},{128,96},{160,128},{192,160},{224,1... | collective-permute-start | bytes 2359304 | tf_op jit(solution)/shard_map/ppermute | solution.py:428
  9.5 11.3 %collective-permute-start = (bf16[256,768]{1,0:T(8,128)(2,1)S(1)}, bf16[256,768]{1,0:T(8,128)(2,1)S(1)}, u32[]{:S(2)}, u32[]{:S(2)}) collective-permute-start(bf16[256,768]{1,0:T(8,128)(2,1)S(1)} %pack_queries.1.refs_0_), channel_id=1, source_target_pairs={{0,16},{16,0},{1,17},{17,1},{2,18},{18,2},{3,19},{19,3},{4,20},{20... | collective-permute-start | bytes 1179656 | tf_op jit(solution)/shard_map/ppermute | solution.py:415
  15.7 27.4 %collective-permute-start.4 = (bf16[384,1536]{1,0:T(8,128)(2,1)S(1)}, bf16[384,1536]{1,0:T(8,128)(2,1)S(1)}, u32[]{:S(2)}, u32[]{:S(2)}) collective-permute-start(bf16[384,1536]{1,0:T(8,128)(2,1)S(1)} %get-tuple-element.36), channel_id=1, source_target_pairs={{0,4},{4,8},{8,12},{12,0},{1,5},{5,9},{9,13},{13,1},{2,6},{6,10},{... | collective-permute-start | bytes 3538952 | tf_op jit(solution)/shard_map/ppermute | solution.py:423
  16.9 26.2 %collective-permute-start.5 = (bf16[384,1536]{1,0:T(8,128)(2,1)S(1)}, bf16[384,1536]{1,0:T(8,128)(2,1)S(1)}, u32[]{:S(2)}, u32[]{:S(2)}) collective-permute-start(bf16[384,1536]{1,0:T(8,128)(2,1)S(1)} %get-tuple-element.35), channel_id=1, source_target_pairs={{0,12},{4,0},{8,4},{12,8},{1,13},{5,1},{9,5},{13,9},{2,14},{6,2},{... | collective-permute-start | bytes 3538952 | tf_op jit(solution)/shard_map/ppermute | solution.py:423
  25.6 19.0 %collective-permute-start.2 = (bf16[2,768,256]{2,1,0:T(8,128)(2,1)S(1)}, bf16[2,768,256]{2,1,0:T(8,128)(2,1)S(1)}, u32[]{:S(2)}, u32[]{:S(2)}) collective-permute-start(bf16[2,768,256]{2,1,0:T(8,128)(2,1)S(1)} %collective-permute-done.1.refs_3_), channel_id=1, source_target_pairs={{0,32},{32,64},{64,96},{96,128},{128,160},{160,192},{192,224},{224... | collective-permute-start | bytes 2359304 | tf_op jit(solution)/shard_map/ppermute | solution.py:428
  25.6 19.0 %collective-permute-start.7 = (bf16[2,768,256]{2,1,0:T(8,128)(2,1)S(1)}, bf16[2,768,256]{2,1,0:T(8,128)(2,1)S(1)}, u32[]{:S(2)}, u32[]{:S(2)}) collective-permute-start(bf16[2,768,256]{2,1,0:T(8,128)(2,1)S(1)} %collective-permute-done.3.refs_4_), channel_id=1, source_target_pairs={{0,224},{32,0},{64,32},{96,64},{128,96},{160,128},{192,160},{224,1... | collective-permute-start | bytes 2359304 | tf_op jit(solution)/shard_map/ppermute | solution.py:428
  43.1 6.6 %copy-start.2 = (bf16[384,1536]{1,0:T(8,128)(2,1)}, bf16[384,1536]{1,0:T(8,128)(2,1)S(1)}, u32[]{:S(2)}) copy-start(bf16[384,1536]{1,0:T(8,128)(2,1)S(1)} %collective-permute-done.4.refs_0_) | copy-start | bytes 3538948
  43.1 1.0 copy-start.3
  44.6 18.1 %collective-permute-start.6 = (bf16[2,768,256]{2,1,0:T(8,128)(2,1)S(1)}, bf16[2,768,256]{2,1,0:T(8,128)(2,1)S(1)}, u32[]{:S(2)}, u32[]{:S(2)}) collective-permute-start(bf16[2,768,256]{2,1,0:T(8,128)(2,1)S(1)} %collective-permute-done.2.refs_2_), channel_id=1, source_target_pairs={{0,32},{32,64},{64,96},{96,128},{128,160},{160,192},{192,224},{224... | collective-permute-start | bytes 2359304 | tf_op jit(solution)/shard_map/ppermute | solution.py:428
  44.6 18.2 %collective-permute-start.9 = (bf16[2,768,256]{2,1,0:T(8,128)(2,1)S(1)}, bf16[2,768,256]{2,1,0:T(8,128)(2,1)S(1)}, u32[]{:S(2)}, u32[]{:S(2)}) collective-permute-start(bf16[2,768,256]{2,1,0:T(8,128)(2,1)S(1)} %collective-permute-done.7.refs_3_), channel_id=1, source_target_pairs={{0,224},{32,0},{64,32},{96,64},{128,96},{160,128},{192,160},{224,1... | collective-permute-start | bytes 2359304 | tf_op jit(solution)/shard_map/ppermute | solution.py:428
  49.8 26.6 %collective-permute-start.15 = (bf16[384,1536]{1,0:T(8,128)(2,1)}, bf16[384,1536]{1,0:T(8,128)(2,1)S(1)}, u32[]{:S(2)}, u32[]{:S(2)}) collective-permute-start(bf16[384,1536]{1,0:T(8,128)(2,1)} %get-tuple-element.26), channel_id=1, source_target_pairs={{0,8},{4,12},{8,0},{12,4},{1,9},{5,13},{9,1},{13,5},{2,10},{6,14},... | collective-permute-start | bytes 3538952 | tf_op jit(solution)/shard_map/ppermute | solution.py:423
  62.8 8.8 %collective-permute-start.8 = (bf16[768,256]{1,0:T(8,128)(2,1)S(1)}, bf16[768,256]{1,0:T(8,128)(2,1)S(1)}, u32[]{:S(2)}, u32[]{:S(2)}) collective-permute-start(bf16[768,256]{1,0:T(8,128)(2,1)S(1)} %slice_bitcast_fusion.1), channel_id=1, source_target_pairs={{0,32},{32,64},{64,96},{96,128},{128,160},{160,192},{192,224},{224... | collective-permute-start | bytes 1179656 | tf_op jit(solution)/shard_map/ppermute | solution.py:428
  62.9 8.7 %collective-permute-start.10 = (bf16[768,256]{1,0:T(8,128)(2,1)S(1)}, bf16[768,256]{1,0:T(8,128)(2,1)S(1)}, u32[]{:S(2)}, u32[]{:S(2)}) collective-permute-start(bf16[768,256]{1,0:T(8,128)(2,1)S(1)} %slice_bitcast_fusion), channel_id=1, source_target_pairs={{0,224},{32,0},{64,32},{96,64},{128,96},{160,128},{192,160},{224,1... | collective-permute-start | bytes 1179656 | tf_op jit(solution)/shard_map/ppermute | solution.py:428
  73.2 7.2 %collective-permute-start.16 = (bf16[544,256]{1,0:T(8,128)(2,1)S(1)}, bf16[544,256]{1,0:T(8,128)(2,1)S(1)}, u32[]{:S(2)}, u32[]{:S(2)}) collective-permute-start(bf16[544,256]{1,0:T(8,128)(2,1)S(1)} %get-tuple-element.31), channel_id=1, source_target_pairs={{0,16},{16,0},{1,17},{17,1},{2,18},{18,2},{3,19},{19,3},{4,20},{20... | collective-permute-start | bytes 835592 | tf_op jit(solution)/shard_map/ppermute | solution.py:445
  76.2 9.3 %collective-permute-start.11 = (bf16[272,256]{1,0:T(8,128)(2,1)S(1)}, bf16[272,256]{1,0:T(8,128)(2,1)S(1)}, u32[]{:S(2)}, u32[]{:S(2)}) collective-permute-start(bf16[272,256]{1,0:T(8,128)(2,1)S(1)} %get-tuple-element.25), channel_id=1, source_target_pairs={{0,16},{16,0},{1,17},{17,1},{2,18},{18,2},{3,19},{19,3},{4,20},{20... | collective-permute-start | bytes 417800 | tf_op jit(solution)/shard_map/ppermute | solution.py:445
  76.4 1.0 copy-start.4
  80.6 6.5 %collective-permute-start.17 = (bf16[512,256]{1,0:T(8,128)(2,1)S(1)}, bf16[512,256]{1,0:T(8,128)(2,1)S(1)}, u32[]{:S(2)}, u32[]{:S(2)}) collective-permute-start(bf16[512,256]{1,0:T(8,128)(2,1)S(1)} %merge.3.refs_0_), channel_id=1, source_target_pairs={{0,4},{4,8},{8,12},{12,0},{1,5},{5,9},{9,13},{13,1},{2,6},{6,10},{... | collective-permute-start | bytes 786440 | tf_op jit(solution)/shard_map/ppermute | solution.py:451
  81.9 9.1 %collective-permute-start.18 = (bf16[512,256]{1,0:T(8,128)(2,1)S(1)}, bf16[512,256]{1,0:T(8,128)(2,1)S(1)}, u32[]{:S(2)}, u32[]{:S(2)}) collective-permute-start(bf16[512,256]{1,0:T(8,128)(2,1)S(1)} %merge.3.refs_0_), channel_id=1, source_target_pairs={{0,8},{4,12},{8,0},{12,4},{1,9},{5,13},{9,1},{13,5},{2,10},{6,14},... | collective-permute-start | bytes 786440 | tf_op jit(solution)/shard_map/ppermute | solution.py:451
  84.4 6.7 %collective-permute-start.19 = (bf16[512,256]{1,0:T(8,128)(2,1)S(1)}, bf16[512,256]{1,0:T(8,128)(2,1)S(1)}, u32[]{:S(2)}, u32[]{:S(2)}) collective-permute-start(bf16[512,256]{1,0:T(8,128)(2,1)S(1)} %merge.3.refs_0_), channel_id=1, source_target_pairs={{0,12},{4,0},{8,4},{12,8},{1,13},{5,1},{9,5},{13,9},{2,14},{6,2},{... | collective-permute-start | bytes 786440 | tf_op jit(solution)/shard_map/ppermute | solution.py:451
  85.7 8.4 %collective-permute-start.12 = (bf16[512,128]{1,0:T(8,128)(2,1)S(1)}, bf16[512,128]{1,0:T(8,128)(2,1)S(1)}, u32[]{:S(2)}, u32[]{:S(2)}) collective-permute-start(bf16[512,128]{1,0:T(8,128)(2,1)S(1)} %merge.2.refs_0_), channel_id=1, source_target_pairs={{0,4},{4,8},{8,12},{12,0},{1,5},{5,9},{9,13},{13,1},{2,6},{6,10},{... | collective-permute-start | bytes 393224 | tf_op jit(solution)/shard_map/ppermute | solution.py:451
  86.3 10.7 %collective-permute-start.13 = (bf16[512,128]{1,0:T(8,128)(2,1)S(1)}, bf16[512,128]{1,0:T(8,128)(2,1)S(1)}, u32[]{:S(2)}, u32[]{:S(2)}) collective-permute-start(bf16[512,128]{1,0:T(8,128)(2,1)S(1)} %merge.2.refs_0_), channel_id=1, source_target_pairs={{0,8},{4,12},{8,0},{12,4},{1,9},{5,13},{9,1},{13,5},{2,10},{6,14},... | collective-permute-start | bytes 393224 | tf_op jit(solution)/shard_map/ppermute | solution.py:451
  87.2 9.8 %collective-permute-start.14 = (bf16[512,128]{1,0:T(8,128)(2,1)S(1)}, bf16[512,128]{1,0:T(8,128)(2,1)S(1)}, u32[]{:S(2)}, u32[]{:S(2)}) collective-permute-start(bf16[512,128]{1,0:T(8,128)(2,1)S(1)} %merge.2.refs_0_), channel_id=1, source_target_pairs={{0,12},{4,0},{8,4},{12,8},{1,13},{5,1},{9,5},{13,9},{2,14},{6,2},{... | collective-permute-start | bytes 393224 | tf_op jit(solution)/shard_map/ppermute | solution.py:451
  93.4 10.3 %copy-start.5 = (f32[768]{0:T(1024)S(1)}, f32[768]{0:T(1024)}, u32[]{:S(2)}) copy-start(f32[768]{0:T(1024)} %param.20) | copy-start | bytes 9220
  93.4 10.3 %copy-start.6 = (f32[768]{0:T(1024)S(1)}, f32[768]{0:T(1024)}, u32[]{:S(2)}) copy-start(f32[768]{0:T(1024)} %param.21) | copy-start | bytes 9220
  97.7 7.9 %collective-permute-start.20 = (bf16[512,768]{1,0:T(8,128)(2,1)S(1)}, bf16[512,768]{1,0:T(8,128)(2,1)S(1)}, u32[]{:S(2)}, u32[]{:S(2)}) collective-permute-start(bf16[512,768]{1,0:T(8,128)(2,1)S(1)} %project.5), channel_id=1, source_target_pairs={{0,2},{2,0},{1,3},{3,1},{4,6},{6,4},{5,7},{7,5},{8,10},{10,8},{9,1... | collective-permute-start | bytes 2359304 | tf_op jit(solution)/shard_map/ppermute | solution.py:456
  103.7 1.9 %copy-start = (bf16[256,768]{1,0:T(8,128)(2,1)S(1)}, bf16[256,768]{1,0:T(8,128)(2,1)}, u32[]{:S(2)}) copy-start(bf16[256,768]{1,0:T(8,128)(2,1)} %res.1) | copy-start | bytes 1179652
  103.7 1.9 %copy-start.1 = (bf16[256,768]{1,0:T(8,128)(2,1)S(1)}, bf16[256,768]{1,0:T(8,128)(2,1)}, u32[]{:S(2)}) copy-start(bf16[256,768]{1,0:T(8,128)(2,1)} %res_t.1) | copy-start | bytes 1179652

commit v4 on v3

--- a/solution.py
+++ b/solution.py
@@ -357,29 +357,35 @@
     )(*arrays)
 
 
-def finish_kernel(mine, other, res, res_t, gate, gate_t, out, out_t):
+def finish_kernel(mine, other, res, res_t, gate, gate_t, out, out_t, block, block_t, sems):
     rows = res.shape[0]
     projected = mine[0:rows, :] + other[0:rows, :].astype(F32)
+    g = gate[...]
+    block[...] = (res[...].astype(F32) + g * projected).astype(block.dtype)
+    first = pltpu.make_async_copy(block, out, sems.at[0])
+    first.start()
     projected_t = mine[rows:, :] + other[rows:, :].astype(F32)
-    g = gate[...]
-    out[...] = (res[...].astype(F32) + g * projected).astype(out.dtype)
-    out_t[...] = (res_t[...].astype(F32) + gate_t[...] * projected + g * projected_t).astype(
-        out_t.dtype
+    block_t[...] = (res_t[...].astype(F32) + gate_t[...] * projected + g * projected_t).astype(
+        block_t.dtype
     )
+    second = pltpu.make_async_copy(block_t, out_t, sems.at[1])
+    second.start()
+    first.wait()
+    second.wait()
 
 
 def finish(mine, other, res, res_t, gate, gate_t):
     rows, width = res.shape
-    step = width // 2
-    tall = pl.BlockSpec((2 * rows, step), lambda i: (0, i))
-    short = pl.BlockSpec((rows, step), lambda i: (0, i))
-    line = pl.BlockSpec((1, step), lambda i: (0, i))
     return pl.pallas_call(
         finish_kernel,
-        grid=(width // step,),
         out_shape=[jax.ShapeDtypeStruct((rows, width), BF16)] * 2,
-        in_specs=[tall, tall, short, short, line, line],
-        out_specs=[short, short],
+        in_specs=[spec_whole()] * 6,
+        out_specs=[pl.BlockSpec(memory_space=pltpu.HBM)] * 2,
+        scratch_shapes=[
+            pltpu.VMEM((rows, width), BF16),
+            pltpu.VMEM((rows, width), BF16),
+            pltpu.SemaphoreType.DMA((2,)),
+        ],
         compiler_params=params(),
         cost_estimate=pl.CostEstimate(flops=0, bytes_accessed=rows * width * 20, transcendentals=0),
         name="finish",
@@ -441,15 +447,17 @@
     step4 = turn(each(step3, state))
     state = run([*step3], state=state)
     own, *far = run([step4], state=state, final=True)
-    staged = stage(groups, here, in_hbm(weight), [in_hbm(item) for item in after(pieces, own)])
-    arrived = [lax.ppermute(item, "y_hi", swap) for item in far]
-    arrived[0] = after(arrived[0], staged)
+    arrived = [
+        lax.ppermute(far[0], "y_hi", swap),
+        lax.ppermute(after(far[1], far_pieces), "y_hi", swap),
+    ]
     gathered = []
     for group, item in zip(groups, arrived):
         att = merge(*group, own, item, 10**10 if group[0] else 0)
         gathered.append(
             [att] + [lax.ppermute(att, "x", ring_pairs(n_x, d)) for d in range(1, n_x)]
         )
+    staged = stage(groups, here, in_hbm(weight), [in_hbm(item) for item in after(pieces, att)])
     acc = project(gathered[0], staged[0], (0, 1), None, F32, 10**10)
     run = functools.partial(project, gathered[1], staged[1])
     to_core = run((1,), acc, BF16)

time: 107 us -> 107 us (level)
  starting transfers between devices: 40.4 us -> 43.5 us
  local copies, waits for them, and re-layouts: 5.35 us -> 3.36 us
  waiting for transfers between devices: 39.9 us -> 38.5 us
    ppermute x6, waiting for transfers between devices: 5.82 us -> 2.48 us  [per_device(): lax.ppermute(att, 'x', ring_pairs(n_x, d))]
    ppermute x2, starting transfers between devices: 3.1 us -> 5.82 us  [the longest x1 3 us: per_device(): lax.ppermute(far[0], 'y_hi', swap)]
    ppermute x2, waiting for transfers between devices: 0.01 us -> 1.1 us  [the longest x1 1.09 us: per_device(): lax.ppermute(far[0], 'y_hi', swap)]
  transfers between devices with their start and end apart: 21 -> 21, of which waited for: 10 -> 10; matrix products, arithmetic and copies ran while one was open for 3% -> 2% of each run, Pallas kernels for 16% -> 16%
where the time goes in v4:
time: 107 us
  starting transfers between devices  43.5 us (41%)
  waiting for transfers between devices  38.5 us (36%)
  Pallas kernels  20.2 us (19%)
  local copies, waits for them, and re-layouts  3.36 us (3%)
    ppermute x8, waiting for transfers between devices, hop(): return (lax.ppermute(pair[0], 'z', up), lax.ppermute(pair[1], 'z', down))  19.8 us
    ppermute x8, starting transfers between devices, hop(): return (lax.ppermute(pair[0], 'z', up), lax.ppermute(pair[1], 'z', down))  14.7 us
    ppermute x3, waiting for transfers between devices, piece(): return lax.ppermute(after(part, *others), 'x', ring_pairs(n_x, d))  10.7 us
    pallas_call x4, Pallas kernels, attend(): pl.pallas_call(functools.partial(attend_kernel, kinds, groups, state is n...  9.77 us
    ppermute x6, starting transfers between devices, per_device(): lax.ppermute(att, 'x', ring_pairs(n_x, d))  8.07 us
    ppermute x1, starting transfers between devices, per_device(): from_core = lax.ppermute(to_core, 'core', swap)  6.31 us
    ppermute x3, starting transfers between devices, piece(): return lax.ppermute(after(part, *others), 'x', ring_pairs(n_x, d))  5.59 us
    pallas_call x3, Pallas kernels, project(): pl.pallas_call(functools.partial(project_kernel, halves, acc is not None)...  3.75 us
  transfers between devices with their start and end apart: 21, of which 10 were waited for; matrix products, arithmetic and copies ran while one was open for 2% of the time, Pallas kernels for 16%

profile of v4, /device:TPU:1, one launch (start us, length us, event | category | flops | bytes accessed | tf_op | source)
XLA Modules:
  0.0 106.7 jit_solution(13068206637851432670)
XLA Ops:
  0.6 1.2 %pack.1.refs_2_ = bf16[2,768,256]{2,1,0:T(8,128)(2,1)S(1)} custom-call(bf16[256,384]{1,0:T(8,128)(2,1)} %k.1, bf16[256,384]{1,0:T(8,128)(2,1)} %kt.1, bf16[256,384]{1,0:T(8,128)(2,1)} %v.1, bf16[256,384]{1,0:T(8,128)(2,1)} %vt.1), custom_call_target="tpu_custom_call" | custom-call | bytes 1572864 | tf_op jit(solution)/shard_map/pack/pallas_call | solution.py:88
  1.9 2.5 %collective-permute-start.1 = (bf16[2,768,256]{2,1,0:T(8,128)(2,1)S(1)}, bf16[2,768,256]{2,1,0:T(8,128)(2,1)S(1)}, u32[]{:S(2)}, u32[]{:S(2)}) collective-permute-start(bf16[2,768,256]{2,1,0:T(8,128)(2,1)S(1)} %pack.1.refs_2_), channel_id=1, source_target_pairs={{0,32},{32,64},{64,96},{96,128},{128,160},{160,192},{192,224},{224... | collective-permute-start | bytes 2359304 | tf_op jit(solution)/shard_map/ppermute | solution.py:434
  4.4 4.0 %collective-permute-start.3 = (bf16[2,768,256]{2,1,0:T(8,128)(2,1)S(1)}, bf16[2,768,256]{2,1,0:T(8,128)(2,1)S(1)}, u32[]{:S(2)}, u32[]{:S(2)}) collective-permute-start(bf16[2,768,256]{2,1,0:T(8,128)(2,1)S(1)} %pack.1.refs_2_), channel_id=1, source_target_pairs={{0,224},{32,0},{64,32},{96,64},{128,96},{160,128},{192,160},{224,1... | collective-permute-start | bytes 2359304 | tf_op jit(solution)/shard_map/ppermute | solution.py:434
  9.5 3.0 %collective-permute-start = (bf16[256,768]{1,0:T(8,128)(2,1)S(1)}, bf16[256,768]{1,0:T(8,128)(2,1)S(1)}, u32[]{:S(2)}, u32[]{:S(2)}) collective-permute-start(bf16[256,768]{1,0:T(8,128)(2,1)S(1)} %pack_queries.1.refs_0_), channel_id=1, source_target_pairs={{0,16},{16,0},{1,17},{17,1},{2,18},{18,2},{3,19},{19,3},{4,20},{20... | collective-permute-start | bytes 1179656 | tf_op jit(solution)/shard_map/ppermute | solution.py:421
  12.5 2.2 %constant_dynamic-slice_fusion = (bf16[384,1536]{1,0:T(8,128)(2,1)S(1)}, bf16[384,1536]{1,0:T(8,128)(2,1)S(1)}, bf16[384,1536]{1,0:T(8,128)(2,1)S(1)}) fusion(bf16[384,6144]{1,0:T(8,128)(2,1)} %weight.1, s32[]{:T(128)S(6)} %select_n.11, s32[]{:T(128)S(6)} %select_n.10, s32[]{:T(128)S(6)} %select_n.9), kind=kLoop, calls=%fused_computation.2 | loop fusion | bytes 7077900 | tf_op jit(solution)/shard_map/dynamic_slice | solution.py:428
  14.7 1.3 %collective-permute-start.4 = (bf16[384,1536]{1,0:T(8,128)(2,1)S(1)}, bf16[384,1536]{1,0:T(8,128)(2,1)S(1)}, u32[]{:S(2)}, u32[]{:S(2)}) collective-permute-start(bf16[384,1536]{1,0:T(8,128)(2,1)S(1)} %get-tuple-element.36), channel_id=1, source_target_pairs={{0,4},{4,8},{8,12},{12,0},{1,5},{5,9},{9,13},{13,1},{2,6},{6,10},{... | collective-permute-start | bytes 3538952 | tf_op jit(solution)/shard_map/ppermute | solution.py:429
  16.0 1.5 %collective-permute-start.5 = (bf16[384,1536]{1,0:T(8,128)(2,1)S(1)}, bf16[384,1536]{1,0:T(8,128)(2,1)S(1)}, u32[]{:S(2)}, u32[]{:S(2)}) collective-permute-start(bf16[384,1536]{1,0:T(8,128)(2,1)S(1)} %get-tuple-element.35), channel_id=1, source_target_pairs={{0,12},{4,0},{8,4},{12,8},{1,13},{5,1},{9,5},{13,9},{2,14},{6,2},{... | collective-permute-start | bytes 3538952 | tf_op jit(solution)/shard_map/ppermute | solution.py:429
  17.5 3.3 %collective-permute-done.refs_1_ = bf16[256,768]{1,0:T(8,128)(2,1)S(1)} collective-permute-done((bf16[256,768]{1,0:T(8,128)(2,1)S(1)}, bf16[256,768]{1,0:T(8,128)(2,1)S(1)}, u32[]{:S(2)}, u32[]{:S(2)}) %collective-permute-start) | collective-permute-done | bytes 393248 | tf_op jit(solution)/shard_map/ppermute | solution.py:421
  20.7 4.9 %collective-permute-done.1.refs_3_ = bf16[2,768,256]{2,1,0:T(8,128)(2,1)S(1)} collective-permute-done((bf16[2,768,256]{2,1,0:T(8,128)(2,1)S(1)}, bf16[2,768,256]{2,1,0:T(8,128)(2,1)S(1)}, u32[]{:S(2)}, u32[]{:S(2)}) %collective-permute-start.1) | collective-permute-done | bytes 786464 | tf_op jit(solution)/shard_map/ppermute | solution.py:434
  25.6 2.7 %collective-permute-start.7 = (bf16[2,768,256]{2,1,0:T(8,128)(2,1)S(1)}, bf16[2,768,256]{2,1,0:T(8,128)(2,1)S(1)}, u32[]{:S(2)}, u32[]{:S(2)}) collective-permute-start(bf16[2,768,256]{2,1,0:T(8,128)(2,1)S(1)} %collective-permute-done.3.refs_4_), channel_id=1, source_target_pairs={{0,224},{32,0},{64,32},{96,64},{128,96},{160,128},{192,160},{224,1... | collective-permute-start | bytes 2359304 | tf_op jit(solution)/shard_map/ppermute | solution.py:434
  28.3 3.2 %attend.4.refs_4_ = f32[792,512]{1,0:T(8,128)S(1)} custom-call(bf16[256,768]{1,0:T(8,128)(2,1)S(1)} %pack_queries.1.refs_0_, bf16[256,768]{1,0:T(8,128)(2,1)S(1)} %collective-permute-done.refs_1_, bf16[2,768,256]{2,1,0:T(8,128)(2,1)S(1)} %pack.1.refs_2_, bf16[2,768,256]{2,1,0:T(8,128)(2,1)S(1)} %collective-permute-done.1.refs_3_, ...), custom_call_target="tpu_custom_call" | custom-call | flops 9663676416 | bytes 3932160 | tf_op jit(solution)/shard_map/attend/pallas_call | solution.py:217
  31.5 10.7 %collective-permute-done.4.refs_0_ = bf16[384,1536]{1,0:T(8,128)(2,1)S(1)} collective-permute-done((bf16[384,1536]{1,0:T(8,128)(2,1)S(1)}, bf16[384,1536]{1,0:T(8,128)(2,1)S(1)}, u32[]{:S(2)}, u32[]{:S(2)}) %collective-permute-start.4) | collective-permute-done | bytes 1179680 | tf_op jit(solution)/shard_map/ppermute | solution.py:429
  43.3 1.3 %collective-permute-done.2.refs_2_ = bf16[2,768,256]{2,1,0:T(8,128)(2,1)S(1)} collective-permute-done((bf16[2,768,256]{2,1,0:T(8,128)(2,1)S(1)}, bf16[2,768,256]{2,1,0:T(8,128)(2,1)S(1)}, u32[]{:S(2)}, u32[]{:S(2)}) %collective-permute-start.2) | collective-permute-done | bytes 786464 | tf_op jit(solution)/shard_map/ppermute | solution.py:434
  44.6 2.7 %collective-permute-start.9 = (bf16[2,768,256]{2,1,0:T(8,128)(2,1)S(1)}, bf16[2,768,256]{2,1,0:T(8,128)(2,1)S(1)}, u32[]{:S(2)}, u32[]{:S(2)}) collective-permute-start(bf16[2,768,256]{2,1,0:T(8,128)(2,1)S(1)} %collective-permute-done.7.refs_3_), channel_id=1, source_target_pairs={{0,224},{32,0},{64,32},{96,64},{128,96},{160,128},{192,160},{224,1... | collective-permute-start | bytes 2359304 | tf_op jit(solution)/shard_map/ppermute | solution.py:434
  47.3 2.5 %attend.5.refs_4_ = f32[792,512]{1,0:T(8,128)S(1)} custom-call(bf16[256,768]{1,0:T(8,128)(2,1)S(1)} %pack_queries.1.refs_0_, bf16[256,768]{1,0:T(8,128)(2,1)S(1)} %collective-permute-done.refs_1_, bf16[2,768,256]{2,1,0:T(8,128)(2,1)S(1)} %collective-permute-done.2.refs_2_, bf16[2,768,256]{2,1,0:T(8,128)(2,1)S(1)} %collective-permute-done.7.refs_3_, ...), custom_call_target="tpu_custom_call" | custom-call | flops 6442450944 | bytes 3145728 | tf_op jit(solution)/shard_map/attend/pallas_call | solution.py:217
  49.8 2.8 %collective-permute-start.11 = (bf16[384,1536]{1,0:T(8,128)(2,1)S(1)}, bf16[384,1536]{1,0:T(8,128)(2,1)S(1)}, u32[]{:S(2)}, u32[]{:S(2)}) collective-permute-start(bf16[384,1536]{1,0:T(8,128)(2,1)S(1)} %get-tuple-element.26), channel_id=1, source_target_pairs={{0,8},{4,12},{8,0},{12,4},{1,9},{5,13},{9,1},{13,5},{2,10},{6,14},... | collective-permute-start | bytes 3538952 | tf_op jit(solution)/shard_map/ppermute | solution.py:429
  52.6 10.1 %collective-permute-done.6.refs_2_ = bf16[2,768,256]{2,1,0:T(8,128)(2,1)S(1)} collective-permute-done((bf16[2,768,256]{2,1,0:T(8,128)(2,1)S(1)}, bf16[2,768,256]{2,1,0:T(8,128)(2,1)S(1)}, u32[]{:S(2)}, u32[]{:S(2)}) %collective-permute-start.6) | collective-permute-done | bytes 786464 | tf_op jit(solution)/shard_map/ppermute | solution.py:434
  62.9 2.7 %collective-permute-start.10 = (bf16[768,256]{1,0:T(8,128)(2,1)S(1)}, bf16[768,256]{1,0:T(8,128)(2,1)S(1)}, u32[]{:S(2)}, u32[]{:S(2)}) collective-permute-start(bf16[768,256]{1,0:T(8,128)(2,1)S(1)} %slice_bitcast_fusion), channel_id=1, source_target_pairs={{0,224},{32,0},{64,32},{96,64},{128,96},{160,128},{192,160},{224,1... | collective-permute-start | bytes 1179656 | tf_op jit(solution)/shard_map/ppermute | solution.py:434
  65.6 2.5 %attend.6.refs_4_ = f32[792,512]{1,0:T(8,128)S(1)} custom-call(bf16[256,768]{1,0:T(8,128)(2,1)S(1)} %pack_queries.1.refs_0_, bf16[256,768]{1,0:T(8,128)(2,1)S(1)} %collective-permute-done.refs_1_, bf16[2,768,256]{2,1,0:T(8,128)(2,1)S(1)} %collective-permute-done.6.refs_2_, bf16[2,768,256]{2,1,0:T(8,128)(2,1)S(1)} %collective-permute-done.9.refs_3_, ...), custom_call_target="tpu_custom_call" | custom-call | flops 6442450944 | bytes 3145728 | tf_op jit(solution)/shard_map/attend/pallas_call | solution.py:217
  68.1 3.5 %collective-permute-done.8.refs_2_ = bf16[768,256]{1,0:T(8,128)(2,1)S(1)} collective-permute-done((bf16[768,256]{1,0:T(8,128)(2,1)S(1)}, bf16[768,256]{1,0:T(8,128)(2,1)S(1)}, u32[]{:S(2)}, u32[]{:S(2)}) %collective-permute-start.8) | collective-permute-done | bytes 393248 | tf_op jit(solution)/shard_map/ppermute | solution.py:434
  71.6 1.6 %attend.7 = (f32[792,256]{1,0:T(8,128)S(1)}, bf16[544,256]{1,0:T(8,128)(2,1)S(1)}, bf16[272,256]{1,0:T(8,128)(2,1)S(1)}) custom-call(bf16[256,768]{1,0:T(8,128)(2,1)S(1)} %pack_queries.1.refs_0_, bf16[256,768]{1,0:T(8,128)(2,1)S(1)} %collective-permute-done.refs_1_, bf16[768,256]{1,0:T(8,128)(2,1)S(1)} %collective-permute-done.8.refs_2_, ...), custom_call_target="tpu_custom_call" | custom-call | flops 3221225472 | bytes 2359296 | tf_op jit(solution)/shard_map/attend/pallas_call | solution.py:217
  73.2 3.0 %collective-permute-start.16 = (bf16[544,256]{1,0:T(8,128)(2,1)S(1)}, bf16[544,256]{1,0:T(8,128)(2,1)S(1)}, u32[]{:S(2)}, u32[]{:S(2)}) collective-permute-start(bf16[544,256]{1,0:T(8,128)(2,1)S(1)} %get-tuple-element.32), channel_id=1, source_target_pairs={{0,16},{16,0},{1,17},{17,1},{2,18},{18,2},{3,19},{19,3},{4,20},{20... | collective-permute-start | bytes 835592 | tf_op jit(solution)/shard_map/ppermute | solution.py:451
  76.2 2.8 %collective-permute-start.12 = (bf16[272,256]{1,0:T(8,128)(2,1)S(1)}, bf16[272,256]{1,0:T(8,128)(2,1)S(1)}, u32[]{:S(2)}, u32[]{:S(2)}) collective-permute-start(bf16[272,256]{1,0:T(8,128)(2,1)S(1)} %get-tuple-element.27), channel_id=1, source_target_pairs={{0,16},{16,0},{1,17},{17,1},{2,18},{18,2},{3,19},{19,3},{4,20},{20... | collective-permute-start | bytes 417800 | tf_op jit(solution)/shard_map/ppermute | solution.py:452
  80.4 1.3 %collective-permute-start.17 = (bf16[512,256]{1,0:T(8,128)(2,1)S(1)}, bf16[512,256]{1,0:T(8,128)(2,1)S(1)}, u32[]{:S(2)}, u32[]{:S(2)}) collective-permute-start(bf16[512,256]{1,0:T(8,128)(2,1)S(1)} %merge.3.refs_0_), channel_id=1, source_target_pairs={{0,4},{4,8},{8,12},{12,0},{1,5},{5,9},{9,13},{13,1},{2,6},{6,10},{... | collective-permute-start | bytes 786440 | tf_op jit(solution)/shard_map/ppermute | solution.py:458
  81.7 2.5 %collective-permute-start.18 = (bf16[512,256]{1,0:T(8,128)(2,1)S(1)}, bf16[512,256]{1,0:T(8,128)(2,1)S(1)}, u32[]{:S(2)}, u32[]{:S(2)}) collective-permute-start(bf16[512,256]{1,0:T(8,128)(2,1)S(1)} %merge.3.refs_0_), channel_id=1, source_target_pairs={{0,8},{4,12},{8,0},{12,4},{1,9},{5,13},{9,1},{13,5},{2,10},{6,14},... | collective-permute-start | bytes 786440 | tf_op jit(solution)/shard_map/ppermute | solution.py:458
  84.2 1.2 %collective-permute-start.19 = (bf16[512,256]{1,0:T(8,128)(2,1)S(1)}, bf16[512,256]{1,0:T(8,128)(2,1)S(1)}, u32[]{:S(2)}, u32[]{:S(2)}) collective-permute-start(bf16[512,256]{1,0:T(8,128)(2,1)S(1)} %merge.3.refs_0_), channel_id=1, source_target_pairs={{0,12},{4,0},{8,4},{12,8},{1,13},{5,1},{9,5},{13,9},{2,14},{6,2},{... | collective-permute-start | bytes 786440 | tf_op jit(solution)/shard_map/ppermute | solution.py:458
  86.7 3.0 %stage.1 = (bf16[1024,1536]{1,0:T(8,128)(2,1)S(1)}, bf16[512,1536]{1,0:T(8,128)(2,1)S(1)}) custom-call(s32[2]{0:T(128)S(1)} %pad_add_fusion.place, bf16[384,6144]{1,0:T(8,128)(2,1)} %weight.1, bf16[384,1536]{1,0:T(8,128)(2,1)} %copy-done.2, bf16[384,1536]{1,0:T(8,128)(2,1)} %copy-done.4, bf16[384,1536]{1,0:T(8,128)(2,1)} %copy-done.3), custom_call_target="tpu_custom_call" | custom-call | bytes 9437184 | tf_op jit(solution)/shard_map/stage/pallas_call | solution.py:308
  89.7 1.9 %collective-permute-start.15 = (bf16[512,128]{1,0:T(8,128)(2,1)S(1)}, bf16[512,128]{1,0:T(8,128)(2,1)S(1)}, u32[]{:S(2)}, u32[]{:S(2)}) collective-permute-start(bf16[512,128]{1,0:T(8,128)(2,1)S(1)} %merge.2.refs_0_), channel_id=1, source_target_pairs={{0,12},{4,0},{8,4},{12,8},{1,13},{5,1},{9,5},{13,9},{2,14},{6,2},{... | collective-permute-start | bytes 393224 | tf_op jit(solution)/shard_map/ppermute | solution.py:458
  91.7 2.3 %project.3.refs_5_ = f32[512,1536]{1,0:T(8,128)S(1)} custom-call(bf16[512,256]{1,0:T(8,128)(2,1)S(1)} %merge.3.refs_0_, bf16[512,256]{1,0:T(8,128)(2,1)S(1)} %collective-permute-done.17.refs_1_, bf16[512,256]{1,0:T(8,128)(2,1)S(1)} %collective-permute-done.18.refs_2_, bf16[512,256]{1,0:T(8,128)(2,1)S(1)} %collective-permute-done.19.refs_3_, ...), custom_call_target="tpu_custom_call" | custom-call | flops 10000000000 | bytes 7864320 | tf_op jit(solution)/shard_map/project/pallas_call | solution.py:345
  94.0 2.3 %collective-permute-done.14.refs_2_ = bf16[512,128]{1,0:T(8,128)(2,1)S(1)} collective-permute-done((bf16[512,128]{1,0:T(8,128)(2,1)S(1)}, bf16[512,128]{1,0:T(8,128)(2,1)S(1)}, u32[]{:S(2)}, u32[]{:S(2)}) %collective-permute-start.14) | collective-permute-done | bytes 131104 | tf_op jit(solution)/shard_map/ppermute | solution.py:458
  97.2 6.3 %collective-permute-start.20 = (bf16[512,768]{1,0:T(8,128)(2,1)S(1)}, bf16[512,768]{1,0:T(8,128)(2,1)S(1)}, u32[]{:S(2)}, u32[]{:S(2)}) collective-permute-start(bf16[512,768]{1,0:T(8,128)(2,1)S(1)} %project.5), channel_id=1, source_target_pairs={{0,2},{2,0},{1,3},{3,1},{4,6},{6,4},{5,7},{7,5},{8,10},{10,8},{9,1... | collective-permute-start | bytes 2359304 | tf_op jit(solution)/shard_map/ppermute | solution.py:464
  104.3 1.1 %collective-permute-done.20.other = bf16[512,768]{1,0:T(8,128)(2,1)S(1)} collective-permute-done((bf16[512,768]{1,0:T(8,128)(2,1)S(1)}, bf16[512,768]{1,0:T(8,128)(2,1)S(1)}, u32[]{:S(2)}, u32[]{:S(2)}) %collective-permute-start.20) | collective-permute-done | bytes 786464 | tf_op jit(solution)/shard_map/ppermute | solution.py:464
  (43 shorter events, 7.8 us)
Async XLA Ops:
  1.9 23.8 %collective-permute-start.1 = (bf16[2,768,256]{2,1,0:T(8,128)(2,1)S(1)}, bf16[2,768,256]{2,1,0:T(8,128)(2,1)S(1)}, u32[]{:S(2)}, u32[]{:S(2)}) collective-permute-start(bf16[2,768,256]{2,1,0:T(8,128)(2,1)S(1)} %pack.1.refs_2_), channel_id=1, source_target_pairs={{0,32},{32,64},{64,96},{96,128},{128,160},{160,192},{192,224},{224... | collective-permute-start | bytes 2359304 | tf_op jit(solution)/shard_map/ppermute | solution.py:434
  4.4 21.2 %collective-permute-start.3 = (bf16[2,768,256]{2,1,0:T(8,128)(2,1)S(1)}, bf16[2,768,256]{2,1,0:T(8,128)(2,1)S(1)}, u32[]{:S(2)}, u32[]{:S(2)}) collective-permute-start(bf16[2,768,256]{2,1,0:T(8,128)(2,1)S(1)} %pack.1.refs_2_), channel_id=1, source_target_pairs={{0,224},{32,0},{64,32},{96,64},{128,96},{160,128},{192,160},{224,1... | collective-permute-start | bytes 2359304 | tf_op jit(solution)/shard_map/ppermute | solution.py:434
  9.5 11.3 %collective-permute-start = (bf16[256,768]{1,0:T(8,128)(2,1)S(1)}, bf16[256,768]{1,0:T(8,128)(2,1)S(1)}, u32[]{:S(2)}, u32[]{:S(2)}) collective-permute-start(bf16[256,768]{1,0:T(8,128)(2,1)S(1)} %pack_queries.1.refs_0_), channel_id=1, source_target_pairs={{0,16},{16,0},{1,17},{17,1},{2,18},{18,2},{3,19},{19,3},{4,20},{20... | collective-permute-start | bytes 1179656 | tf_op jit(solution)/shard_map/ppermute | solution.py:421
  14.7 27.5 %collective-permute-start.4 = (bf16[384,1536]{1,0:T(8,128)(2,1)S(1)}, bf16[384,1536]{1,0:T(8,128)(2,1)S(1)}, u32[]{:S(2)}, u32[]{:S(2)}) collective-permute-start(bf16[384,1536]{1,0:T(8,128)(2,1)S(1)} %get-tuple-element.36), channel_id=1, source_target_pairs={{0,4},{4,8},{8,12},{12,0},{1,5},{5,9},{9,13},{13,1},{2,6},{6,10},{... | collective-permute-start | bytes 3538952 | tf_op jit(solution)/shard_map/ppermute | solution.py:429
  16.0 26.2 %collective-permute-start.5 = (bf16[384,1536]{1,0:T(8,128)(2,1)S(1)}, bf16[384,1536]{1,0:T(8,128)(2,1)S(1)}, u32[]{:S(2)}, u32[]{:S(2)}) collective-permute-start(bf16[384,1536]{1,0:T(8,128)(2,1)S(1)} %get-tuple-element.35), channel_id=1, source_target_pairs={{0,12},{4,0},{8,4},{12,8},{1,13},{5,1},{9,5},{13,9},{2,14},{6,2},{... | collective-permute-start | bytes 3538952 | tf_op jit(solution)/shard_map/ppermute | solution.py:429
  25.6 19.0 %collective-permute-start.2 = (bf16[2,768,256]{2,1,0:T(8,128)(2,1)S(1)}, bf16[2,768,256]{2,1,0:T(8,128)(2,1)S(1)}, u32[]{:S(2)}, u32[]{:S(2)}) collective-permute-start(bf16[2,768,256]{2,1,0:T(8,128)(2,1)S(1)} %collective-permute-done.1.refs_3_), channel_id=1, source_target_pairs={{0,32},{32,64},{64,96},{96,128},{128,160},{160,192},{192,224},{224... | collective-permute-start | bytes 2359304 | tf_op jit(solution)/shard_map/ppermute | solution.py:434
  25.6 19.0 %collective-permute-start.7 = (bf16[2,768,256]{2,1,0:T(8,128)(2,1)S(1)}, bf16[2,768,256]{2,1,0:T(8,128)(2,1)S(1)}, u32[]{:S(2)}, u32[]{:S(2)}) collective-permute-start(bf16[2,768,256]{2,1,0:T(8,128)(2,1)S(1)} %collective-permute-done.3.refs_4_), channel_id=1, source_target_pairs={{0,224},{32,0},{64,32},{96,64},{128,96},{160,128},{192,160},{224,1... | collective-permute-start | bytes 2359304 | tf_op jit(solution)/shard_map/ppermute | solution.py:434
  42.2 7.6 %copy-start.2 = (bf16[384,1536]{1,0:T(8,128)(2,1)}, bf16[384,1536]{1,0:T(8,128)(2,1)S(1)}, u32[]{:S(2)}) copy-start(bf16[384,1536]{1,0:T(8,128)(2,1)S(1)} %collective-permute-done.4.refs_0_) | copy-start | bytes 3538948
  42.2 1.1 copy-start.3
  44.6 18.1 %collective-permute-start.6 = (bf16[2,768,256]{2,1,0:T(8,128)(2,1)S(1)}, bf16[2,768,256]{2,1,0:T(8,128)(2,1)S(1)}, u32[]{:S(2)}, u32[]{:S(2)}) collective-permute-start(bf16[2,768,256]{2,1,0:T(8,128)(2,1)S(1)} %collective-permute-done.2.refs_2_), channel_id=1, source_target_pairs={{0,32},{32,64},{64,96},{96,128},{128,160},{160,192},{192,224},{224... | collective-permute-start | bytes 2359304 | tf_op jit(solution)/shard_map/ppermute | solution.py:434
  44.6 18.2 %collective-permute-start.9 = (bf16[2,768,256]{2,1,0:T(8,128)(2,1)S(1)}, bf16[2,768,256]{2,1,0:T(8,128)(2,1)S(1)}, u32[]{:S(2)}, u32[]{:S(2)}) collective-permute-start(bf16[2,768,256]{2,1,0:T(8,128)(2,1)S(1)} %collective-permute-done.7.refs_3_), channel_id=1, source_target_pairs={{0,224},{32,0},{64,32},{96,64},{128,96},{160,128},{192,160},{224,1... | collective-permute-start | bytes 2359304 | tf_op jit(solution)/shard_map/ppermute | solution.py:434
  49.8 26.4 %collective-permute-start.11 = (bf16[384,1536]{1,0:T(8,128)(2,1)S(1)}, bf16[384,1536]{1,0:T(8,128)(2,1)S(1)}, u32[]{:S(2)}, u32[]{:S(2)}) collective-permute-start(bf16[384,1536]{1,0:T(8,128)(2,1)S(1)} %get-tuple-element.26), channel_id=1, source_target_pairs={{0,8},{4,12},{8,0},{12,4},{1,9},{5,13},{9,1},{13,5},{2,10},{6,14},... | collective-permute-start | bytes 3538952 | tf_op jit(solution)/shard_map/ppermute | solution.py:429
  62.8 8.8 %collective-permute-start.8 = (bf16[768,256]{1,0:T(8,128)(2,1)S(1)}, bf16[768,256]{1,0:T(8,128)(2,1)S(1)}, u32[]{:S(2)}, u32[]{:S(2)}) collective-permute-start(bf16[768,256]{1,0:T(8,128)(2,1)S(1)} %slice_bitcast_fusion.1), channel_id=1, source_target_pairs={{0,32},{32,64},{64,96},{96,128},{128,160},{160,192},{192,224},{224... | collective-permute-start | bytes 1179656 | tf_op jit(solution)/shard_map/ppermute | solution.py:434
  62.9 8.7 %collective-permute-start.10 = (bf16[768,256]{1,0:T(8,128)(2,1)S(1)}, bf16[768,256]{1,0:T(8,128)(2,1)S(1)}, u32[]{:S(2)}, u32[]{:S(2)}) collective-permute-start(bf16[768,256]{1,0:T(8,128)(2,1)S(1)} %slice_bitcast_fusion), channel_id=1, source_target_pairs={{0,224},{32,0},{64,32},{96,64},{128,96},{160,128},{192,160},{224,1... | collective-permute-start | bytes 1179656 | tf_op jit(solution)/shard_map/ppermute | solution.py:434
  73.2 7.0 %collective-permute-start.16 = (bf16[544,256]{1,0:T(8,128)(2,1)S(1)}, bf16[544,256]{1,0:T(8,128)(2,1)S(1)}, u32[]{:S(2)}, u32[]{:S(2)}) collective-permute-start(bf16[544,256]{1,0:T(8,128)(2,1)S(1)} %get-tuple-element.32), channel_id=1, source_target_pairs={{0,16},{16,0},{1,17},{17,1},{2,18},{18,2},{3,19},{19,3},{4,20},{20... | collective-permute-start | bytes 835592 | tf_op jit(solution)/shard_map/ppermute | solution.py:451
  76.2 9.3 %copy-start.4 = (bf16[384,1536]{1,0:T(8,128)(2,1)}, bf16[384,1536]{1,0:T(8,128)(2,1)S(1)}, u32[]{:S(2)}) copy-start(bf16[384,1536]{1,0:T(8,128)(2,1)S(1)} %collective-permute-done.11.refs_1_) | copy-start | bytes 3538948
  76.2 9.1 %collective-permute-start.12 = (bf16[272,256]{1,0:T(8,128)(2,1)S(1)}, bf16[272,256]{1,0:T(8,128)(2,1)S(1)}, u32[]{:S(2)}, u32[]{:S(2)}) collective-permute-start(bf16[272,256]{1,0:T(8,128)(2,1)S(1)} %get-tuple-element.27), channel_id=1, source_target_pairs={{0,16},{16,0},{1,17},{17,1},{2,18},{18,2},{3,19},{19,3},{4,20},{20... | collective-permute-start | bytes 417800 | tf_op jit(solution)/shard_map/ppermute | solution.py:452
  80.4 9.3 %collective-permute-start.17 = (bf16[512,256]{1,0:T(8,128)(2,1)S(1)}, bf16[512,256]{1,0:T(8,128)(2,1)S(1)}, u32[]{:S(2)}, u32[]{:S(2)}) collective-permute-start(bf16[512,256]{1,0:T(8,128)(2,1)S(1)} %merge.3.refs_0_), channel_id=1, source_target_pairs={{0,4},{4,8},{8,12},{12,0},{1,5},{5,9},{9,13},{13,1},{2,6},{6,10},{... | collective-permute-start | bytes 786440 | tf_op jit(solution)/shard_map/ppermute | solution.py:458
  81.7 10.0 %collective-permute-start.18 = (bf16[512,256]{1,0:T(8,128)(2,1)S(1)}, bf16[512,256]{1,0:T(8,128)(2,1)S(1)}, u32[]{:S(2)}, u32[]{:S(2)}) collective-permute-start(bf16[512,256]{1,0:T(8,128)(2,1)S(1)} %merge.3.refs_0_), channel_id=1, source_target_pairs={{0,8},{4,12},{8,0},{12,4},{1,9},{5,13},{9,1},{13,5},{2,10},{6,14},... | collective-permute-start | bytes 786440 | tf_op jit(solution)/shard_map/ppermute | solution.py:458
  84.2 7.5 %collective-permute-start.19 = (bf16[512,256]{1,0:T(8,128)(2,1)S(1)}, bf16[512,256]{1,0:T(8,128)(2,1)S(1)}, u32[]{:S(2)}, u32[]{:S(2)}) collective-permute-start(bf16[512,256]{1,0:T(8,128)(2,1)S(1)} %merge.3.refs_0_), channel_id=1, source_target_pairs={{0,12},{4,0},{8,4},{12,8},{1,13},{5,1},{9,5},{13,9},{2,14},{6,2},{... | collective-permute-start | bytes 786440 | tf_op jit(solution)/shard_map/ppermute | solution.py:458
  85.5 8.5 %collective-permute-start.13 = (bf16[512,128]{1,0:T(8,128)(2,1)S(1)}, bf16[512,128]{1,0:T(8,128)(2,1)S(1)}, u32[]{:S(2)}, u32[]{:S(2)}) collective-permute-start(bf16[512,128]{1,0:T(8,128)(2,1)S(1)} %merge.2.refs_0_), channel_id=1, source_target_pairs={{0,4},{4,8},{8,12},{12,0},{1,5},{5,9},{9,13},{13,1},{2,6},{6,10},{... | collective-permute-start | bytes 393224 | tf_op jit(solution)/shard_map/ppermute | solution.py:458
  85.9 10.4 %collective-permute-start.14 = (bf16[512,128]{1,0:T(8,128)(2,1)S(1)}, bf16[512,128]{1,0:T(8,128)(2,1)S(1)}, u32[]{:S(2)}, u32[]{:S(2)}) collective-permute-start(bf16[512,128]{1,0:T(8,128)(2,1)S(1)} %merge.2.refs_0_), channel_id=1, source_target_pairs={{0,8},{4,12},{8,0},{12,4},{1,9},{5,13},{9,1},{13,5},{2,10},{6,14},... | collective-permute-start | bytes 393224 | tf_op jit(solution)/shard_map/ppermute | solution.py:458
  89.7 6.7 %collective-permute-start.15 = (bf16[512,128]{1,0:T(8,128)(2,1)S(1)}, bf16[512,128]{1,0:T(8,128)(2,1)S(1)}, u32[]{:S(2)}, u32[]{:S(2)}) collective-permute-start(bf16[512,128]{1,0:T(8,128)(2,1)S(1)} %merge.2.refs_0_), channel_id=1, source_target_pairs={{0,12},{4,0},{8,4},{12,8},{1,13},{5,1},{9,5},{13,9},{2,14},{6,2},{... | collective-permute-start | bytes 393224 | tf_op jit(solution)/shard_map/ppermute | solution.py:458
  96.5 7.0 %copy-start.5 = (f32[768]{0:T(1024)S(1)}, f32[768]{0:T(1024)}, u32[]{:S(2)}) copy-start(f32[768]{0:T(1024)} %param.20) | copy-start | bytes 9220
  96.5 7.0 %copy-start.6 = (f32[768]{0:T(1024)S(1)}, f32[768]{0:T(1024)}, u32[]{:S(2)}) copy-start(f32[768]{0:T(1024)} %param.21) | copy-start | bytes 9220
  97.2 8.2 %collective-permute-start.20 = (bf16[512,768]{1,0:T(8,128)(2,1)S(1)}, bf16[512,768]{1,0:T(8,128)(2,1)S(1)}, u32[]{:S(2)}, u32[]{:S(2)}) collective-permute-start(bf16[512,768]{1,0:T(8,128)(2,1)S(1)} %project.5), channel_id=1, source_target_pairs={{0,2},{2,0},{1,3},{3,1},{4,6},{6,4},{5,7},{7,5},{8,10},{10,8},{9,1... | collective-permute-start | bytes 2359304 | tf_op jit(solution)/shard_map/ppermute | solution.py:464
  103.5 1.9 %copy-start = (bf16[256,768]{1,0:T(8,128)(2,1)S(1)}, bf16[256,768]{1,0:T(8,128)(2,1)}, u32[]{:S(2)}) copy-start(bf16[256,768]{1,0:T(8,128)(2,1)} %res.1) | copy-start | bytes 1179652
  103.6 1.9 %copy-start.1 = (bf16[256,768]{1,0:T(8,128)(2,1)S(1)}, bf16[256,768]{1,0:T(8,128)(2,1)}, u32[]{:S(2)}) copy-start(bf16[256,768]{1,0:T(8,128)(2,1)} %res_t.1) | copy-start | bytes 1179652
